TPU v7x, 128 devices: a whole 4x4x4 slice. The times are simulated.
128 devices in a mesh: dp: 64 (over x_lo, z, y, core), tensor: 2 (over x_hi).
Axes of the slice: x: 4 (x_hi: 2, x_lo: 2; x = x_hi * 2 + x_lo), y: 4, z: 4, core: 2. Of those that a mesh axis runs over, the one named last changes fastest.
Arguments:
- tokens: bfloat16 [14336, 2048], P(('dp', 'tensor')), may hold values from -24 to 24
- segment_ids: int32 [14336], P('dp'), may hold values from 0 to 3, as said below
- attn_gain: bfloat16 [2048], P('dp'), may hold values from 0.099609375 to 1.8984375
- w_query: bfloat16 [2048, 2048], P('dp', 'tensor'), may hold values from -0.125 to 0.125
- w_key: bfloat16 [2048, 512], P('dp', 'tensor'), may hold values from -0.125 to 0.125
- w_value: bfloat16 [2048, 512], P('dp', 'tensor'), may hold values from -0.125 to 0.125
- w_out: bfloat16 [2048, 2048], P('tensor', 'dp'), may hold values from -0.75 to 0.75
- mlp_gain: bfloat16 [2048], P('dp'), may hold values from 0.099609375 to 1.8984375
- w_gate: bfloat16 [2048, 8192], P('dp', 'tensor'), may hold values from -0.125 to 0.125
- w_up: bfloat16 [2048, 8192], P('dp', 'tensor'), may hold values from -0.125 to 0.125
- w_down: bfloat16 [8192, 2048], P('tensor', 'dp'), may hold values from -0.125 to 0.125
- cotangent: bfloat16 [14336, 2048], P(('dp', 'tensor')), may hold values from -24 to 24
Outputs:
- layer_output: bfloat16 [14336, 2048], P(('dp', 'tensor'))
- input_grad: float32 [14336, 2048], P(('dp', 'tensor'))
- attn_gain_grad: float32 [2048], P('dp')
- query_grad: float32 [2048, 2048], P('dp', 'tensor')
- key_grad: float32 [2048, 512], P('dp', 'tensor')
- value_grad: float32 [2048, 512], P('dp', 'tensor')
- out_grad: float32 [2048, 2048], P('tensor', 'dp')
- mlp_gain_grad: float32 [2048], P('dp')
- gate_grad: float32 [2048, 8192], P('dp', 'tensor')
- up_grad: float32 [2048, 8192], P('dp', 'tensor')
- down_grad: float32 [8192, 2048], P('tensor', 'dp')
Inputs may be any that keep to these rules, and one draw needn't show every extreme that they name: `segment_ids`: within each aligned block of 224 tokens (the tokens of one index of dp) the ids start at 0, never fall and rise by one at each new sequence; a block holds 1 to 4 sequences and some block holds 4; sequences never cross a block's end, and equal ids in different blocks are different sequences.
All inputs are finite; a program needn't handle non-finite values.
Results may differ from a plain program's by a relative error of at most 0.015.
Values may be sent and summed in bfloat16 or wider, within the bound.
No kernel may reach another device: no remote copies, remote signals or barrier semaphores. Data moves between devices by JAX's collectives and lax.ppermute only.
A program may use at most 320 MiB of HBM per device.

v0:
```python
import math

import jax
import jax.numpy as jnp
from jax import lax
from jax.sharding import PartitionSpec as P

HEADS = 32
KV_HEADS = 8
HEAD = 64


EPSILON = 1e-05
ROPE_BASE = 500000.0
MASKED = -1e30


def positions_of(segment):
    earlier = jnp.sum((segment[None, :] < segment[:, None]).astype(jnp.int32), axis=1)
    return jnp.arange(segment.shape[0], dtype=jnp.int32) - earlier


def rotary_tables(positions, half_width):
    exponent = jnp.arange(half_width).astype(jnp.float32) / half_width
    frequency = jnp.exp(-math.log(ROPE_BASE) * exponent)
    angles = positions.astype(jnp.float32)[..., None] * frequency
    return (jnp.cos(angles)[..., None, :], jnp.sin(angles)[..., None, :])


def rotate(values, cosines, sines):
    half_width = values.shape[-1] // 2
    first_half = values[..., :half_width]
    second_half = values[..., half_width:]
    return jnp.concatenate(
        [first_half * cosines - second_half * sines, second_half * cosines + first_half * sines],
        axis=-1,
    )


def norm_rows(values, gain_row):
    factor = lax.rsqrt(jnp.mean(values * values, axis=-1, keepdims=True) + EPSILON)
    return (values * factor * gain_row, factor)


def norm_back(values, factor, gain_row, upstream):
    rescaled = values * factor
    inner = upstream * gain_row
    back = factor * (inner - rescaled * jnp.mean(inner * rescaled, axis=-1, keepdims=True))
    return (back, jnp.sum(upstream * rescaled, axis=0))


def product(left, right):
    return jnp.dot(left, right, preferred_element_type=jnp.float32)


def product_nt(left, right):
    return lax.dot_general(
        left, right, (((1,), (1,)), ((), ())), preferred_element_type=jnp.float32
    )


def product_tn(left, right):
    return lax.dot_general(
        left, right, (((0,), (0,)), ((), ())), preferred_element_type=jnp.float32
    )


def whole_rows(local_part):
    return lax.all_gather(local_part, "tensor", axis=0, tiled=True)


def summed_rows(term, local_rows):
    return lax.psum_scatter(
        term(jnp.int32(0), local_rows * lax.axis_size("tensor")),
        "tensor",
        scatter_dimension=0,
        tiled=True,
    )


def pair_total(partial_value):
    return lax.psum(partial_value, "tensor")


def masked_scores(query_b, key_b, allowed):
    scores = jnp.einsum("ahgd,bhd->hgab", query_b, key_b, preferred_element_type=jnp.float32) * (
        1.0 / math.sqrt(HEAD)
    )
    return jnp.where(allowed, scores, MASKED)


def local(
    tokens,
    segment_ids,
    attn_gain,
    w_query,
    w_key,
    w_value,
    w_out,
    mlp_gain,
    w_gate,
    w_up,
    w_down,
    cotangent,
):
    half_type = jnp.bfloat16
    query_full, key_full, value_full, out_full, attn_gain_full = (
        lax.all_gather(w_query, "dp", axis=0, tiled=True),
        lax.all_gather(w_key, "dp", axis=0, tiled=True),
        lax.all_gather(w_value, "dp", axis=0, tiled=True),
        lax.all_gather(w_out, "dp", axis=1, tiled=True),
        lax.all_gather(attn_gain, "dp", axis=0, tiled=True),
    )
    gate_full, up_full, down_full, mlp_gain_full = (
        lax.all_gather(w_gate, "dp", axis=0, tiled=True),
        lax.all_gather(w_up, "dp", axis=0, tiled=True),
        lax.all_gather(w_down, "dp", axis=1, tiled=True),
        lax.all_gather(mlp_gain, "dp", axis=0, tiled=True),
    )
    local_rows = tokens.shape[0]
    group_size = HEADS // KV_HEADS
    local_kv = key_full.shape[1] // HEAD
    local_query = query_full.shape[1] // HEAD
    block_rows = segment_ids.shape[0]
    cosines, sines = rotary_tables(positions_of(segment_ids), HEAD // 2)
    token_order = jnp.arange(block_rows)
    allowed = (segment_ids[:, None] == segment_ids[None, :]) & (
        token_order[None, :] <= token_order[:, None]
    )
    resid_in = tokens.astype(jnp.float32)
    normed, factor_attn = norm_rows(resid_in, attn_gain_full)
    normed_all = whole_rows(normed.astype(half_type))
    query = product(normed_all, query_full).reshape(block_rows, local_query, HEAD)
    key_rows = product(normed_all, key_full).reshape(block_rows, local_kv, HEAD)
    value_b = product(normed_all, value_full).astype(half_type).reshape(block_rows, local_kv, HEAD)
    query_b = (
        rotate(query, cosines, sines)
        .astype(half_type)
        .reshape(block_rows, local_kv, group_size, HEAD)
    )
    key_b = rotate(key_rows, cosines, sines).astype(half_type)
    scores = masked_scores(query_b, key_b, allowed)
    row_max = jnp.max(scores, axis=-1, keepdims=True)
    weights = jnp.exp(scores - row_max)
    row_total = jnp.sum(weights, axis=-1, keepdims=True)
    log_total = row_max + jnp.log(row_total)
    attention_b = (weights / row_total).astype(half_type)
    mixed_b = (
        jnp.einsum("hgab,bhd->ahgd", attention_b, value_b, preferred_element_type=jnp.float32)
        .astype(half_type)
        .reshape(block_rows, local_query * HEAD)
    )

    def attn_term(first_row, row_count):
        return product(mixed_b, out_full)

    resid = resid_in + summed_rows(attn_term, local_rows)
    normed2, factor_mlp = norm_rows(resid, mlp_gain_full)
    normed2_all = whole_rows(normed2.astype(half_type))
    gate = product(normed2_all, gate_full)
    up_rows = product(normed2_all, up_full)
    sigmoid_gate = jax.nn.sigmoid(gate)
    silu_gate = gate * sigmoid_gate
    hidden_b = (silu_gate * up_rows).astype(half_type)

    def mlp_term(first_row, row_count):
        return product(hidden_b, down_full)

    layer_output = (resid + summed_rows(mlp_term, local_rows)).astype(half_type)
    gate_back, up_back, down_back, mlp_gain_back = (
        lax.all_gather(w_gate, "dp", axis=0, tiled=True),
        lax.all_gather(w_up, "dp", axis=0, tiled=True),
        lax.all_gather(w_down, "dp", axis=1, tiled=True),
        lax.all_gather(mlp_gain, "dp", axis=0, tiled=True),
    )
    upstream = cotangent.astype(jnp.float32)
    upstream_all = whole_rows(cotangent)
    d_hidden = product_nt(upstream_all, down_back)
    d_gate_b = (d_hidden * up_rows * sigmoid_gate * (1.0 + gate * (1.0 - sigmoid_gate))).astype(
        half_type
    )
    d_up_b = (d_hidden * silu_gate).astype(half_type)
    down_grad = product_tn(hidden_b, upstream_all)
    gate_grad = product_tn(normed2_all, d_gate_b)
    up_grad = product_tn(normed2_all, d_up_b)

    def mlp_back(first_row, row_count):
        return product_nt(d_gate_b, gate_back) + product_nt(d_up_b, up_back)

    back_mlp, mlp_gain_part = norm_back(
        resid, factor_mlp, mlp_gain_back, summed_rows(mlp_back, local_rows)
    )
    d_resid = upstream + back_mlp
    mlp_gain_sum = pair_total(mlp_gain_part)
    gate_grad, up_grad, down_grad, mlp_gain_sum = (
        lax.psum_scatter(gate_grad, "dp", scatter_dimension=0, tiled=True),
        lax.psum_scatter(up_grad, "dp", scatter_dimension=0, tiled=True),
        lax.psum_scatter(down_grad, "dp", scatter_dimension=1, tiled=True),
        lax.psum_scatter(mlp_gain_sum, "dp", scatter_dimension=0, tiled=True),
    )
    query_back, key_back, value_back, out_back, attn_gain_back = (
        lax.all_gather(w_query, "dp", axis=0, tiled=True),
        lax.all_gather(w_key, "dp", axis=0, tiled=True),
        lax.all_gather(w_value, "dp", axis=0, tiled=True),
        lax.all_gather(w_out, "dp", axis=1, tiled=True),
        lax.all_gather(attn_gain, "dp", axis=0, tiled=True),
    )
    d_branch_all = whole_rows(d_resid.astype(half_type))
    out_grad = product_tn(mixed_b, d_branch_all)
    d_mixed_b = (
        product_nt(d_branch_all, out_back)
        .astype(half_type)
        .reshape(block_rows, local_kv, group_size, HEAD)
    )
    scores = masked_scores(query_b, key_b, allowed)
    attention = jnp.exp(scores - log_total)
    d_value = jnp.einsum(
        "hgab,ahgd->bhd", attention.astype(half_type), d_mixed_b, preferred_element_type=jnp.float32
    )
    d_attention = jnp.einsum(
        "ahgd,bhd->hgab", d_mixed_b, value_b, preferred_element_type=jnp.float32
    )
    d_scores_b = (
        attention * (d_attention - jnp.sum(d_attention * attention, axis=-1, keepdims=True))
    ).astype(half_type)
    d_query_rot = jnp.einsum(
        "hgab,bhd->ahgd", d_scores_b, key_b, preferred_element_type=jnp.float32
    ) * (1.0 / math.sqrt(HEAD))
    d_key_rot = jnp.einsum(
        "hgab,ahgd->bhd", d_scores_b, query_b, preferred_element_type=jnp.float32
    ) * (1.0 / math.sqrt(HEAD))
    d_query_b = (
        rotate(d_query_rot.reshape(block_rows, local_query, HEAD), cosines, -sines)
        .astype(half_type)
        .reshape(block_rows, local_query * HEAD)
    )
    d_key_b = (
        rotate(d_key_rot, cosines, -sines).astype(half_type).reshape(block_rows, local_kv * HEAD)
    )
    d_value_b = d_value.astype(half_type).reshape(block_rows, local_kv * HEAD)
    query_grad = product_tn(normed_all, d_query_b)
    key_grad = product_tn(normed_all, d_key_b)
    value_grad = product_tn(normed_all, d_value_b)

    def attn_back(first_row, row_count):
        total_term = product_nt(d_query_b, query_back)
        total_term = total_term + product_nt(d_key_b, key_back)
        return total_term + product_nt(d_value_b, value_back)

    back_attn, attn_gain_part = norm_back(
        resid_in, factor_attn, attn_gain_back, summed_rows(attn_back, local_rows)
    )
    input_grad = d_resid + back_attn
    attn_gain_sum = pair_total(attn_gain_part)
    query_grad, key_grad, value_grad, out_grad, attn_gain_grad = (
        lax.psum_scatter(query_grad, "dp", scatter_dimension=0, tiled=True),
        lax.psum_scatter(key_grad, "dp", scatter_dimension=0, tiled=True),
        lax.psum_scatter(value_grad, "dp", scatter_dimension=0, tiled=True),
        lax.psum_scatter(out_grad, "dp", scatter_dimension=1, tiled=True),
        lax.psum_scatter(attn_gain_sum, "dp", scatter_dimension=0, tiled=True),
    )
    return (
        layer_output,
        input_grad,
        attn_gain_grad,
        query_grad,
        key_grad,
        value_grad,
        out_grad,
        mlp_gain_sum,
        gate_grad,
        up_grad,
        down_grad,
    )


def solution(mesh):
    return jax.shard_map(
        local,
        mesh=mesh,
        in_specs=(
            P(("dp", "tensor"), None),
            P("dp"),
            P("dp"),
            P("dp", "tensor"),
            P("dp", "tensor"),
            P("dp", "tensor"),
            P("tensor", "dp"),
            P("dp"),
            P("dp", "tensor"),
            P("dp", "tensor"),
            P("tensor", "dp"),
            P(("dp", "tensor"), None),
        ),
        out_specs=(
            P(("dp", "tensor"), None),
            P(("dp", "tensor"), None),
            P("dp"),
            P("dp", "tensor"),
            P("dp", "tensor"),
            P("dp", "tensor"),
            P("tensor", "dp"),
            P("dp"),
            P("dp", "tensor"),
            P("dp", "tensor"),
            P("tensor", "dp"),
        ),
        check_vma=False,
    )
```

profile of v0, /device:TPU:0, one launch (start us, length us, event | category | flops | bytes accessed | tf_op | source)
XLA Modules:
  0.0 3215.2 jit_solution(10782665602567455832)
XLA Ops:
  13.7 147.6 %all-reduce.6 = (bf16[2048]{0:T(1024)(128)(2,1)S(1)}, bf16[2048]{0:T(1024)(128)(2,1)S(1)}) all-reduce(bf16[2048]{0:T(1024)(128)(2,1)S(1)} %dynamic-update-slice, bf16[2048]{0:T(1024)(128)(2,1)S(1)} %dynamic-update-slice.1), channel_id=1, replica_groups=mesh['dp'=64,'tensor'=2] {'dp'}, use_global_device_ids=true, to_apply=%add | all-reduce | flops 4096 | bytes 16384
  165.8 11.1 all_gather.49
  176.8 1.6 convolution_convert_fusion.1
  178.6 38.0 %all-gather.10.cloned.1.call-done = bf16[2048,256]{1,0:T(8,128)(2,1)} async-done(((bf16[32,256]{1,0:T(8,128)(2,1)}), bf16[2048,256]{1,0:T(8,128)(2,1)}) %all-gather.10.cloned.1.call-update) | async-done | bytes 1048592 | tf_op jit(solution)/shard_map/all_gather | solution.py:109
  216.6 1.7 fusion.38
  218.4 104.8 %all-gather.12.cloned.1.call-done = bf16[2048,1024]{1,0:T(8,128)(2,1)} async-done(((bf16[32,1024]{1,0:T(8,128)(2,1)}), bf16[2048,1024]{1,0:T(8,128)(2,1)}) %all-gather.12.cloned.1.call-update) | async-done | bytes 4194320 | tf_op jit(solution)/shard_map/all_gather | solution.py:108
  323.2 3.9 fusion.39
  330.7 99.1 %all-gather.14.cloned.1.call-done = bf16[1024,2048]{0,1:T(8,128)(2,1)} async-done(((bf16[1024,32]{0,1:T(8,128)(2,1)}), bf16[1024,2048]{0,1:T(8,128)(2,1)}) %all-gather.14.cloned.1.call-update) | async-done | bytes 4194320 | tf_op jit(solution)/shard_map/all_gather | solution.py:111
  429.8 5.0 fusion.40
  437.0 22.6 all_gather.59
  459.5 13.3 reduce-scatter.12.cloned.1.call-done
  474.4 19.8 all_gather.55
  494.2 104.2 %all-gather.18.cloned.1.call-done = bf16[2048,4096]{1,0:T(8,128)(2,1)} async-done(((bf16[32,4096]{1,0:T(8,128)(2,1)}), bf16[2048,4096]{1,0:T(8,128)(2,1)}) %all-gather.18.cloned.1.call-update) | async-done | bytes 16777232 | tf_op jit(solution)/shard_map/all_gather | solution.py:116
  598.4 9.7 fusion.42
  608.1 114.2 %all-gather.16.cloned.1.call-done = bf16[2048,4096]{1,0:T(8,128)(2,1)} async-done(((bf16[32,4096]{1,0:T(8,128)(2,1)}), bf16[2048,4096]{1,0:T(8,128)(2,1)}) %all-gather.16.cloned.1.call-update) | async-done | bytes 16777232 | tf_op jit(solution)/shard_map/all_gather | solution.py:115
  722.3 9.6 fusion.41
  731.9 114.6 %all-gather.20.cloned.1.call-done = bf16[4096,2048]{0,1:T(8,128)(2,1)} async-done(((bf16[4096,32]{0,1:T(8,128)(2,1)}), bf16[4096,2048]{0,1:T(8,128)(2,1)}) %all-gather.20.cloned.1.call-update) | async-done | bytes 16777232 | tf_op jit(solution)/shard_map/all_gather | solution.py:117
  846.5 12.6 multiply_convert_fusion
  859.1 12.7 fusion.44
  871.8 13.2 convolution_add_fusion.2
  885.1 31.6 reduce-scatter.16.cloned.1.call-done
  916.7 2.2 multiply_reduce_fusion
  918.9 1.6 fusion.35
  920.5 14.8 all_gather.60
  936.3 1.9 convolution_convert_fusion
  938.2 2.0 copy.52
  940.2 3.0 fusion.20
  947.1 1.6 copy-done.8
  948.7 1.5 fusion.45
  951.4 1.8 convolution_add_fusion
  953.3 12.8 fusion.43
  966.1 1.8 fusion.48
  968.0 1.8 fusion.47
  970.0 5.7 fusion.46
  976.9 5.6 fusion.49
  982.6 15.2 fusion.51
  997.8 14.8 fusion.50
  1013.8 14.7 fusion.52
  1029.4 1.6 fusion.28
  1031.0 278.2 %all-reduce.4 = (f32[2048]{0:T(1024)S(1)}, f32[2048]{0:T(1024)S(1)}) all-reduce(f32[2048]{0:T(1024)S(1)} %get-tuple-element.13, f32[2048]{0:T(1024)S(1)} %copy-done.28), channel_id=6, replica_groups=mesh['dp'=64,'tensor'=2] {'dp'}, use_global_device_ids=true, to_apply=%region_14.15.clone | all-reduce | flops 4096 | bytes 32768
  1309.4 6.9 all-reduce.5
  1316.4 2.9 fusion.27
  1319.3 276.4 %reduce-scatter.22.cloned.1.call-done = f32[32,256]{1,0:T(8,128)} async-done(((f32[2048,256]{1,0:T(8,128)}), f32[32,256]{1,0:T(8,128)}) %reduce-scatter.22.cloned.1.call-update) | async-done | bytes 32784 | tf_op jit(solution)/shard_map/reduce_scatter | solution.py:257
  1595.7 296.9 %reduce-scatter.20.cloned.1.call-done = f32[32,1024]{1,0:T(8,128)} async-done(((f32[2048,1024]{1,0:T(8,128)}), f32[32,1024]{1,0:T(8,128)}) %reduce-scatter.20.cloned.1.call-update) | async-done | bytes 131088 | tf_op jit(solution)/shard_map/reduce_scatter | solution.py:256
  1892.6 296.9 %reduce-scatter.26.cloned.1.call-done = f32[1024,32]{0,1:T(8,128)} async-done(((f32[1024,2048]{0,1:T(8,128)}), f32[1024,32]{0,1:T(8,128)}) %reduce-scatter.26.cloned.1.call-update) | async-done | bytes 131088 | tf_op jit(solution)/shard_map/reduce_scatter | solution.py:259
  2189.5 339.9 %reduce-scatter.30.cloned.1.call-done = f32[32,4096]{1,0:T(8,128)} async-done(((f32[2048,4096]{1,0:T(8,128)}), f32[32,4096]{1,0:T(8,128)}) %reduce-scatter.30.cloned.1.call-update) | async-done | bytes 524304 | tf_op jit(solution)/shard_map/reduce_scatter | solution.py:197
  2529.5 339.1 %reduce-scatter.28.cloned.1.call-done = f32[32,4096]{1,0:T(8,128)} async-done(((f32[2048,4096]{1,0:T(8,128)}), f32[32,4096]{1,0:T(8,128)}) %reduce-scatter.28.cloned.1.call-update) | async-done | bytes 524304 | tf_op jit(solution)/shard_map/reduce_scatter | solution.py:196
  2868.5 339.6 %reduce-scatter.32.cloned.1.call-done = f32[4096,32]{0,1:T(8,128)} async-done(((f32[4096,2048]{0,1:T(8,128)}), f32[4096,32]{0,1:T(8,128)}) %reduce-scatter.32.cloned.1.call-update) | async-done | bytes 524304 | tf_op jit(solution)/shard_map/reduce_scatter | solution.py:198
  (147 shorter events, 26.5 us)
Async XLA Ops:
  7.2 169.6 %all-gather.8.cloned.1.call-start = ((), (), s32[]{:S(2)}) async-start(), calls=%async_computation.11 | async-start | bytes 1064960 | tf_op jit(solution)/shard_map/all_gather | solution.py:110
  7.9 208.7 %all-gather.10.cloned.1.call-start = ((), (), s32[]{:S(2)}) async-start(), calls=%async_computation.12 | async-start | bytes 1064960 | tf_op jit(solution)/shard_map/all_gather | solution.py:109
  8.7 314.6 %all-gather.12.cloned.1.call-start = ((), (), s32[]{:S(2)}) async-start(), calls=%async_computation.13 | async-start | bytes 4259840 | tf_op jit(solution)/shard_map/all_gather | solution.py:108
  9.4 420.4 %all-gather.14.cloned.1.call-start = ((), (), s32[]{:S(2)}) async-start(), calls=%async_computation.14 | async-start | bytes 4259840 | tf_op jit(solution)/shard_map/all_gather | solution.py:111
  10.0 462.9 %reduce-scatter.12.cloned.1.call-start = ((), (), s32[]{:S(2)}) async-start(), calls=%async_computation.15 | async-start | bytes 2752512 | tf_op jit(solution)/shard_map/reduce_scatter | solution.py:73
  161.4 56.9 %copy-start.26 = (f32[2048]{0:T(1024)}, f32[2048]{0:T(1024)S(1)}, u32[]{:S(2)}) copy-start(f32[2048]{0:T(1024)S(1)} %convert_element_type.93) | copy-start | bytes 24580
  163.5 54.9 %copy-start.31 = (f32[112]{0:T(128)}, f32[112]{0:T(128)S(1)}, u32[]{:S(2)}) copy-start(f32[112]{0:T(128)S(1)} %add_rsqrt_fusion.1) | copy-start | bytes 1348
  218.4 109.0 %copy-start.20 = (bf16[224,4,32]{0,2,1:T(8,128)(2,1)}, bf16[224,4,32]{0,2,1:T(8,128)(2,1)S(1)}, u32[]{:S(2)}) copy-start(bf16[224,4,32]{0,2,1:T(8,128)(2,1)S(1)} %get-tuple-element.34) | copy-start | bytes 172036
  218.4 109.0 %copy-start.22 = (bf16[224,4,32]{0,2,1:T(8,128)(2,1)}, bf16[224,4,32]{0,2,1:T(8,128)(2,1)S(1)}, u32[]{:S(2)}) copy-start(bf16[224,4,32]{0,2,1:T(8,128)(2,1)S(1)} %get-tuple-element.35) | copy-start | bytes 172036
  327.3 1.4 copy-start.16
  327.3 1.4 copy-start.18
  328.2 1.8 copy-start
  330.7 104.1 %copy-start.15 = (bf16[4,64,4,224]{3,1,2,0:T(8,128)(2,1)}, bf16[4,64,4,224]{3,1,2,0:T(8,128)(2,1)S(1)}, u32[]{:S(2)}) copy-start(bf16[4,64,4,224]{3,1,2,0:T(8,128)(2,1)S(1)} %fusion.14) | copy-start | bytes 1376260
  429.8 7.1 copy-start.10
  429.8 43.0 %copy-start.2 = (bf16[112,2048]{1,0:T(8,128)(2,1)S(1)}, bf16[112,2048]{1,0:T(8,128)(2,1)}, u32[]{:S(2)}) copy-start(bf16[112,2048]{1,0:T(8,128)(2,1)} %param.12) | copy-start | bytes 1376260
  434.8 163.6 %all-gather.18.cloned.1.call-start = ((), (), s32[]{:S(2)}) async-start(), calls=%async_computation.17 | async-start | bytes 17039360 | tf_op jit(solution)/shard_map/all_gather | solution.py:116
  435.4 286.9 %all-gather.16.cloned.1.call-start = ((), (), s32[]{:S(2)}) async-start(), calls=%async_computation.16 | async-start | bytes 17039360 | tf_op jit(solution)/shard_map/all_gather | solution.py:115
  436.1 410.4 %all-gather.20.cloned.1.call-start = ((), (), s32[]{:S(2)}) async-start(), calls=%async_computation.18 | async-start | bytes 17039360 | tf_op jit(solution)/shard_map/all_gather | solution.py:117
  436.9 479.8 %reduce-scatter.16.cloned.1.call-start = ((), (), s32[]{:S(2)}) async-start(), calls=%async_computation.20 | async-start | bytes 2752512 | tf_op jit(solution)/shard_map/reduce_scatter | solution.py:73
  437.0 481.9 %copy-start.24 = (f32[2048]{0:T(1024)}, f32[2048]{0:T(1024)S(1)}, u32[]{:S(2)}) copy-start(f32[2048]{0:T(1024)S(1)} %convert_element_type.102) | copy-start | bytes 24580
  474.3 444.6 %copy-start.29 = (f32[112]{0:T(128)}, f32[112]{0:T(128)S(1)}, u32[]{:S(2)}) copy-start(f32[112]{0:T(128)S(1)} %add_rsqrt_fusion) | copy-start | bytes 1348
  885.1 144.4 %reduce-scatter.18.cloned.1.call-start = ((), (), s32[]{:S(2)}) async-start(), calls=%async_computation.21 | async-start | bytes 2752512 | tf_op jit(solution)/shard_map/reduce_scatter | solution.py:73
  916.7 19.6 copy-start.9
  918.9 19.3 copy-start.33
  940.2 3.3 copy-start.1
  940.2 3.4 copy-start.5
  944.6 1.7 copy-start.21
  944.6 1.7 copy-start.23
  946.3 2.4 copy-start.8
  947.0 3.2 copy-start.7
  947.1 3.6 copy-start.4
  950.2 1.2 copy-start.6
  953.2 363.1 %reduce-scatter.14.cloned.1.call-start = ((), (), s32[]{:S(2)}) async-start(), calls=%async_computation.19 | async-start | bytes 2752512 | tf_op jit(solution)/shard_map/reduce_scatter | solution.py:73
  966.1 353.2 %reduce-scatter.24.cloned.1.call-start = ((), (), s32[]{:S(2)}) async-start(), calls=%async_computation.24 | async-start | bytes 2129920 | tf_op jit(solution)/shard_map/reduce_scatter | solution.py:258
  967.9 627.8 %reduce-scatter.22.cloned.1.call-start = ((), (), s32[]{:S(2)}) async-start(), calls=%async_computation.23 | async-start | bytes 2129920 | tf_op jit(solution)/shard_map/reduce_scatter | solution.py:257
  969.8 922.8 %reduce-scatter.20.cloned.1.call-start = ((), (), s32[]{:S(2)}) async-start(), calls=%async_computation.22 | async-start | bytes 8519680 | tf_op jit(solution)/shard_map/reduce_scatter | solution.py:256
  975.7 1.2 copy-start.13
  975.8 1213.8 %reduce-scatter.26.cloned.1.call-start = ((), (), s32[]{:S(2)}) async-start(), calls=%async_computation.25 | async-start | bytes 8519680 | tf_op jit(solution)/shard_map/reduce_scatter | solution.py:259
  982.5 1546.9 %reduce-scatter.30.cloned.1.call-start = ((), (), s32[]{:S(2)}) async-start(), calls=%async_computation.27 | async-start | bytes 34078720 | tf_op jit(solution)/shard_map/reduce_scatter | solution.py:197
  997.8 1870.8 %reduce-scatter.28.cloned.1.call-start = ((), (), s32[]{:S(2)}) async-start(), calls=%async_computation.26 | async-start | bytes 34078720 | tf_op jit(solution)/shard_map/reduce_scatter | solution.py:196
  1012.6 1.2 copy-start.14
  1012.7 2195.5 %reduce-scatter.32.cloned.1.call-start = ((), (), s32[]{:S(2)}) async-start(), calls=%async_computation.28 | async-start | bytes 34078720 | tf_op jit(solution)/shard_map/reduce_scatter | solution.py:198
  1028.6 2.4 copy-start.28
  1028.6 287.8 %copy-start.3 = (f32[112,2048]{1,0:T(8,128)S(1)}, f32[112,2048]{1,0:T(8,128)}, u32[]{:S(2)}) copy-start(f32[112,2048]{1,0:T(8,128)} %reduce-scatter.16.cloned.1.call-done) | copy-start | bytes 2752516
  1028.6 287.8 %copy-start.11 = (bf16[112,2048]{1,0:T(8,128)(2,1)S(1)}, bf16[112,2048]{1,0:T(8,128)(2,1)}, u32[]{:S(2)}) copy-start(bf16[112,2048]{1,0:T(8,128)(2,1)} %param.23) | copy-start | bytes 1376260
  1028.6 287.7 %copy-start.25 = (f32[2048]{0:T(1024)S(1)}, f32[2048]{0:T(1024)}, u32[]{:S(2)}) copy-start(f32[2048]{0:T(1024)} %copy-done.24) | copy-start | bytes 24580
  1028.6 287.7 %copy-start.30 = (f32[112]{0:T(128)S(1)}, f32[112]{0:T(128)}, u32[]{:S(2)}) copy-start(f32[112]{0:T(128)} %copy-done.29) | copy-start | bytes 1348
  1028.6 287.7 %copy-start.34 = (f32[112]{0:T(128)S(1)}, f32[112]{0:T(128)}, u32[]{:S(2)}) copy-start(f32[112]{0:T(128)} %copy-done.33) | copy-start | bytes 1348
  (5 other events, 4.6 us)
Sparse Core Ops, SparseCore 0:
  9.7 104.0 all-gather.7
  115.5 100.9 all-gather.9
  218.3 104.9 all-gather.11
  324.8 104.9 all-gather.13
  434.9 37.8 reduce-scatter.11
  474.5 123.8 all-gather.17
  600.3 121.9 all-gather.15
  724.1 122.3 all-gather.19
  885.2 31.4 reduce-scatter.15
  953.3 32.4 reduce-scatter.17
  988.3 32.4 reduce-scatter.13
  1023.5 286.3 reduce-scatter.23
  1312.9 282.7 reduce-scatter.21
  1598.5 294.0 reduce-scatter.19
  1895.4 294.0 reduce-scatter.25
  2192.4 337.0 reduce-scatter.29
  2532.3 336.2 reduce-scatter.27
  2871.4 336.7 reduce-scatter.31
where the time goes:
time: 3220 us
  waiting for transfers between devices  2510 us (78%)
  blocking collectives  501 us (16%)
  matrix products  155 us (5%)
    unnamed x2, blocking collectives  426 us
    reduce_scatter x1, waiting for transfers between devices, local(): lax.psum_scatter(up_grad, 'dp', scatter_dimension=0, tiled=True)  340 us
    reduce_scatter x1, waiting for transfers between devices, local(): lax.psum_scatter(down_grad, 'dp', scatter_dimension=1, tiled=True)  340 us
    reduce_scatter x1, waiting for transfers between devices, local(): lax.psum_scatter(gate_grad, 'dp', scatter_dimension=0, tiled=True)  339 us
    reduce_scatter x1, waiting for transfers between devices, local(): lax.psum_scatter(query_grad, 'dp', scatter_dimension=0, tiled=True)  297 us
    reduce_scatter x1, waiting for transfers between devices, local(): lax.psum_scatter(out_grad, 'dp', scatter_dimension=1, tiled=True)  297 us
    reduce_scatter x1, waiting for transfers between devices, local(): lax.psum_scatter(key_grad, 'dp', scatter_dimension=0, tiled=True)  276 us
    all_gather x1, waiting for transfers between devices, local(): lax.all_gather(w_down, 'dp', axis=1, tiled=True)  115 us
  transfers between devices with their start and end apart: 18, of which 14 were waited for; matrix products, arithmetic and copies ran while one was open for 4% of the time, Pallas kernels for 0%

commit v1 on v0

v1 whole, which is shorter than its diff:
```python
import math

import jax
import jax.numpy as jnp
from jax import lax
from jax.sharding import Mesh
from jax.sharding import PartitionSpec as P

HEADS = 32
KV_HEADS = 8
GROUP = HEADS // KV_HEADS
EPSILON = 1e-05
ROPE_BASE = 500000.0
MASKED = -1e30
GAIN_COLS = 128
BF = jnp.bfloat16
F32 = jnp.float32

SWAP = [(0, 1), (1, 0)]


def mm(left, right):
    return jnp.dot(left, right, preferred_element_type=F32)


def mm_nt(left, right):
    return lax.dot_general(left, right, (((1,), (1,)), ((), ())), preferred_element_type=F32)


def mm_tn(left, right):
    return lax.dot_general(left, right, (((0,), (0,)), ((), ())), preferred_element_type=F32)


AT = (0, 2, 1, 3)


def from_chip(value, k):
    return lax.ppermute(value, ("a", "t"), [(AT[(i + k) % 4], AT[i]) for i in range(4)])


def to_chip(value, k):
    return lax.ppermute(value, ("a", "t"), [(AT[i], AT[(i + k) % 4]) for i in range(4)])


def gather_rows(rows):
    mine = jnp.concatenate(
        [rows, from_chip(rows, 2), from_chip(rows, 1), from_chip(rows, 3)], axis=0
    )
    return jnp.concatenate([mine, lax.ppermute(mine, "c", SWAP)], axis=0)


def scatter_rows(partial):
    half = partial.shape[0] // 2
    other = lax.ppermute(partial[half:].astype(BF), "c", SWAP)
    chip = partial[:half] + other.astype(F32)
    part = half // 4
    own, p2, p1, p3 = (chip[i * part : (i + 1) * part] for i in range(4))
    total = own
    for piece, k in ((p2, 2), (p1, 1), (p3, 3)):
        total = total + to_chip(piece.astype(BF), k).astype(F32)
    return total


def spread(pack, a, c):
    _, r, n = pack.shape
    by_core = pack.reshape(2, 2, r, n)
    keep = lax.dynamic_index_in_dim(by_core, c, 1, keepdims=False)
    give = lax.dynamic_index_in_dim(by_core, 1 - c, 1, keepdims=False)
    got = lax.ppermute(give, "c", SWAP)
    first = c == 0
    both = jnp.concatenate([jnp.where(first, keep, got), jnp.where(first, got, keep)], axis=1)
    keep_a = lax.dynamic_index_in_dim(both, a, 0, keepdims=False)
    give_a = lax.dynamic_index_in_dim(both, 1 - a, 0, keepdims=False)
    got_a = lax.ppermute(give_a, "a", SWAP)
    first_a = a == 0
    return jnp.where(first_a, keep_a, got_a), jnp.where(first_a, got_a, keep_a)


def unspread(low, high, a, c):
    rows, n = low.shape
    r = rows // 2
    first_a = a == 0
    keep_a = jnp.where(first_a, low, high)
    give_a = jnp.where(first_a, high, low)
    got_a = lax.ppermute(give_a, "a", SWAP)
    quarters = jnp.stack([jnp.where(first_a, keep_a, got_a), jnp.where(first_a, got_a, keep_a)])
    quarters = quarters.reshape(2, 2, r, n)
    keep = lax.dynamic_index_in_dim(quarters, c, 1, keepdims=False)
    give = lax.dynamic_index_in_dim(quarters, 1 - c, 1, keepdims=False)
    got = lax.ppermute(give, "c", SWAP)
    first = c == 0
    return jnp.stack([jnp.where(first, keep, got), jnp.where(first, got, keep)], axis=1).reshape(
        4, r, n
    )


def quarters_of(weight):
    rows, columns = weight.shape
    return weight.reshape(rows, 4, columns // 4).transpose(1, 0, 2)


def whole_columns(quarters):
    _, rows, columns = quarters.shape
    return quarters.transpose(1, 0, 2).reshape(rows, 4 * columns)


def rotate(values, cosines, sines):
    half = values.shape[-1] // 2
    first, second = values[..., :half], values[..., half:]
    return jnp.concatenate([first * cosines - second * sines, second * cosines + first * sines], -1)


def norm_back(rescaled, factor, gain, upstream):
    inner = upstream * gain
    return factor * (inner - rescaled * jnp.mean(inner * rescaled, axis=-1, keepdims=True))


def local(
    tokens, segment_ids, attn_gain, w_query, w_key, w_value, w_out,
    mlp_gain, w_gate, w_up, w_down, cotangent,
):
    a, c, t = lax.axis_index("a"), lax.axis_index("c"), lax.axis_index("t")
    own, d_model = tokens.shape
    block = segment_ids.shape[0]
    r = w_query.shape[0]
    nq = w_query.shape[1] // 4
    nk = w_key.shape[1] // 4
    ff = w_gate.shape[1] // 4
    head = nk
    scale = 1.0 / math.sqrt(head)

    gains = jnp.stack([attn_gain, mlp_gain], axis=1)
    gains = jnp.pad(gains, ((0, 0), (0, GAIN_COLS - 2)))
    attn_pack = jnp.concatenate(
        [
            quarters_of(w_query),
            quarters_of(w_key),
            quarters_of(w_value),
            quarters_of(w_out.T),
            jnp.broadcast_to(gains, (4, r, GAIN_COLS)),
        ],
        axis=2,
    )
    attn_low, attn_high = spread(attn_pack, a, c)
    x_rows = gather_rows(tokens)
    attn_low = lax.all_gather(attn_low, ("z", "y"), axis=0, tiled=True)
    attn_high = lax.all_gather(attn_high, ("z", "y"), axis=0, tiled=True)
    attn_w = jnp.concatenate([attn_low, attn_high], axis=0)
    mlp_pack = jnp.concatenate(
        [quarters_of(w_gate), quarters_of(w_up), quarters_of(w_down.T)], axis=2
    )
    mlp_low, mlp_high = spread(mlp_pack, a, c)
    mlp_low = lax.all_gather(mlp_low, ("z", "y"), axis=0, tiled=True)
    mlp_high = lax.all_gather(mlp_high, ("z", "y"), axis=0, tiled=True)
    half_d = d_model // 2

    cut = nq + 2 * nk
    w_qkv, w_out_t = attn_w[:, :cut], attn_w[:, cut : cut + nq]
    gain_a = attn_w[:, cut + nq].astype(F32)
    gain_m = attn_w[:, cut + nq + 1].astype(F32)

    seg_pair = jnp.stack([segment_ids, lax.ppermute(segment_ids, "a", SWAP)])
    seg = jnp.concatenate([seg_pair, lax.ppermute(seg_pair, "c", SWAP)], axis=0)
    turn = jnp.stack([t, t ^ a, t, t ^ a])[:, None]
    seg = jnp.where(turn == 0, seg, jnp.roll(seg, own, axis=1))
    order = (jnp.arange(block, dtype=jnp.int32)[None, :] + turn * own) % block
    earlier = jnp.sum((seg[:, None, :] < seg[:, :, None]).astype(jnp.int32), axis=2)
    positions = order - earlier
    allowed = (seg[:, :, None] == seg[:, None, :]) & (order[:, None, :] <= order[:, :, None])
    frequency = jnp.exp(
        -math.log(ROPE_BASE) * (jnp.arange(head // 2).astype(F32) / (head // 2))
    )
    angles = positions.astype(F32)[:, :, None, None] * frequency
    cosines, sines = jnp.cos(angles), jnp.sin(angles)

    xf = x_rows.astype(F32)
    factor1 = lax.rsqrt(jnp.mean(xf * xf, axis=-1, keepdims=True) + EPSILON)
    u1 = xf * factor1
    normed = (u1 * gain_a).astype(BF)
    qkv = mm(normed, w_qkv)
    query = rotate(qkv[:, :nq].reshape(4, block, GROUP, head), cosines, sines).astype(BF)
    key = rotate(qkv[:, nq : nq + nk].reshape(4, block, 1, head), cosines, sines)
    key = key.astype(BF).reshape(4, block, head)
    value = qkv[:, nq + nk :].astype(BF).reshape(4, block, head)
    scores = jnp.einsum("nahd,nbd->nhab", query, key, preferred_element_type=F32) * scale
    scores = jnp.where(allowed[:, None], scores, MASKED)
    row_max = jnp.max(scores, axis=-1, keepdims=True)
    weights = jnp.exp(scores - row_max)
    probs = weights / jnp.sum(weights, axis=-1, keepdims=True)
    probs_b = probs.astype(BF)
    mixed = jnp.einsum("nhab,nbd->nahd", probs_b, value, preferred_element_type=F32)
    mixed = mixed.astype(BF).reshape(4 * block, nq)
    resid = tokens.astype(F32) + scatter_rows(mm_nt(mixed, w_out_t))

    factor2 = lax.rsqrt(jnp.mean(resid * resid, axis=-1, keepdims=True) + EPSILON)
    u2 = resid * factor2
    n2 = gather_rows((u2 * gain_m).astype(BF))
    c_rows = gather_rows(cotangent)
    gate_up = mm(n2[:, :half_d], mlp_low[:, : 2 * ff]) + mm(n2[:, half_d:], mlp_high[:, : 2 * ff])
    gate, up = gate_up[:, :ff], gate_up[:, ff:]
    sig = jax.nn.sigmoid(gate)
    silu = gate * sig
    hidden = (silu * up).astype(BF)
    d_hidden = mm(c_rows[:, :half_d], mlp_low[:, 2 * ff :]) + mm(
        c_rows[:, half_d:], mlp_high[:, 2 * ff :]
    )
    d_gate = (d_hidden * up * sig * (1.0 + gate * (1.0 - sig))).astype(BF)
    d_up = (d_hidden * silu).astype(BF)
    d_gu = jnp.concatenate([d_gate, d_up], axis=1)
    d_n2 = scatter_rows(
        jnp.concatenate(
            [mm_nt(d_gu, mlp_low[:, : 2 * ff]), mm_nt(d_gu, mlp_high[:, : 2 * ff])], axis=1
        )
    )

    def mlp_grads(part):
        grads = jnp.concatenate(
            [mm_tn(n2[:, part], d_gu).astype(BF), mm_tn(c_rows[:, part], hidden).astype(BF)], axis=1
        )
        return lax.psum_scatter(grads, ("z", "y"), scatter_dimension=0, tiled=True)

    g_low = mlp_grads(slice(0, half_d))
    g_high = mlp_grads(slice(half_d, d_model))
    out_part = jnp.concatenate(
        [mm_nt(hidden, mlp_low[:, 2 * ff :]), mm_nt(hidden, mlp_high[:, 2 * ff :])], axis=1
    )
    layer_output = (resid + scatter_rows(out_part)).astype(BF)

    upstream = cotangent.astype(F32)
    mlp_gain_part = jnp.sum(d_n2 * u2, axis=0)
    d_resid = upstream + norm_back(u2, factor2, gain_m, d_n2)
    d_branch = gather_rows(d_resid.astype(BF))

    out_grad = mm_tn(d_branch, mixed)
    d_mixed = mm(d_branch, w_out_t).astype(BF).reshape(4, block, GROUP, head)
    d_value = jnp.einsum("nhab,nahd->nbd", probs_b, d_mixed, preferred_element_type=F32)
    d_probs = jnp.einsum("nahd,nbd->nhab", d_mixed, value, preferred_element_type=F32)
    d_scores = (probs * (d_probs - jnp.sum(d_probs * probs, axis=-1, keepdims=True))).astype(BF)
    d_query = jnp.einsum("nhab,nbd->nahd", d_scores, key, preferred_element_type=F32) * scale
    d_key = jnp.einsum("nhab,nahd->nbd", d_scores, query, preferred_element_type=F32) * scale
    d_query = rotate(d_query, cosines, -sines).astype(BF).reshape(4 * block, nq)
    d_key = rotate(d_key[:, :, None, :], cosines, -sines).astype(BF).reshape(4 * block, nk)
    d_value = d_value.astype(BF).reshape(4 * block, nk)
    d_qkv = jnp.concatenate([d_query, d_key, d_value], axis=1)
    qkv_grad = mm_tn(normed, d_qkv)
    d_n1_part = mm_nt(d_qkv, w_qkv)
    attn_gain_part = jnp.sum(d_n1_part * u1, axis=0)
    d_n1 = scatter_rows(d_n1_part)
    input_grad = d_resid + norm_back(u1[:own], factor1[:own], gain_a, d_n1)

    gain_parts = jnp.stack([attn_gain_part, mlp_gain_part], axis=1).astype(BF)
    gain_parts = jnp.pad(gain_parts, ((0, 0), (0, GAIN_COLS - 2)))
    attn_grads = jnp.concatenate([qkv_grad.astype(BF), out_grad.astype(BF), gain_parts], axis=1)
    h_low = lax.psum_scatter(attn_grads[:half_d], ("z", "y"), scatter_dimension=0, tiled=True)
    h_high = lax.psum_scatter(attn_grads[half_d:], ("z", "y"), scatter_dimension=0, tiled=True)

    g = unspread(g_low, g_high, a, c).astype(F32)
    gate_grad = whole_columns(g[:, :, :ff])
    up_grad = whole_columns(g[:, :, ff : 2 * ff])
    down_grad = whole_columns(g[:, :, 2 * ff :]).T
    h = unspread(h_low, h_high, a, c).astype(F32)
    query_grad = whole_columns(h[:, :, :nq])
    key_grad = whole_columns(h[:, :, nq : nq + nk])
    value_grad = whole_columns(h[:, :, nq + nk : cut])
    out_grad = whole_columns(h[:, :, cut : cut + nq]).T
    gain_grads = jnp.sum(h[:, :, cut + nq : cut + nq + 2], axis=0).T
    gain_grads = gain_grads + lax.ppermute(gain_grads, "t", SWAP)
    return (
        layer_output, input_grad, gain_grads[0], query_grad, key_grad, value_grad, out_grad,
        gain_grads[1], gate_grad, up_grad, down_grad,
    )


def solution(mesh):
    fine = Mesh(mesh.devices.reshape(2, 4, 4, 2, 2), ("a", "z", "y", "c", "t"))
    dp = ("a", "z", "y", "c")
    rows = P(dp + ("t",), None)
    return jax.shard_map(
        local,
        mesh=fine,
        in_specs=(
            rows, P(dp), P(dp), P(dp, "t"), P(dp, "t"), P(dp, "t"), P("t", dp),
            P(dp), P(dp, "t"), P(dp, "t"), P("t", dp), rows,
        ),
        out_specs=(
            rows, rows, P(dp), P(dp, "t"), P(dp, "t"), P(dp, "t"), P("t", dp),
            P(dp), P(dp, "t"), P(dp, "t"), P("t", dp),
        ),
        check_vma=False,
    )
```

time: 3220 us -> 723 us (0.22)
  waiting for transfers between devices: 2510 us -> 433 us
  blocking collectives: 501 us -> 0 us
  local copies, waits for them, and re-layouts: 12.4 us -> 63.9 us
  starting transfers between devices: 0.89 us -> 50.7 us
  matrix products: 155 us -> 111 us
    reduce_scatter x11 -> x4, waiting for transfers between devices: 1930 us -> 231 us  [the longest x2 157 us: mlp_grads(): return lax.psum_scatter(grads, ('z', 'y'), scatter_dimension=0, tiled=True)]
    all_gather x7 -> x4, waiting for transfers between devices: 575 us -> 41 us  [the longest x1 36.6 us: local(): attn_high = lax.all_gather(attn_high, ('z', 'y'), axis=0, tiled=True)]
    unnamed x2 -> x0, blocking collectives: 426 us -> none
    ppermute x0 -> x43, waiting for transfers between devices: none -> 160 us  [the longest x12 61.8 us: from_chip(): lax.ppermute(value, ('a', 't'), [(AT[(i + k) % 4], AT[i]) for i in range(...]
    all_gather x4 -> x0, blocking collectives: 68.3 us -> none  [whole_rows(): return lax.all_gather(local_part, 'tensor', axis=0, tiled=True)]
    ppermute x0 -> x43, starting transfers between devices: none -> 50 us  [the longest x12 19.2 us: to_chip(): lax.ppermute(value, ('a', 't'), [(AT[i], AT[(i + k) % 4]) for i in range(...]
    dot_general x27 -> x23, matrix products: 155 us -> 106 us  [the longest x6 40.6 us: mm(): return jnp.dot(left, right, preferred_element_type=F32)]
  transfers between devices with their start and end apart: 18 -> 51, of which waited for: 14 -> 32; matrix products, arithmetic and copies ran while one was open for 4% -> 18% of each run, Pallas kernels for 0% -> 0%
where the time goes in v1:
time: 723 us; the launch traced here: 715 us
  waiting for transfers between devices  433 us (60%)
  matrix products  111 us (15%)
  local copies, waits for them, and re-layouts  63.9 us (9%)
  starting transfers between devices  50.7 us (7%)
  other arithmetic  41.4 us (6%)
  between operations  15.7 us (2%)
    reduce_scatter x2, waiting for transfers between devices, mlp_grads(): return lax.psum_scatter(grads, ('z', 'y'), scatter_dimension=0, tiled=True)  157 us
    reduce_scatter x1, waiting for transfers between devices, local(): lax.psum_scatter(attn_grads[half_d:], ('z', 'y'), scatter_dimension=0, ti...  73.8 us
    ppermute x12, waiting for transfers between devices, from_chip(): lax.ppermute(value, ('a', 't'), [(AT[(i + k) % 4], AT[i]) for i in range(...  61.8 us
    ppermute x12, waiting for transfers between devices, to_chip(): lax.ppermute(value, ('a', 't'), [(AT[i], AT[(i + k) % 4]) for i in range(...  43.5 us
    dot_general x6, matrix products, mm(): return jnp.dot(left, right, preferred_element_type=F32)  40.6 us
    all_gather x1, waiting for transfers between devices, local(): attn_high = lax.all_gather(attn_high, ('z', 'y'), axis=0, tiled=True)  36.6 us
    dot_general x6, matrix products, mm_tn(): lax.dot_general(left, right, (((0,), (0,)), ((), ())), preferred_element_...  28.6 us
    dot_general x6, matrix products, mm_nt(): lax.dot_general(left, right, (((1,), (1,)), ((), ())), preferred_element_...  28.5 us
  transfers between devices with their start and end apart: 51, of which 32 were waited for; matrix products, arithmetic and copies ran while one was open for 18% of the time, Pallas kernels for 0%

profile of v1, /device:TPU:0, one launch (start us, length us, event | category | flops | bytes accessed | tf_op | source)
XLA Modules:
  0.0 715.1 jit_solution(5764182048361856722)
XLA Ops:
  14.9 3.3 collective-permute-done.5
  25.7 9.6 %collective-permute-done.17 = bf16[64,3072]{1,0:T(8,128)(2,1)S(1)} collective-permute-done((bf16[64,3072]{1,0:T(8,128)(2,1)S(1)}, bf16[64,3072]{1,0:T(8,128)(2,1)S(1)}, u32[]{:S(2)}, u32[]{:S(2)}) %collective-permute-start.17) | collective-permute-done | bytes 393248 | tf_op jit(solution)/shard_map/ppermute | solution.py:74
  43.1 16.4 %collective-permute-done.6 = s32[224]{0:T(256)S(1)} collective-permute-done((s32[224]{0:T(256)S(1)}, s32[224]{0:T(256)S(1)}, u32[]{:S(2)}, u32[]{:S(2)}) %collective-permute-start.6) | collective-permute-done | bytes 928 | tf_op jit(solution)/shard_map/ppermute | solution.py:162
  67.8 2.9 constant_dynamic-update-slice_fusion
  75.1 36.6 %all-gather.7.cloned.1.call-done = bf16[1024,768]{1,0:T(8,128)(2,1)} async-done(((bf16[64,768]{1,0:T(8,128)(2,1)}), bf16[1024,768]{1,0:T(8,128)(2,1)}) %all-gather.7.cloned.1.call-update) | async-done | bytes 1572880 | tf_op jit(solution)/shard_map/all_gather | solution.py:147
  113.8 4.6 fusion.46
  124.3 3.0 reshape.475
  132.1 5.0 fusion.146
  156.0 3.9 collective-permute-done.24
  161.2 18.8 %collective-permute-done.23 = bf16[112,2048]{1,0:T(8,128)(2,1)S(1)} collective-permute-done((bf16[112,2048]{1,0:T(8,128)(2,1)S(1)}, bf16[112,2048]{1,0:T(8,128)(2,1)S(1)}, u32[]{:S(2)}, u32[]{:S(2)}) %collective-permute-start.23) | collective-permute-done | bytes 458784 | tf_op jit(solution)/shard_map/ppermute | solution.py:38
  181.5 7.8 %collective-permute-done.11 = bf16[112,2048]{1,0:T(8,128)(2,1)S(1)} collective-permute-done((bf16[112,2048]{1,0:T(8,128)(2,1)S(1)}, bf16[112,2048]{1,0:T(8,128)(2,1)S(1)}, u32[]{:S(2)}, u32[]{:S(2)}) %collective-permute-start.11) | collective-permute-done | bytes 458784 | tf_op jit(solution)/shard_map/ppermute | solution.py:42
  195.4 19.7 %collective-permute-done.14 = bf16[112,2048]{1,0:T(8,128)(2,1)S(1)} collective-permute-done((bf16[112,2048]{1,0:T(8,128)(2,1)S(1)}, bf16[112,2048]{1,0:T(8,128)(2,1)S(1)}, u32[]{:S(2)}, u32[]{:S(2)}) %collective-permute-start.14) | collective-permute-done | bytes 458784 | tf_op jit(solution)/shard_map/ppermute | solution.py:38
  220.4 6.2 fusion.24
  226.6 7.7 %fusion.4 = f32[896,2048]{1,0:T(8,128)} fusion(bf16[1024,3072]{1,0:T(8,128)(2,1)S(1)} %copy-done.32, bf16[896,2048]{1,0:T(8,128)(2,1)} %constant_dynamic-update-slice_fusion.7), kind=kOutput, calls=%fused_computation.16 | convolution fusion | flops 3758096384 | bytes 13369344 | tf_op jit(solution)/shard_map/dot_general | solution.py:23
  234.3 4.4 all-gather.9.cloned.1.call-done
  238.7 11.9 %fusion.20 = f32[896,2048]{1,0:T(8,128)} fusion(f32[896,2048]{1,0:T(8,128)} %fusion.4, bf16[1024,3072]{1,0:T(8,128)(2,1)} %all-gather.9.cloned.1.call-done, bf16[896,2048]{1,0:T(8,128)(2,1)} %constant_dynamic-update-slice_fusion.7), kind=kOutput, calls=%fused_computation.47 | convolution fusion | flops 3759931392 | bytes 20709376 | tf_op jit(solution)/shard_map/dot_general | solution.py:23
  250.6 7.1 multiply_convert_fusion.2
  257.8 4.0 fusion.2
  261.8 4.0 fusion.6
  266.2 3.8 collective-permute-done.26
  271.0 3.1 collective-permute-start.27
  276.0 9.9 %collective-permute-done.27 = bf16[112,2048]{1,0:T(8,128)(2,1)S(1)} collective-permute-done((bf16[112,2048]{1,0:T(8,128)(2,1)S(1)}, bf16[112,2048]{1,0:T(8,128)(2,1)S(1)}, u32[]{:S(2)}, u32[]{:S(2)}) %collective-permute-start.27) | collective-permute-done | bytes 458784 | tf_op jit(solution)/shard_map/ppermute | solution.py:42
  286.0 9.0 %collective-permute-done.29 = bf16[112,2048]{1,0:T(8,128)(2,1)S(1)} collective-permute-done((bf16[112,2048]{1,0:T(8,128)(2,1)S(1)}, bf16[112,2048]{1,0:T(8,128)(2,1)S(1)}, u32[]{:S(2)}, u32[]{:S(2)}) %collective-permute-start.29) | collective-permute-done | bytes 458784 | tf_op jit(solution)/shard_map/ppermute | solution.py:42
  300.9 8.7 %collective-permute-done.32 = bf16[112,2048]{1,0:T(8,128)(2,1)S(1)} collective-permute-done((bf16[112,2048]{1,0:T(8,128)(2,1)S(1)}, bf16[112,2048]{1,0:T(8,128)(2,1)S(1)}, u32[]{:S(2)}, u32[]{:S(2)}) %collective-permute-start.32) | collective-permute-done | bytes 458784 | tf_op jit(solution)/shard_map/ppermute | solution.py:38
  309.5 9.1 %collective-permute-done.31 = bf16[112,2048]{1,0:T(8,128)(2,1)S(1)} collective-permute-done((bf16[112,2048]{1,0:T(8,128)(2,1)S(1)}, bf16[112,2048]{1,0:T(8,128)(2,1)S(1)}, u32[]{:S(2)}, u32[]{:S(2)}) %collective-permute-start.31) | collective-permute-done | bytes 458784 | tf_op jit(solution)/shard_map/ppermute | solution.py:38
  321.3 3.0 collective-permute-done.33
  324.5 3.2 convolution_convert_fusion.7
  333.5 3.0 fusion.54
  349.9 4.2 convolution_convert_fusion.2
  354.1 10.0 %multiply_reduce_fusion = (bf16[2048]{0:T(1024)(128)(2,1)S(1)}, f32[896,2048]{1,0:T(8,128)}, f32[896,2048]{1,0:T(8,128)}) fusion(f32[896]{0:T(1024)S(1)} %copy-done.25, bf16[896,2048]{1,0:T(8,128)(2,1)} %constant_dynamic-update-slice_fusion, bf16[896,384]{0,1:T(8,128)(2,1)S(1)} %constant_dynamic-update-slice_fusion.22, bf16[2048,768]{1,0:T(8,128)(2,1)S(1)} %copy-done.1), kind=kOutput, calls=%fused_computation.8 | convolution fusion | flops 1416624128 | bytes 20619264 | tf_op jit(solution)/shard_map/dot_general | solution.py:27
  371.9 4.6 convolution_convert_fusion.5
  376.6 6.5 convolution_convert_fusion.1
  383.1 3.2 pad_maximum_fusion
  386.4 4.6 convolution_convert_fusion.4
  391.0 6.5 convolution_convert_fusion
  397.5 3.1 pad_maximum_fusion.1
  400.6 4.4 fusion.26
  405.1 3.9 fusion.30
  417.6 3.1 collective-permute-start.37
  425.8 5.9 collective-permute-done.35
  432.9 8.1 %collective-permute-done.37 = bf16[112,2048]{1,0:T(8,128)(2,1)S(1)} collective-permute-done((bf16[112,2048]{1,0:T(8,128)(2,1)S(1)}, bf16[112,2048]{1,0:T(8,128)(2,1)S(1)}, u32[]{:S(2)}, u32[]{:S(2)}) %collective-permute-start.37) | collective-permute-done | bytes 458784 | tf_op jit(solution)/shard_map/ppermute | solution.py:42
  444.0 73.8 %reduce-scatter.15.cloned.1.call-done = bf16[64,768]{1,0:T(8,128)(2,1)} async-done(((bf16[1024,768]{1,0:T(8,128)(2,1)}), bf16[64,768]{1,0:T(8,128)(2,1)}) %reduce-scatter.15.cloned.1.call-update) | async-done | bytes 98320 | tf_op jit(solution)/shard_map/reduce_scatter | solution.py:255
  520.2 3.2 collective-permute-done.38
  524.5 4.3 multiply_add_fusion
  528.9 73.0 %reduce-scatter.9.cloned.1.call-done = bf16[64,3072]{1,0:T(8,128)(2,1)} async-done(((bf16[1024,3072]{1,0:T(8,128)(2,1)}), bf16[64,3072]{1,0:T(8,128)(2,1)}) %reduce-scatter.9.cloned.1.call-update) | async-done | bytes 393232 | tf_op jit(solution)/shard_map/reduce_scatter | solution.py:220
  601.9 84.3 %reduce-scatter.11.cloned.1.call-done = bf16[64,3072]{1,0:T(8,128)(2,1)} async-done(((bf16[1024,3072]{1,0:T(8,128)(2,1)}), bf16[64,3072]{1,0:T(8,128)(2,1)}) %reduce-scatter.11.cloned.1.call-update) | async-done | bytes 393232 | tf_op jit(solution)/shard_map/reduce_scatter | solution.py:220
  689.0 8.2 %collective-permute-done.41 = bf16[64,3072]{1,0:T(8,128)(2,1)S(1)} collective-permute-done((bf16[64,3072]{1,0:T(8,128)(2,1)S(1)}, bf16[64,3072]{1,0:T(8,128)(2,1)S(1)}, u32[]{:S(2)}, u32[]{:S(2)}) %collective-permute-start.41) | collective-permute-done | bytes 393248 | tf_op jit(solution)/shard_map/ppermute | solution.py:85
  698.4 3.1 collective-permute-start.40
  (330 shorter events, 152.1 us)
Async XLA Ops:
  7.2 66.4 %all-gather.5.cloned.1.call-start = ((), (), s32[]{:S(2)}) async-start(), calls=%async_computation.4 | async-start | bytes 1671168 | tf_op jit(solution)/shard_map/all_gather | solution.py:146
  13.2 4.9 collective-permute-start.5
  18.9 92.8 %all-gather.7.cloned.1.call-start = ((), (), s32[]{:S(2)}) async-start(), calls=%async_computation.5 | async-start | bytes 1671168 | tf_op jit(solution)/shard_map/all_gather | solution.py:147
  21.5 199.0 %all-gather.11.cloned.1.call-start = ((), (), s32[]{:S(2)}) async-start(), calls=%async_computation.7 | async-start | bytes 6684672 | tf_op jit(solution)/shard_map/all_gather | solution.py:154
  24.1 11.2 %collective-permute-start.17 = (bf16[64,3072]{1,0:T(8,128)(2,1)S(1)}, bf16[64,3072]{1,0:T(8,128)(2,1)S(1)}, u32[]{:S(2)}, u32[]{:S(2)}) collective-permute-start(bf16[64,3072]{1,0:T(8,128)(2,1)S(1)} %fusion.80), channel_id=1, source_target_pairs={{0,64},{64,0},{1,65},{65,1},{2,66},{66,2},{3,67},{67,3},{4,68},{68... | collective-permute-start | bytes 1179656 | tf_op jit(solution)/shard_map/ppermute | solution.py:74
  36.4 202.3 %all-gather.9.cloned.1.call-start = ((), (), s32[]{:S(2)}) async-start(), calls=%async_computation.6 | async-start | bytes 6684672 | tf_op jit(solution)/shard_map/all_gather | solution.py:153
  36.4 24.4 %collective-permute-start.2 = (bf16[112,2048]{1,0:T(8,128)(2,1)S(1)}, bf16[112,2048]{1,0:T(8,128)(2,1)S(1)}, u32[]{:S(2)}, u32[]{:S(2)}) collective-permute-start(bf16[112,2048]{1,0:T(8,128)(2,1)S(1)} %copy-done.4), channel_id=1, source_target_pairs={{65,0},{0,64},{64,1},{1,65},{67,2},{2,66},{66,3},{3,67},{69,4},{4,... | collective-permute-start | bytes 1376264 | tf_op jit(solution)/shard_map/ppermute | solution.py:38
  38.1 22.7 %collective-permute-start.1 = (bf16[112,2048]{1,0:T(8,128)(2,1)S(1)}, bf16[112,2048]{1,0:T(8,128)(2,1)S(1)}, u32[]{:S(2)}, u32[]{:S(2)}) collective-permute-start(bf16[112,2048]{1,0:T(8,128)(2,1)S(1)} %copy-done.4), channel_id=1, source_target_pairs={{64,0},{1,64},{65,1},{0,65},{66,2},{3,66},{67,3},{2,67},{68,4},{5,... | collective-permute-start | bytes 1376264 | tf_op jit(solution)/shard_map/ppermute | solution.py:38
  39.7 21.1 %collective-permute-start = (bf16[112,2048]{1,0:T(8,128)(2,1)S(1)}, bf16[112,2048]{1,0:T(8,128)(2,1)S(1)}, u32[]{:S(2)}, u32[]{:S(2)}) collective-permute-start(bf16[112,2048]{1,0:T(8,128)(2,1)S(1)} %copy-done.4), channel_id=1, source_target_pairs={{1,0},{65,64},{0,1},{64,65},{3,2},{67,66},{2,3},{66,67},{5,4},{69,... | collective-permute-start | bytes 1376264 | tf_op jit(solution)/shard_map/ppermute | solution.py:38
  41.6 17.9 %collective-permute-start.6 = (s32[224]{0:T(256)S(1)}, s32[224]{0:T(256)S(1)}, u32[]{:S(2)}, u32[]{:S(2)}) collective-permute-start(s32[224]{0:T(256)S(1)} %copy-done.26), channel_id=1, source_target_pairs={{0,64},{64,0},{1,65},{65,1},{2,66},{66,2},{3,67},{67,3},{4,68},{68... | collective-permute-start | bytes 2696 | tf_op jit(solution)/shard_map/ppermute | solution.py:162
  62.2 5.6 collective-permute-start.3
  67.5 376.5 %reduce-scatter.13.cloned.1.call-start = ((), (), s32[]{:S(2)}) async-start(), calls=%async_computation.10 | async-start | bytes 1671168 | tf_op jit(solution)/shard_map/reduce_scatter | solution.py:254
  145.5 5.8 collective-permute-start.8
  146.3 13.6 %collective-permute-start.24 = (bf16[112,2048]{1,0:T(8,128)(2,1)S(1)}, bf16[112,2048]{1,0:T(8,128)(2,1)S(1)}, u32[]{:S(2)}, u32[]{:S(2)}) collective-permute-start(bf16[112,2048]{1,0:T(8,128)(2,1)S(1)} %copy-done.3), channel_id=1, source_target_pairs={{65,0},{0,64},{64,1},{1,65},{67,2},{2,66},{66,3},{3,67},{69,4},{4,... | collective-permute-start | bytes 1376264 | tf_op jit(solution)/shard_map/ppermute | solution.py:38
  147.7 32.2 %collective-permute-start.23 = (bf16[112,2048]{1,0:T(8,128)(2,1)S(1)}, bf16[112,2048]{1,0:T(8,128)(2,1)S(1)}, u32[]{:S(2)}, u32[]{:S(2)}) collective-permute-start(bf16[112,2048]{1,0:T(8,128)(2,1)S(1)} %copy-done.3), channel_id=1, source_target_pairs={{64,0},{1,64},{65,1},{0,65},{66,2},{3,66},{67,3},{2,67},{68,4},{5,... | collective-permute-start | bytes 1376264 | tf_op jit(solution)/shard_map/ppermute | solution.py:38
  149.5 30.4 %collective-permute-start.22 = (bf16[112,2048]{1,0:T(8,128)(2,1)S(1)}, bf16[112,2048]{1,0:T(8,128)(2,1)S(1)}, u32[]{:S(2)}, u32[]{:S(2)}) collective-permute-start(bf16[112,2048]{1,0:T(8,128)(2,1)S(1)} %copy-done.3), channel_id=1, source_target_pairs={{1,0},{65,64},{0,1},{64,65},{3,2},{67,66},{2,3},{66,67},{5,4},{69,... | collective-permute-start | bytes 1376264 | tf_op jit(solution)/shard_map/ppermute | solution.py:38
  152.3 29.2 %collective-permute-start.9 = (bf16[112,2048]{1,0:T(8,128)(2,1)S(1)}, bf16[112,2048]{1,0:T(8,128)(2,1)S(1)}, u32[]{:S(2)}, u32[]{:S(2)}) collective-permute-start(bf16[112,2048]{1,0:T(8,128)(2,1)S(1)} %get-tuple-element.50), channel_id=1, source_target_pairs={{0,1},{64,65},{1,0},{65,64},{2,3},{66,67},{3,2},{67,66},{4,5},{68,... | collective-permute-start | bytes 1376264 | tf_op jit(solution)/shard_map/ppermute | solution.py:42
  154.2 35.1 %collective-permute-start.11 = (bf16[112,2048]{1,0:T(8,128)(2,1)S(1)}, bf16[112,2048]{1,0:T(8,128)(2,1)S(1)}, u32[]{:S(2)}, u32[]{:S(2)}) collective-permute-start(bf16[112,2048]{1,0:T(8,128)(2,1)S(1)} %get-tuple-element.51), channel_id=1, source_target_pairs={{0,65},{64,0},{1,64},{65,1},{2,67},{66,2},{3,66},{67,3},{4,69},{68... | collective-permute-start | bytes 1376264 | tf_op jit(solution)/shard_map/ppermute | solution.py:42
  159.9 30.3 %collective-permute-start.10 = (bf16[112,2048]{1,0:T(8,128)(2,1)S(1)}, bf16[112,2048]{1,0:T(8,128)(2,1)S(1)}, u32[]{:S(2)}, u32[]{:S(2)}) collective-permute-start(bf16[112,2048]{1,0:T(8,128)(2,1)S(1)} %get-tuple-element.52), channel_id=1, source_target_pairs={{0,64},{64,1},{1,65},{65,0},{2,66},{66,3},{3,67},{67,2},{4,68},{68... | collective-permute-start | bytes 1376264 | tf_op jit(solution)/shard_map/ppermute | solution.py:42
  180.1 35.4 %collective-permute-start.25 = (bf16[448,2048]{1,0:T(8,128)(2,1)S(1)}, bf16[448,2048]{1,0:T(8,128)(2,1)S(1)}, u32[]{:S(2)}, u32[]{:S(2)}) collective-permute-start(bf16[448,2048]{1,0:T(8,128)(2,1)S(1)} %pad_maximum_fusion.8), channel_id=1, source_target_pairs={{0,2},{2,0},{1,3},{3,1},{4,6},{6,4},{5,7},{7,5},{8,10},{10,8},{9,1... | collective-permute-start | bytes 5505032 | tf_op jit(solution)/shard_map/ppermute | solution.py:49
  191.6 23.5 %collective-permute-start.14 = (bf16[112,2048]{1,0:T(8,128)(2,1)S(1)}, bf16[112,2048]{1,0:T(8,128)(2,1)S(1)}, u32[]{:S(2)}, u32[]{:S(2)}) collective-permute-start(bf16[112,2048]{1,0:T(8,128)(2,1)S(1)} %get-tuple-element.27), channel_id=1, source_target_pairs={{65,0},{0,64},{64,1},{1,65},{67,2},{2,66},{66,3},{3,67},{69,4},{4,... | collective-permute-start | bytes 1376264 | tf_op jit(solution)/shard_map/ppermute | solution.py:38
  192.1 22.9 %collective-permute-start.13 = (bf16[112,2048]{1,0:T(8,128)(2,1)S(1)}, bf16[112,2048]{1,0:T(8,128)(2,1)S(1)}, u32[]{:S(2)}, u32[]{:S(2)}) collective-permute-start(bf16[112,2048]{1,0:T(8,128)(2,1)S(1)} %get-tuple-element.27), channel_id=1, source_target_pairs={{64,0},{1,64},{65,1},{0,65},{66,2},{3,66},{67,3},{2,67},{68,4},{5,... | collective-permute-start | bytes 1376264 | tf_op jit(solution)/shard_map/ppermute | solution.py:38
  194.8 20.3 %collective-permute-start.12 = (bf16[112,2048]{1,0:T(8,128)(2,1)S(1)}, bf16[112,2048]{1,0:T(8,128)(2,1)S(1)}, u32[]{:S(2)}, u32[]{:S(2)}) collective-permute-start(bf16[112,2048]{1,0:T(8,128)(2,1)S(1)} %get-tuple-element.27), channel_id=1, source_target_pairs={{1,0},{65,64},{0,1},{64,65},{3,2},{67,66},{2,3},{66,67},{5,4},{69,... | collective-permute-start | bytes 1376264 | tf_op jit(solution)/shard_map/ppermute | solution.py:38
  215.2 3.9 collective-permute-start.15
  266.1 3.9 collective-permute-start.26
  271.0 15.0 %collective-permute-start.27 = (bf16[112,2048]{1,0:T(8,128)(2,1)S(1)}, bf16[112,2048]{1,0:T(8,128)(2,1)S(1)}, u32[]{:S(2)}, u32[]{:S(2)}) collective-permute-start(bf16[112,2048]{1,0:T(8,128)(2,1)S(1)} %get-tuple-element.44), channel_id=1, source_target_pairs={{0,1},{64,65},{1,0},{65,64},{2,3},{66,67},{3,2},{67,66},{4,5},{68,... | collective-permute-start | bytes 1376264 | tf_op jit(solution)/shard_map/ppermute | solution.py:42
  274.0 21.0 %collective-permute-start.29 = (bf16[112,2048]{1,0:T(8,128)(2,1)S(1)}, bf16[112,2048]{1,0:T(8,128)(2,1)S(1)}, u32[]{:S(2)}, u32[]{:S(2)}) collective-permute-start(bf16[112,2048]{1,0:T(8,128)(2,1)S(1)} %get-tuple-element.45), channel_id=1, source_target_pairs={{0,65},{64,0},{1,64},{65,1},{2,67},{66,2},{3,66},{67,3},{4,69},{68... | collective-permute-start | bytes 1376264 | tf_op jit(solution)/shard_map/ppermute | solution.py:42
  275.2 19.8 %collective-permute-start.28 = (bf16[112,2048]{1,0:T(8,128)(2,1)S(1)}, bf16[112,2048]{1,0:T(8,128)(2,1)S(1)}, u32[]{:S(2)}, u32[]{:S(2)}) collective-permute-start(bf16[112,2048]{1,0:T(8,128)(2,1)S(1)} %get-tuple-element.46), channel_id=1, source_target_pairs={{0,64},{64,1},{1,65},{65,0},{2,66},{66,3},{3,67},{67,2},{4,68},{68... | collective-permute-start | bytes 1376264 | tf_op jit(solution)/shard_map/ppermute | solution.py:42
  295.9 13.7 %collective-permute-start.32 = (bf16[112,2048]{1,0:T(8,128)(2,1)S(1)}, bf16[112,2048]{1,0:T(8,128)(2,1)S(1)}, u32[]{:S(2)}, u32[]{:S(2)}) collective-permute-start(bf16[112,2048]{1,0:T(8,128)(2,1)S(1)} %get-tuple-element.20), channel_id=1, source_target_pairs={{65,0},{0,64},{64,1},{1,65},{67,2},{2,66},{66,3},{3,67},{69,4},{4,... | collective-permute-start | bytes 1376264 | tf_op jit(solution)/shard_map/ppermute | solution.py:38
  297.4 21.3 %collective-permute-start.31 = (bf16[112,2048]{1,0:T(8,128)(2,1)S(1)}, bf16[112,2048]{1,0:T(8,128)(2,1)S(1)}, u32[]{:S(2)}, u32[]{:S(2)}) collective-permute-start(bf16[112,2048]{1,0:T(8,128)(2,1)S(1)} %get-tuple-element.20), channel_id=1, source_target_pairs={{64,0},{1,64},{65,1},{0,65},{66,2},{3,66},{67,3},{2,67},{68,4},{5,... | collective-permute-start | bytes 1376264 | tf_op jit(solution)/shard_map/ppermute | solution.py:38
  299.2 21.1 %collective-permute-start.30 = (bf16[112,2048]{1,0:T(8,128)(2,1)S(1)}, bf16[112,2048]{1,0:T(8,128)(2,1)S(1)}, u32[]{:S(2)}, u32[]{:S(2)}) collective-permute-start(bf16[112,2048]{1,0:T(8,128)(2,1)S(1)} %get-tuple-element.20), channel_id=1, source_target_pairs={{1,0},{65,64},{0,1},{64,65},{3,2},{67,66},{2,3},{66,67},{5,4},{69,... | collective-permute-start | bytes 1376264 | tf_op jit(solution)/shard_map/ppermute | solution.py:38
  320.5 3.9 collective-permute-start.33
  369.0 148.7 %reduce-scatter.15.cloned.1.call-start = ((), (), s32[]{:S(2)}) async-start(), calls=%async_computation.11 | async-start | bytes 1671168 | tf_op jit(solution)/shard_map/reduce_scatter | solution.py:255
  371.7 230.2 %reduce-scatter.9.cloned.1.call-start = ((), (), s32[]{:S(2)}) async-start(), calls=%async_computation.8 | async-start | bytes 6684672 | tf_op jit(solution)/shard_map/reduce_scatter | solution.py:220
  386.3 299.9 %reduce-scatter.11.cloned.1.call-start = ((), (), s32[]{:S(2)}) async-start(), calls=%async_computation.9 | async-start | bytes 6684672 | tf_op jit(solution)/shard_map/reduce_scatter | solution.py:220
  409.3 3.9 collective-permute-start.18
  409.8 5.9 collective-permute-start.34
  416.7 15.0 %collective-permute-start.35 = (bf16[112,2048]{1,0:T(8,128)(2,1)S(1)}, bf16[112,2048]{1,0:T(8,128)(2,1)S(1)}, u32[]{:S(2)}, u32[]{:S(2)}) collective-permute-start(bf16[112,2048]{1,0:T(8,128)(2,1)S(1)} %get-tuple-element.41), channel_id=1, source_target_pairs={{0,1},{64,65},{1,0},{65,64},{2,3},{66,67},{3,2},{67,66},{4,5},{68,... | collective-permute-start | bytes 1376264 | tf_op jit(solution)/shard_map/ppermute | solution.py:42
  417.6 23.4 %collective-permute-start.37 = (bf16[112,2048]{1,0:T(8,128)(2,1)S(1)}, bf16[112,2048]{1,0:T(8,128)(2,1)S(1)}, u32[]{:S(2)}, u32[]{:S(2)}) collective-permute-start(bf16[112,2048]{1,0:T(8,128)(2,1)S(1)} %get-tuple-element.42), channel_id=1, source_target_pairs={{0,65},{64,0},{1,64},{65,1},{2,67},{66,2},{3,66},{67,3},{4,69},{68... | collective-permute-start | bytes 1376264 | tf_op jit(solution)/shard_map/ppermute | solution.py:42
  420.7 20.9 %collective-permute-start.36 = (bf16[112,2048]{1,0:T(8,128)(2,1)S(1)}, bf16[112,2048]{1,0:T(8,128)(2,1)S(1)}, u32[]{:S(2)}, u32[]{:S(2)}) collective-permute-start(bf16[112,2048]{1,0:T(8,128)(2,1)S(1)} %get-tuple-element.43), channel_id=1, source_target_pairs={{0,64},{64,1},{1,65},{65,0},{2,66},{66,3},{3,67},{67,2},{4,68},{68... | collective-permute-start | bytes 1376264 | tf_op jit(solution)/shard_map/ppermute | solution.py:42
  421.8 102.6 %collective-permute-start.19 = (bf16[112,2048]{1,0:T(8,128)(2,1)}, bf16[112,2048]{1,0:T(8,128)(2,1)}, u32[]{:S(2)}, u32[]{:S(2)}) collective-permute-start(bf16[112,2048]{1,0:T(8,128)(2,1)} %get-tuple-element.47), channel_id=1, source_target_pairs={{0,1},{64,65},{1,0},{65,64},{2,3},{66,67},{3,2},{67,66},{4,5},{68,... | collective-permute-start | bytes 1376264 | tf_op jit(solution)/shard_map/ppermute | solution.py:42
  423.7 100.8 %collective-permute-start.21 = (bf16[112,2048]{1,0:T(8,128)(2,1)}, bf16[112,2048]{1,0:T(8,128)(2,1)}, u32[]{:S(2)}, u32[]{:S(2)}) collective-permute-start(bf16[112,2048]{1,0:T(8,128)(2,1)} %get-tuple-element.48), channel_id=1, source_target_pairs={{0,65},{64,0},{1,64},{65,1},{2,67},{66,2},{3,66},{67,3},{4,69},{68... | collective-permute-start | bytes 1376264 | tf_op jit(solution)/shard_map/ppermute | solution.py:42
  431.7 92.7 %collective-permute-start.20 = (bf16[112,2048]{1,0:T(8,128)(2,1)}, bf16[112,2048]{1,0:T(8,128)(2,1)}, u32[]{:S(2)}, u32[]{:S(2)}) collective-permute-start(bf16[112,2048]{1,0:T(8,128)(2,1)} %get-tuple-element.49), channel_id=1, source_target_pairs={{0,64},{64,1},{1,65},{65,0},{2,66},{66,3},{3,67},{67,2},{4,68},{68... | collective-permute-start | bytes 1376264 | tf_op jit(solution)/shard_map/ppermute | solution.py:42
  518.7 4.7 collective-permute-start.38
  524.3 4.5 collective-permute-start.39
  687.3 9.9 %collective-permute-start.41 = (bf16[64,3072]{1,0:T(8,128)(2,1)S(1)}, bf16[64,3072]{1,0:T(8,128)(2,1)S(1)}, u32[]{:S(2)}, u32[]{:S(2)}) collective-permute-start(bf16[64,3072]{1,0:T(8,128)(2,1)S(1)} %broadcast_select_fusion.2), channel_id=1, source_target_pairs={{0,64},{64,0},{1,65},{65,1},{2,66},{66,2},{3,67},{67,3},{4,68},{68... | collective-permute-start | bytes 1179656 | tf_op jit(solution)/shard_map/ppermute | solution.py:85
  698.3 6.7 collective-permute-start.42
  698.4 5.9 collective-permute-start.40
  (50 other events, 837.5 us)
Sparse Core Ops, SparseCore 0:
  19.0 46.6 all-gather.4
  68.4 43.2 all-gather.6
  114.4 60.6 all-gather.10
  177.6 60.9 all-gather.8
  369.1 72.4 reduce-scatter.12
  444.7 72.9 reduce-scatter.14
  521.2 80.6 reduce-scatter.8
  605.4 80.8 reduce-scatter.10

commit v2 on v1

v2 whole, which is shorter than its diff:
```python
import math

import jax
import jax.numpy as jnp
from jax import lax
from jax.experimental import pallas as pl
from jax.experimental.pallas import tpu as pltpu
from jax.sharding import Mesh
from jax.sharding import PartitionSpec as P

HEADS = 32
KV_HEADS = 8
GROUP = HEADS // KV_HEADS
EPSILON = 1e-05
ROPE_BASE = 500000.0
MASKED = -1e30
GAIN_COLS = 128
VMEM_LIMIT = 56 * 2**20
BF = jnp.bfloat16
F32 = jnp.float32

SWAP = [(0, 1), (1, 0)]


def mm(left, right):
    return jnp.dot(left, right, preferred_element_type=F32)


def mm_nt(left, right):
    return lax.dot_general(left, right, (((1,), (1,)), ((), ())), preferred_element_type=F32)


def mm_tn(left, right):
    return lax.dot_general(left, right, (((0,), (0,)), ((), ())), preferred_element_type=F32)


AT = (0, 2, 1, 3)


def from_chip(value, k):
    return lax.ppermute(value, ("a", "t"), [(AT[(i + k) % 4], AT[i]) for i in range(4)])


def to_chip(value, k):
    return lax.ppermute(value, ("a", "t"), [(AT[i], AT[(i + k) % 4]) for i in range(4)])


def gather_rows(rows):
    mine = [rows, from_chip(rows, 2), from_chip(rows, 1), from_chip(rows, 3)]
    return mine + [lax.ppermute(piece, "c", SWAP) for piece in mine]


def scatter_rows(mine, other):
    got = lax.ppermute(other, "c", SWAP)
    rows = mine.shape[0] // 4
    chip = [
        mine[i * rows : (i + 1) * rows].astype(F32) + got[i * rows : (i + 1) * rows].astype(F32)
        for i in range(4)
    ]
    total = chip[0]
    for i, k in ((1, 2), (2, 1), (3, 3)):
        total = total + to_chip(chip[i].astype(BF), k).astype(F32)
    return total


def spread(pack, a, c):
    _, r, n = pack.shape
    by_core = pack.reshape(2, 2, r, n)
    keep = lax.dynamic_index_in_dim(by_core, c, 1, keepdims=False)
    give = lax.dynamic_index_in_dim(by_core, 1 - c, 1, keepdims=False)
    got = lax.ppermute(give, "c", SWAP)
    first = c == 0
    both = jnp.concatenate([jnp.where(first, keep, got), jnp.where(first, got, keep)], axis=1)
    keep_a = lax.dynamic_index_in_dim(both, a, 0, keepdims=False)
    give_a = lax.dynamic_index_in_dim(both, 1 - a, 0, keepdims=False)
    got_a = lax.ppermute(give_a, "a", SWAP)
    first_a = a == 0
    return jnp.concatenate(
        [jnp.where(first_a, keep_a, got_a), jnp.where(first_a, got_a, keep_a)], axis=0
    )


def unspread(rows, a, c):
    r, n = rows.shape[0] // 4, rows.shape[1]
    low, high = rows[: 2 * r], rows[2 * r :]
    first_a = a == 0
    keep_a = jnp.where(first_a, low, high)
    give_a = jnp.where(first_a, high, low)
    got_a = lax.ppermute(give_a, "a", SWAP)
    quarters = jnp.stack([jnp.where(first_a, keep_a, got_a), jnp.where(first_a, got_a, keep_a)])
    quarters = quarters.reshape(2, 2, r, n)
    keep = lax.dynamic_index_in_dim(quarters, c, 1, keepdims=False)
    give = lax.dynamic_index_in_dim(quarters, 1 - c, 1, keepdims=False)
    got = lax.ppermute(give, "c", SWAP)
    first = c == 0
    return jnp.stack([jnp.where(first, keep, got), jnp.where(first, got, keep)], axis=1).reshape(
        4, r, n
    )


def scatter_along(grads, axis, place):
    total = lax.dynamic_index_in_dim(grads, place, 1, keepdims=False).astype(F32)
    for k in (2, 1, 3):
        piece = lax.dynamic_index_in_dim(grads, (place + k) % 4, 1, keepdims=False)
        got = lax.ppermute(piece, axis, [(i, (i + k) % 4) for i in range(4)])
        total = total + got.astype(F32)
    return total


def scatter_zy(grads, first):
    rows, n = grads.shape
    i = rows // 16
    z, y = lax.axis_index("z"), lax.axis_index("y")
    if first == "z":
        part = scatter_along(grads.reshape(1, 4, 4 * i, n), "z", z).astype(BF)
        part = scatter_along(part.reshape(1, 4, i, n), "y", y)
    else:
        part = scatter_along(grads.reshape(4, 4, i, n), "y", y).astype(BF)
        part = scatter_along(part.reshape(1, 4, i, n), "z", z)
    return part.reshape(i, n).astype(BF)


def quarters_of(weight):
    rows, columns = weight.shape
    return weight.reshape(rows, 4, columns // 4).transpose(1, 0, 2)


def whole_columns(quarters):
    _, rows, columns = quarters.shape
    return quarters.transpose(1, 0, 2).reshape(rows, 4 * columns)


def to_place(rows):
    n, d = rows.shape
    return rows.reshape(n, 2, 16, d // 32).transpose(0, 2, 1, 3).reshape(n, d)


def from_place(rows):
    n, d = rows.shape
    return rows.reshape(n, 16, 2, d // 32).transpose(0, 2, 1, 3).reshape(n, d)


def norm_back(rescaled, factor, gain, upstream):
    inner = upstream * gain
    return factor * (inner - rescaled * jnp.mean(inner * rescaled, axis=-1, keepdims=True))


def step_block(s):
    return (s + 2) % 4


def row_block(width):
    return lambda rows: pl.BlockSpec((rows, width), lambda s: (step_block(s), 0))


def fixed(shape):
    return pl.BlockSpec(shape, lambda *_: (0,) * len(shape))


def halves(rows, width):
    return [
        pl.BlockSpec((rows, width), lambda s: (jnp.maximum(s - 2, 0), 0)),
        pl.BlockSpec((rows, width), lambda s: (jnp.minimum(s, 1), 0)),
    ]


def load_block(s, pieces, scratch):
    part = pieces[0].shape[0]
    for b in range(4):

        @pl.when(step_block(s) == b)
        def _():
            scratch[:part] = pieces[2 * b][...]
            scratch[part:] = pieces[2 * b + 1][...]


def store_half(s, mine_ref, other_ref, value):
    @pl.when(s < 2)
    def _():
        other_ref[...] = value

    @pl.when(s >= 2)
    def _():
        mine_ref[...] = value


def pick_rows(columns):
    one = (
        lax.broadcasted_iota(jnp.int32, (8, columns.shape[1]), 0)
        == lax.broadcasted_iota(jnp.int32, (8, columns.shape[1]), 1)
    ).astype(BF)
    return mm_nt(one, columns)


def turn(values, cosines, sines, head):
    width = values.shape[1]
    lane = lax.broadcasted_iota(jnp.int32, values.shape, 1)
    low = lane % head < head // 2
    partner = jnp.where(
        low, pltpu.roll(values, width - head // 2, 1), pltpu.roll(values, head // 2, 1)
    )
    return values * cosines + partner * sines


def double(values, times):
    return jnp.concatenate([values] * times, axis=1)


def by_head(values, head):
    lane = lax.broadcasted_iota(jnp.int32, values.shape, 1) // head
    zero = jnp.zeros_like(values)
    return jnp.concatenate([jnp.where(lane == h, values, zero) for h in range(GROUP)], axis=0)


def take_heads(values, rows, head):
    lane = lax.broadcasted_iota(jnp.int32, (rows, values.shape[1]), 1) // head
    out = values[:rows]
    for h in range(1, GROUP):
        out = jnp.where(lane == h, values[h * rows : (h + 1) * rows], out)
    return out


def fold_heads(values, head):
    pair = values[:, : 2 * head] + values[:, 2 * head :]
    return pair + pltpu.roll(pair, head, 1)


def attn_forward_kernel(head, *refs):
    pieces = refs[:8]
    (w_ref, cos_ref, sin_ref, mask_ref,
     mine_ref, other_ref, normed_ref, factor_ref, q_ref, k_ref, v_ref, probs_ref, mixed_ref,
     gains_ref, x_ref, gain_scr) = refs[8:]
    s = pl.program_id(0)
    nq, cut = GROUP * head, (GROUP + 2) * head
    rows = x_ref.shape[0]

    @pl.when(s == 0)
    def _():
        gain_scr[...] = pick_rows(w_ref[:, cut + nq :])
        gains_ref[...] = gain_scr[...]

    load_block(s, pieces, x_ref)
    x = x_ref[...].astype(F32)
    factor = lax.rsqrt(jnp.mean(x * x, axis=-1, keepdims=True) + EPSILON)
    factor_ref[...] = jnp.broadcast_to(factor, factor_ref.shape)
    normed = (x * factor * gain_scr[0:1, :]).astype(BF)
    normed_ref[...] = normed
    qkv = mm(normed, w_ref[:, :cut])
    cosines, sines = cos_ref[...], sin_ref[...]
    query = turn(qkv[:, :nq], double(cosines, 2), double(sines, 2), head).astype(BF)
    kv = qkv[:, nq:]
    turned = turn(kv, cosines, sines, head)
    low = lax.broadcasted_iota(jnp.int32, kv.shape, 1) < head
    key = double(jnp.where(low, turned, pltpu.roll(turned, head, 1)), 2).astype(BF)
    value = double(jnp.where(low, pltpu.roll(kv, head, 1), kv), 2).astype(BF)
    q_ref[...] = query
    k_ref[...] = key
    v_ref[...] = value
    scores = mm_nt(by_head(query, head), key) * (1.0 / math.sqrt(head))
    allowed = mask_ref[...] == 0
    scores = jnp.where(jnp.concatenate([allowed] * GROUP, axis=0), scores, MASKED)
    weights = jnp.exp(scores - jnp.max(scores, axis=-1, keepdims=True))
    probs = weights / jnp.sum(weights, axis=-1, keepdims=True)
    probs_ref[...] = probs
    mixed = take_heads(mm(probs.astype(BF), value), rows, head).astype(BF)
    mixed_ref[...] = mixed
    store_half(s, mine_ref, other_ref, mm_nt(mixed, w_ref[:, cut : cut + nq]).astype(BF))


def attn_forward(pieces, w, cosines, sines, mask, head):
    part, d = pieces[0].shape
    rows = 2 * part
    nq = GROUP * head
    spec = lambda width: row_block(width)(rows)
    return pl.pallas_call(
        lambda *refs: attn_forward_kernel(head, *refs),
        grid=(4,),
        in_specs=[fixed(p.shape) for p in pieces]
        + [fixed(w.shape), spec(2 * head), spec(2 * head), spec(rows)],
        out_specs=halves(rows, d)
        + [spec(d), spec(128), spec(nq), spec(nq), spec(nq)]
        + [pl.BlockSpec((GROUP * rows, rows), lambda s: (step_block(s), 0)), spec(nq), fixed((8, d))],
        out_shape=[jax.ShapeDtypeStruct((2 * rows, d), BF)] * 2
        + [jax.ShapeDtypeStruct((4 * rows, d), BF), jax.ShapeDtypeStruct((4 * rows, 128), F32)]
        + [jax.ShapeDtypeStruct((4 * rows, nq), BF)] * 3
        + [
            jax.ShapeDtypeStruct((4 * GROUP * rows, rows), F32),
            jax.ShapeDtypeStruct((4 * rows, nq), BF),
            jax.ShapeDtypeStruct((8, d), F32),
        ],
        scratch_shapes=[pltpu.VMEM((rows, d), BF), pltpu.VMEM((8, d), F32)],
        compiler_params=pltpu.CompilerParams(vmem_limit_bytes=VMEM_LIMIT),
        cost_estimate=pl.CostEstimate(
            flops=8 * rows * d * (GROUP * 2 + 2) * head + 16 * rows * rows * nq * 2,
            bytes_accessed=20 * 2**20,
            transcendentals=16 * rows * rows,
        ),
    )(*pieces, w, cosines, sines, mask)


def attn_backward_kernel(head, *refs):
    d_pieces, x_pieces = refs[:8], refs[8:16]
    (w_ref, cos_ref, sin_ref, factor_ref, normed_ref, q_ref, k_ref, v_ref, probs_ref, mixed_ref,
     extra_ref,
     mine_ref, other_ref, gq_ref, gkv_ref, go_ref,
     db_ref, x_ref, acc_q, acc_kv, acc_o, gain_acc) = refs[16:]
    s = pl.program_id(0)
    nq, cut = GROUP * head, (GROUP + 2) * head
    rows = x_ref.shape[0]
    scale = 1.0 / math.sqrt(head)

    @pl.when(s == 0)
    def _():
        acc_q[...] = jnp.zeros_like(acc_q)
        acc_kv[...] = jnp.zeros_like(acc_kv)
        acc_o[...] = jnp.zeros_like(acc_o)
        gain_acc[...] = jnp.zeros_like(gain_acc)

    load_block(s, d_pieces, db_ref)
    load_block(s, x_pieces, x_ref)
    d_branch = db_ref[...]
    acc_o[...] += mm_tn(d_branch, mixed_ref[...])
    d_mixed = by_head(mm(d_branch, w_ref[:, cut : cut + nq]).astype(BF), head)
    d_probs = mm_nt(d_mixed, v_ref[...])
    probs = probs_ref[...]
    d_value = fold_heads(mm_tn(probs.astype(BF), d_mixed), head)
    d_scores = probs * (d_probs - jnp.sum(d_probs * probs, axis=-1, keepdims=True))
    d_scores = d_scores.astype(BF)
    d_query = take_heads(mm(d_scores, k_ref[...]), rows, head) * scale
    d_key = fold_heads(mm_tn(d_scores, by_head(q_ref[...], head)), head) * scale
    cosines, sines = cos_ref[...], -sin_ref[...]
    d_query = turn(d_query, double(cosines, 2), double(sines, 2), head).astype(BF)
    d_key = turn(d_key, cosines, sines, head)
    low = lax.broadcasted_iota(jnp.int32, d_key.shape, 1) < head
    d_kv = jnp.where(low, d_key, d_value).astype(BF)
    normed = normed_ref[...]
    acc_q[...] += mm_tn(normed, d_query)
    acc_kv[...] += mm_tn(normed, d_kv)
    d_normed = mm_nt(d_query, w_ref[:, :nq]) + mm_nt(d_kv, w_ref[:, nq:cut])
    store_half(s, mine_ref, other_ref, d_normed.astype(BF))
    u1 = x_ref[...].astype(F32) * factor_ref[:, :1]
    gain_acc[0:1, :] += jnp.sum(d_normed * u1, axis=0, keepdims=True)

    @pl.when(s == 3)
    def _():
        gq_ref[...] = acc_q[...].astype(BF)
        go_ref[...] = acc_o[...].astype(BF)
        gkv_ref[:, : 2 * head] = acc_kv[...].astype(BF)
        gains = gain_acc[...] + extra_ref[...]
        one = (
            lax.broadcasted_iota(jnp.int32, (8, 128), 0)
            == lax.broadcasted_iota(jnp.int32, (8, 128), 1)
        ).astype(BF)
        gkv_ref[:, 2 * head :] = mm_tn(gains.astype(BF), one).astype(BF)


def attn_backward(d_pieces, x_pieces, w, cosines, sines, saved, extra, head):
    factor, normed, query, key, value, probs, mixed = saved
    part, d = d_pieces[0].shape
    rows = 2 * part
    nq = GROUP * head
    spec = lambda width: row_block(width)(rows)
    return pl.pallas_call(
        lambda *refs: attn_backward_kernel(head, *refs),
        grid=(4,),
        in_specs=[fixed(p.shape) for p in (*d_pieces, *x_pieces)]
        + [fixed(w.shape), spec(2 * head), spec(2 * head), spec(128), spec(d)]
        + [spec(nq), spec(nq), spec(nq)]
        + [pl.BlockSpec((GROUP * rows, rows), lambda s: (step_block(s), 0)), spec(nq), fixed((8, d))],
        out_specs=halves(rows, d) + [fixed((d, nq)), fixed((d, 2 * head + 128)), fixed((d, nq))],
        out_shape=[jax.ShapeDtypeStruct((2 * rows, d), BF)] * 2
        + [
            jax.ShapeDtypeStruct((d, nq), BF),
            jax.ShapeDtypeStruct((d, 2 * head + 128), BF),
            jax.ShapeDtypeStruct((d, nq), BF),
        ],
        scratch_shapes=[
            pltpu.VMEM((rows, d), BF),
            pltpu.VMEM((rows, d), BF),
            pltpu.VMEM((d, nq), F32),
            pltpu.VMEM((d, 2 * head), F32),
            pltpu.VMEM((d, nq), F32),
            pltpu.VMEM((8, d), F32),
        ],
        compiler_params=pltpu.CompilerParams(vmem_limit_bytes=VMEM_LIMIT),
        cost_estimate=pl.CostEstimate(
            flops=16 * rows * d * (GROUP * 2 + 2) * head + 16 * rows * rows * nq * 6,
            bytes_accessed=30 * 2**20,
            transcendentals=0,
        ),
    )(*d_pieces, *x_pieces, w, cosines, sines, factor, normed, query, key, value, probs, mixed, extra)


def mlp_kernel(tile, *refs):
    n_pieces, c_pieces = refs[:8], refs[8:16]
    w_ref, h_ref, mine_ref, other_ref, n_ref, c_ref, acc = refs[16:]
    j = pl.program_id(0)
    part = n_pieces[0].shape[0]

    @pl.when(j == 0)
    def _():
        for i in range(8):
            n_ref[i * part : (i + 1) * part] = n_pieces[i][...]
            c_ref[i * part : (i + 1) * part] = c_pieces[i][...]

    chunk = 4 * part
    for m in range(2):
        rows = slice(m * chunk, (m + 1) * chunk)
        gate_up = mm(n_ref[rows], w_ref[:, : 2 * tile])
        d_hidden = mm(c_ref[rows], w_ref[:, 2 * tile :])
        gate, up = gate_up[:, :tile], gate_up[:, tile:]
        sig = jax.nn.sigmoid(gate)
        silu = gate * sig
        h_ref[rows, 2 * tile :] = (silu * up).astype(BF)
        h_ref[rows, :tile] = (d_hidden * up * sig * (1.0 + gate * (1.0 - sig))).astype(BF)
        h_ref[rows, tile : 2 * tile] = (d_hidden * silu).astype(BF)
        update = mm_nt(h_ref[rows, : 2 * tile], w_ref[:, : 2 * tile])

        @pl.when(j == 0)
        def _():
            acc[rows] = update

        @pl.when((j > 0) & (j < 3))
        def _():
            acc[rows] += update

        @pl.when(j == 3)
        def _():
            (mine_ref, other_ref)[m][...] = (acc[rows] + update).astype(BF)


def mlp(n_pieces, c_pieces, w):
    part, d = n_pieces[0].shape
    rows, columns = 8 * part, w.shape[1]
    tile = columns // 12
    once = lambda shape: pl.BlockSpec(shape, lambda j: (0, 0))
    return pl.pallas_call(
        lambda *refs: mlp_kernel(tile, *refs),
        grid=(4,),
        in_specs=[once((part, d))] * 16 + [pl.BlockSpec((d, 3 * tile), lambda j: (0, j))],
        out_specs=[pl.BlockSpec((rows, 3 * tile), lambda j: (0, j))]
        + [once((rows // 2, d))] * 2
        + [once((rows, d))] * 2,
        out_shape=[jax.ShapeDtypeStruct((rows, columns), BF)]
        + [jax.ShapeDtypeStruct((rows // 2, d), BF)] * 2
        + [jax.ShapeDtypeStruct((rows, d), BF)] * 2,
        scratch_shapes=[pltpu.VMEM((rows, d), F32)],
        compiler_params=pltpu.CompilerParams(vmem_limit_bytes=VMEM_LIMIT),
        cost_estimate=pl.CostEstimate(
            flops=2 * rows * d * columns * 5 // 3, bytes_accessed=40 * 2**20, transcendentals=0
        ),
    )(*n_pieces, *c_pieces, w)


def mlp_grads_kernel(tile, n_ref, c_ref, h_ref, w_ref, g_ref, mine_ref, other_ref, nt, ct, acc):
    j = pl.program_id(0)

    @pl.when(j == 0)
    def _():
        nt[...] = n_ref[...].T
        ct[...] = c_ref[...].T

    g_ref[:, : 2 * tile] = mm(nt[...], h_ref[:, : 2 * tile]).astype(BF)
    g_ref[:, 2 * tile :] = mm(ct[...], h_ref[:, 2 * tile :]).astype(BF)
    half = acc.shape[0] // 2
    for m in range(2):
        rows = slice(m * half, (m + 1) * half)
        update = mm_nt(h_ref[rows, 2 * tile :], w_ref[...])

        @pl.when(j == 0)
        def _():
            acc[rows] = update

        @pl.when((j > 0) & (j < 3))
        def _():
            acc[rows] += update

        @pl.when(j == 3)
        def _():
            (mine_ref, other_ref)[m][...] = (acc[rows] + update).astype(BF)


def mlp_grads(n_all, c_all, h_all, w):
    rows, d = n_all.shape
    columns = h_all.shape[1]
    tile = columns // 12
    once = lambda shape: pl.BlockSpec(shape, lambda j: (0, 0))
    return pl.pallas_call(
        lambda *refs: mlp_grads_kernel(tile, *refs),
        grid=(4,),
        in_specs=[once((rows, d))] * 2
        + [
            pl.BlockSpec((rows, 3 * tile), lambda j: (0, j)),
            pl.BlockSpec((d, tile), lambda j: (0, 3 * j + 2)),
        ],
        out_specs=[pl.BlockSpec((d, 3 * tile), lambda j: (0, j))] + [once((rows // 2, d))] * 2,
        out_shape=[jax.ShapeDtypeStruct((d, columns), BF)]
        + [jax.ShapeDtypeStruct((rows // 2, d), BF)] * 2,
        scratch_shapes=[
            pltpu.VMEM((d, rows), BF),
            pltpu.VMEM((d, rows), BF),
            pltpu.VMEM((rows, d), F32),
        ],
        compiler_params=pltpu.CompilerParams(vmem_limit_bytes=VMEM_LIMIT),
        cost_estimate=pl.CostEstimate(
            flops=2 * rows * d * columns * 4 // 3, bytes_accessed=40 * 2**20, transcendentals=0
        ),
    )(n_all, c_all, h_all, w)


def local(
    tokens, segment_ids, attn_gain, w_query, w_key, w_value, w_out,
    mlp_gain, w_gate, w_up, w_down, cotangent,
):
    a, c, t = lax.axis_index("a"), lax.axis_index("c"), lax.axis_index("t")
    own, d_model = tokens.shape
    block = segment_ids.shape[0]
    r = w_query.shape[0]
    nq = w_query.shape[1] // 4
    nk = w_key.shape[1] // 4
    ff = w_gate.shape[1] // 4
    head = nk
    tile = ff // 4
    cut = nq + 2 * nk

    gains = jnp.stack([attn_gain, mlp_gain], axis=1)
    gains = jnp.pad(gains, ((0, 0), (0, GAIN_COLS - 2)))
    attn_pack = jnp.concatenate(
        [
            quarters_of(w_query),
            quarters_of(w_key),
            quarters_of(w_value),
            quarters_of(w_out.T),
            jnp.broadcast_to(gains, (4, r, GAIN_COLS)),
        ],
        axis=2,
    )
    attn_w = lax.all_gather(spread(attn_pack, a, c), ("z", "y"), axis=0, tiled=True)
    mlp_pack = jnp.stack(
        [w.reshape(r, 4, 4, tile).transpose(1, 0, 2, 3) for w in (w_gate, w_up, w_down.T)], axis=3
    ).reshape(4, r, 3 * ff)
    mlp_w = lax.all_gather(spread(mlp_pack, a, c), ("z", "y"), axis=0, tiled=True)

    x_own = to_place(tokens)
    x_pieces = gather_rows(x_own)

    seg_pair = jnp.stack([segment_ids, lax.ppermute(segment_ids, "a", SWAP)])
    seg = jnp.concatenate([seg_pair, lax.ppermute(seg_pair, "c", SWAP)], axis=0)
    shift = jnp.stack([t, t ^ a, t, t ^ a])[:, None]
    seg = jnp.where(shift == 0, seg, jnp.roll(seg, own, axis=1))
    order = (jnp.arange(block, dtype=jnp.int32)[None, :] + shift * own) % block
    earlier = jnp.sum((seg[:, None, :] < seg[:, :, None]).astype(jnp.int32), axis=2)
    positions = (order - earlier).reshape(4 * block, 1)
    allowed = (seg[:, :, None] == seg[:, None, :]) & (order[:, None, :] <= order[:, :, None])
    mask = jnp.where(allowed, 0.0, MASKED).astype(F32).reshape(4 * block, block)
    lane = jnp.arange(2 * head)
    frequency = jnp.exp(
        -math.log(ROPE_BASE) * ((lane % (head // 2)).astype(F32) / (head // 2))
    )
    angles = positions.astype(F32) * frequency
    cosines = jnp.cos(angles)
    sines = jnp.where(lane % head < head // 2, -1.0, 1.0) * jnp.sin(angles)

    forward = attn_forward(x_pieces, attn_w, cosines, sines, mask, head)
    mine, other, normed, factor1, query, key, value, probs, mixed, gain_rows = forward
    gain_a, gain_m = gain_rows[0], gain_rows[1]
    resid = x_own.astype(F32) + scatter_rows(mine, other)

    factor2 = lax.rsqrt(jnp.mean(resid * resid, axis=-1, keepdims=True) + EPSILON)
    u2 = resid * factor2
    n_pieces = gather_rows((u2 * gain_m).astype(BF))
    c_own = to_place(cotangent)
    c_pieces = gather_rows(c_own)
    h_all, mine, other, n_all, c_all = mlp(n_pieces, c_pieces, mlp_w)
    d_n2 = scatter_rows(mine, other)
    mlp_grad, mine, other = mlp_grads(n_all, c_all, h_all, mlp_w)
    mlp_grad = lax.psum_scatter(mlp_grad, ("z", "y"), scatter_dimension=0, tiled=True)
    layer_output = from_place((resid + scatter_rows(mine, other)).astype(BF))

    mlp_gain_part = jnp.sum(d_n2 * u2, axis=0)
    d_resid = c_own.astype(F32) + norm_back(u2, factor2, gain_m, d_n2)
    d_pieces = gather_rows(d_resid.astype(BF))
    extra = jnp.pad(mlp_gain_part[None], ((1, 6), (0, 0)))
    saved = (factor1, normed, query, key, value, probs, mixed)
    mine, other, grad_q, grad_kv, grad_o = attn_backward(
        d_pieces, x_pieces, attn_w, cosines, sines, saved, extra, head
    )
    h = jnp.concatenate(
        [scatter_zy(grad_q, "z"), scatter_zy(grad_kv, "y"), scatter_zy(grad_o, "z")], axis=1
    )
    d_n1 = scatter_rows(mine, other)
    u1 = x_own.astype(F32) * factor1[:own, :1]
    input_grad = from_place(d_resid + norm_back(u1, factor1[:own, :1], gain_a, d_n1))

    g = unspread(mlp_grad, a, c).astype(F32).reshape(4, r, 4, 3, tile)
    gate_grad, up_grad, down_grad = (
        whole_columns(g[:, :, :, i].reshape(4, r, ff)) for i in range(3)
    )
    h = unspread(h, a, c).astype(F32)
    query_grad = whole_columns(h[:, :, :nq])
    key_grad = whole_columns(h[:, :, nq : nq + nk])
    value_grad = whole_columns(h[:, :, nq + nk : cut])
    out_grad = whole_columns(h[:, :, cut + GAIN_COLS :]).T
    gain_grads = jnp.sum(h[:, :, cut : cut + 2], axis=0).T
    gain_grads = gain_grads + lax.ppermute(gain_grads, "t", SWAP)
    return (
        layer_output, input_grad, gain_grads[0], query_grad, key_grad, value_grad, out_grad,
        gain_grads[1], gate_grad, up_grad, down_grad.T,
    )


def solution(mesh):
    fine = Mesh(mesh.devices.reshape(2, 4, 4, 2, 2), ("a", "z", "y", "c", "t"))
    dp = ("a", "z", "y", "c")
    rows = P(dp + ("t",), None)
    return jax.shard_map(
        local,
        mesh=fine,
        in_specs=(
            rows, P(dp), P(dp), P(dp, "t"), P(dp, "t"), P(dp, "t"), P("t", dp),
            P(dp), P(dp, "t"), P(dp, "t"), P("t", dp), rows,
        ),
        out_specs=(
            rows, rows, P(dp), P(dp, "t"), P(dp, "t"), P(dp, "t"), P("t", dp),
            P(dp), P(dp, "t"), P(dp, "t"), P("t", dp),
        ),
        check_vma=False,
    )
```

time: 723 us -> 467 us (0.65)
  waiting for transfers between devices: 433 us -> 186 us
  Pallas kernels: 0 us -> 112 us
  matrix products: 111 us -> 0 us
  starting transfers between devices: 50.7 us -> 78.1 us
  local copies, waits for them, and re-layouts: 63.9 us -> 36.7 us
  other arithmetic: 41.4 us -> 31 us
    reduce_scatter x4 -> x1, waiting for transfers between devices: 231 us -> 0.01 us  [local(): lax.psum_scatter(mlp_grad, ('z', 'y'), scatter_dimension=0, tiled=True)]
    pallas_call x0 -> x4, Pallas kernels: none -> 112 us  [the longest x1 40 us: mlp(): pl.pallas_call(lambda *refs: mlp_kernel(tile, *refs), grid=(4,), in_specs...]
    dot_general x23 -> x0, matrix products: 106 us -> none  [the longest x6 40.6 us: mm(): return jnp.dot(left, right, preferred_element_type=F32)]
    all_gather x4 -> x2, waiting for transfers between devices: 41 us -> 4.37 us  [the longest x1 2.47 us: local(): lax.all_gather(spread(mlp_pack, a, c), ('z', 'y'), axis=0, tiled=True)]
    ppermute x8 -> x38, starting transfers between devices: 1.27 us -> 31 us  [the longest x18 27.2 us: scatter_along(): got = lax.ppermute(piece, axis, [(i, (i + k) % 4) for i in range(4)])]
    ppermute x12, waiting for transfers between devices: 43.5 us -> 63.9 us  [to_chip(): lax.ppermute(value, ('a', 't'), [(AT[i], AT[(i + k) % 4]) for i in range(...]
    reshape x7 -> x5, local copies, waits for them, and re-layouts: 14.1 us -> 0.96 us  [the longest x3 0.54 us: local(): w.reshape(r, 4, 4, tile).transpose(1, 0, 2, 3)]
    unnamed x115 -> x100, local copies, waits for them, and re-layouts: 16.5 us -> 5.65 us
  transfers between devices with their start and end apart: 51 -> 76, of which waited for: 32 -> 37; matrix products, arithmetic and copies ran while one was open for 18% -> 10% of each run, Pallas kernels for 0% -> 8%
where the time goes in v2:
time: 467 us; the launch traced here: 459 us
  waiting for transfers between devices  186 us (40%)
  Pallas kernels  112 us (24%)
  starting transfers between devices  78.1 us (17%)
  local copies, waits for them, and re-layouts  36.7 us (8%)
  other arithmetic  31 us (7%)
  between operations  15 us (3%)
    ppermute x12, waiting for transfers between devices, to_chip(): lax.ppermute(value, ('a', 't'), [(AT[i], AT[(i + k) % 4]) for i in range(...  63.9 us
    ppermute x12, waiting for transfers between devices, from_chip(): lax.ppermute(value, ('a', 't'), [(AT[(i + k) % 4], AT[i]) for i in range(...  54.9 us
    pallas_call x1, Pallas kernels, mlp(): pl.pallas_call(lambda *refs: mlp_kernel(tile, *refs), grid=(4,), in_specs...  40 us
    pallas_call x1, Pallas kernels, mlp_grads(): pl.pallas_call(lambda *refs: mlp_grads_kernel(tile, *refs), grid=(4,), in...  33.8 us
    ppermute x18, starting transfers between devices, scatter_along(): got = lax.ppermute(piece, axis, [(i, (i + k) % 4) for i in range(4)])  27.2 us
    pallas_call x1, Pallas kernels, attn_backward(): pl.pallas_call(lambda *refs: attn_backward_kernel(head, *refs), grid=(4,)...  22.7 us
    ppermute x12, starting transfers between devices, from_chip(): lax.ppermute(value, ('a', 't'), [(AT[(i + k) % 4], AT[i]) for i in range(...  21.8 us
    ppermute x1, waiting for transfers between devices, local(): seg_pair = jnp.stack([segment_ids, lax.ppermute(segment_ids, 'a', SWAP)])  17.4 us
  transfers between devices with their start and end apart: 76, of which 37 were waited for; matrix products, arithmetic and copies ran while one was open for 10% of the time, Pallas kernels for 8%

profile of v2, /device:TPU:0, one launch (start us, length us, event | category | flops | bytes accessed | tf_op | source)
XLA Modules:
  0.0 458.8 jit_solution(5619850331246081171)
XLA Ops:
  15.0 3.3 collective-permute-done.8
  25.2 9.6 %collective-permute-done.30 = bf16[64,3072]{1,0:T(8,128)(2,1)S(1)} collective-permute-done((bf16[64,3072]{1,0:T(8,128)(2,1)S(1)}, bf16[64,3072]{1,0:T(8,128)(2,1)S(1)}, u32[]{:S(2)}, u32[]{:S(2)}) %collective-permute-start.30) | collective-permute-done | bytes 393248 | tf_op jit(solution)/shard_map/ppermute | solution.py:76
  36.6 3.2 collective-permute-start
  42.5 17.4 %collective-permute-done.9 = s32[224]{0:T(256)S(1)} collective-permute-done((s32[224]{0:T(256)S(1)}, s32[224]{0:T(256)S(1)}, u32[]{:S(2)}, u32[]{:S(2)}) %collective-permute-start.9) | collective-permute-done | bytes 928 | tf_op jit(solution)/shard_map/ppermute | solution.py:547
  64.4 2.6 fusion.17
  69.8 15.7 %shard_map.203 = (bf16[448,2048]{1,0:T(8,128)(2,1)}, bf16[448,2048]{1,0:T(8,128)(2,1)}, bf16[896,2048]{1,0:T(8,128)(2,1)}, f32[896,128]{1,0:T(8,128)}, bf16[896,...) custom-call(bf16[112,2048]{1,0:T(8,128)(2,1)} %copy-done, ...), custom_call_target="tpu_custom_call" | custom-call | flops 2759852032 | bytes 20971520 | tf_op jit(solution)/shard_map/pallas_call | solution.py:275
  86.2 3.0 collective-permute-start.22
  94.3 2.3 collective-permute-start.12
  97.6 3.5 collective-permute-done.22.refs_9_
  102.6 8.4 %collective-permute-done.23.refs_10_ = bf16[112,2048]{1,0:T(8,128)(2,1)S(1)} collective-permute-done((bf16[112,2048]{1,0:T(8,128)(2,1)S(1)}, bf16[112,2048]{1,0:T(8,128)(2,1)S(1)}, u32[]{:S(2)}, u32[]{:S(2)}) %collective-permute-start.23) | collective-permute-done | bytes 458784 | tf_op jit(solution)/shard_map/ppermute | solution.py:41
  111.0 9.8 %collective-permute-done.14 = bf16[112,2048]{1,0:T(8,128)(2,1)S(1)} collective-permute-done((bf16[112,2048]{1,0:T(8,128)(2,1)S(1)}, bf16[112,2048]{1,0:T(8,128)(2,1)S(1)}, u32[]{:S(2)}, u32[]{:S(2)}) %collective-permute-start.14) | collective-permute-done | bytes 458784 | tf_op jit(solution)/shard_map/ppermute | solution.py:45
  123.0 2.6 collective-permute-start.15
  125.6 4.9 %collective-permute-done.24.refs_11_ = bf16[112,2048]{1,0:T(8,128)(2,1)S(1)} collective-permute-done((bf16[112,2048]{1,0:T(8,128)(2,1)S(1)}, bf16[112,2048]{1,0:T(8,128)(2,1)S(1)}, u32[]{:S(2)}, u32[]{:S(2)}) %collective-permute-start.24) | collective-permute-done | bytes 458784 | tf_op jit(solution)/shard_map/ppermute | solution.py:41
  130.5 5.7 %collective-permute-start.16 = (bf16[112,2048]{1,0:T(8,128)(2,1)S(1)}, bf16[112,2048]{1,0:T(8,128)(2,1)S(1)}, u32[]{:S(2)}, u32[]{:S(2)}) collective-permute-start(bf16[112,2048]{1,0:T(8,128)(2,1)S(1)} %multiply_convert_fusion.refs_0_), channel_id=1, source_target_pairs={{64,0},{1,64},{65,1},{0,65},{66,2},{3,66},{67,3},{2,67},{68,4},{5,... | collective-permute-start | bytes 1376264 | tf_op jit(solution)/shard_map/ppermute | solution.py:41
  136.8 3.7 collective-permute-done.15.refs_1_
  140.5 15.0 %collective-permute-done.16.refs_2_ = bf16[112,2048]{1,0:T(8,128)(2,1)S(1)} collective-permute-done((bf16[112,2048]{1,0:T(8,128)(2,1)S(1)}, bf16[112,2048]{1,0:T(8,128)(2,1)S(1)}, u32[]{:S(2)}, u32[]{:S(2)}) %collective-permute-start.16) | collective-permute-done | bytes 458784 | tf_op jit(solution)/shard_map/ppermute | solution.py:41
  158.4 2.5 all-gather.5.cloned.1.call-done.refs_16_.refs_3_
  160.9 40.0 %shard_map.204 = (bf16[896,3072]{1,0:T(8,128)(2,1)}, bf16[448,2048]{1,0:T(8,128)(2,1)}, bf16[448,2048]{1,0:T(8,128)(2,1)}, bf16[896,2048]{1,0:T(8,128)(2,1)}, bf16[896,2048]{1,0:T(8,128)(2,1)}) custom-call(bf16[112,2048]{1,0:T(8,128)(2,1)} %copy-done.18, bf16[112,2048]{1,0:T(8,128)(2,1)} %copy-done.40, bf16[112,2048]{1,0:T(8,128)(2,1)} %copy-done.41, ...), custom_call_target="tpu_custom_call" | custom-call | flops 18790481920 | bytes 41943040 | tf_op jit(solution)/shard_map/pallas_call | solution.py:437
  200.9 33.8 %shard_map.205 = (bf16[2048,3072]{1,0:T(8,128)(2,1)}, bf16[448,2048]{1,0:T(8,128)(2,1)}, bf16[448,2048]{1,0:T(8,128)(2,1)}) custom-call(bf16[896,2048]{1,0:T(8,128)(2,1)} %get-tuple-element.37.refs_0_, bf16[896,2048]{1,0:T(8,128)(2,1)} %get-tuple-element.38.refs_1_, bf16[896,3072]{1,0:T(8,128)(2,1)} %get-tuple-element.39.refs_2_, ...), custom_call_target="tpu_custom_call" | custom-call | flops 15032385536 | bytes 41943040 | tf_op jit(solution)/shard_map/pallas_call | solution.py:488
  235.3 3.5 collective-permute-done.35
  239.2 2.8 collective-permute-start.38
  242.0 2.3 collective-permute-start.36
  247.2 15.4 %collective-permute-done.38 = bf16[112,2048]{1,0:T(8,128)(2,1)S(1)} collective-permute-done((bf16[112,2048]{1,0:T(8,128)(2,1)S(1)}, bf16[112,2048]{1,0:T(8,128)(2,1)S(1)}, u32[]{:S(2)}, u32[]{:S(2)}) %collective-permute-start.38) | collective-permute-done | bytes 458784 | tf_op jit(solution)/shard_map/ppermute | solution.py:45
  262.6 3.9 collective-permute-done.37
  268.1 13.5 %collective-permute-done.34 = bf16[112,2048]{1,0:T(8,128)(2,1)S(1)} collective-permute-done((bf16[112,2048]{1,0:T(8,128)(2,1)S(1)}, bf16[112,2048]{1,0:T(8,128)(2,1)S(1)}, u32[]{:S(2)}, u32[]{:S(2)}) %collective-permute-start.34) | collective-permute-done | bytes 458784 | tf_op jit(solution)/shard_map/ppermute | solution.py:45
  281.6 3.4 collective-permute-done.33
  288.4 12.5 %collective-permute-done.39.refs_1_ = bf16[112,2048]{1,0:T(8,128)(2,1)} collective-permute-done((bf16[112,2048]{1,0:T(8,128)(2,1)S(1)}, bf16[112,2048]{1,0:T(8,128)(2,1)}, u32[]{:S(2)}, u32[]{:S(2)}) %collective-permute-start.39) | collective-permute-done | bytes 458784 | tf_op jit(solution)/shard_map/ppermute | solution.py:41
  300.9 5.8 %collective-permute-done.40.refs_2_ = bf16[112,2048]{1,0:T(8,128)(2,1)} collective-permute-done((bf16[112,2048]{1,0:T(8,128)(2,1)S(1)}, bf16[112,2048]{1,0:T(8,128)(2,1)}, u32[]{:S(2)}, u32[]{:S(2)}) %collective-permute-start.40) | collective-permute-done | bytes 458784 | tf_op jit(solution)/shard_map/ppermute | solution.py:41
  310.0 22.7 %shard_map.206 = (bf16[448,2048]{1,0:T(8,128)(2,1)}, bf16[448,2048]{1,0:T(8,128)(2,1)}, bf16[2048,256]{1,0:T(8,128)(2,1)}, bf16[2048,256]{1,0:T(8,128)(2,1)}, bf16[2048,256]{1,0:T(8,128)(2,1)}) custom-call(bf16[112,2048]{1,0:T(8,128)(2,1)} %copy-done.15, bf16[112,2048]{1,0:T(8,128)(2,1)} %collective-permute-done.39.refs_1_, ...), custom_call_target="tpu_custom_call" | custom-call | flops 5930745856 | bytes 31457280 | tf_op jit(solution)/shard_map/pallas_call | solution.py:363
  334.0 2.9 collective-permute-start.64
  336.9 2.2 collective-permute-start.62
  342.4 5.9 %collective-permute-done.64 = bf16[1,512,256]{2,1,0:T(8,128)(2,1)S(1)} collective-permute-done((bf16[1,512,256]{2,1,0:T(8,128)(2,1)S(1)}, bf16[1,512,256]{2,1,0:T(8,128)(2,1)S(1)}, u32[]{:S(2)}, u32[]{:S(2)}) %collective-permute-start.64) | collective-permute-done | bytes 262176 | tf_op jit(solution)/shard_map/ppermute | solution.py:105
  348.4 3.4 collective-permute-done.63
  355.1 3.3 collective-permute-start.67
  359.6 7.1 %collective-permute-start.65 = (bf16[1,128,256]{2,1,0:T(8,128)(2,1)S(1)}, bf16[1,128,256]{2,1,0:T(8,128)(2,1)S(1)}, u32[]{:S(2)}, u32[]{:S(2)}) collective-permute-start(bf16[1,128,256]{2,1,0:T(8,128)(2,1)S(1)} %get-tuple-element.173), channel_id=1, source_target_pairs={{0,8},{4,12},{8,0},{12,4},{1,9},{5,13},{9,1},{13,5},{2,10},{6,14},... | collective-permute-start | bytes 196616 | tf_op jit(solution)/shard_map/ppermute | solution.py:105
  366.7 3.7 collective-permute-start.61
  374.4 2.2 collective-permute-done.60
  377.8 2.4 collective-permute-done.53
  381.0 3.9 collective-permute-done.68
  395.5 3.1 add_convert_fusion.2
  398.6 2.1 collective-permute-start.49
  403.6 2.5 collective-permute-start.71
  406.1 6.1 %collective-permute-done.49 = bf16[112,2048]{1,0:T(8,128)(2,1)S(1)} collective-permute-done((bf16[112,2048]{1,0:T(8,128)(2,1)}, bf16[112,2048]{1,0:T(8,128)(2,1)S(1)}, u32[]{:S(2)}, u32[]{:S(2)}) %collective-permute-start.49) | collective-permute-done | bytes 458784 | tf_op jit(solution)/shard_map/ppermute | solution.py:45
  412.2 10.9 %collective-permute-done.48 = bf16[112,2048]{1,0:T(8,128)(2,1)} collective-permute-done((bf16[112,2048]{1,0:T(8,128)(2,1)}, bf16[112,2048]{1,0:T(8,128)(2,1)}, u32[]{:S(2)}, u32[]{:S(2)}) %collective-permute-start.48) | collective-permute-done | bytes 458784 | tf_op jit(solution)/shard_map/ppermute | solution.py:45
  426.0 3.2 collective-permute-done.71
  431.1 3.2 fusion.5
  439.5 2.8 reshape.527
  442.3 5.3 %slice_reduce_fusion = (f32[4,32,4,256]{3,2,1,0:T(4,128)S(1)}, f32[4,32,4,256]{3,2,1,0:T(4,128)}, f32[4,32,4,256]{3,2,1,0:T(4,128)}) fusion(f32[4,32,4,3,256]{4,3,2,1,0:T(4,128)S(1)} %reshape.527), kind=kLoop, calls=%fused_computation.46 | loop fusion | bytes 3145728 | tf_op jit(solution)/shard_map/slice | solution.py:597
  (324 shorter events, 94.7 us)
Async XLA Ops:
  7.2 62.6 %all-gather.3.cloned.1.call-start = ((), (), s32[]{:S(2)}) async-start(), calls=%async_computation.1 | async-start | bytes 3342336 | tf_op jit(solution)/shard_map/all_gather | solution.py:538
  19.0 141.8 %all-gather.5.cloned.1.call-start = ((), (), s32[]{:S(2)}) async-start(), calls=%async_computation.2 | async-start | bytes 13369344 | tf_op jit(solution)/shard_map/all_gather | solution.py:542
  35.9 366.5 %reduce-scatter.2.cloned.1.call-start = ((), (), s32[]{:S(2)}) async-start(), calls=%async_computation.3 | async-start | bytes 13369344 | tf_op jit(solution)/shard_map/reduce_scatter | solution.py:577
  36.6 25.5 %collective-permute-start = (bf16[112,2048]{1,0:T(8,128)(2,1)S(1)}, bf16[112,2048]{1,0:T(8,128)(2,1)S(1)}, u32[]{:S(2)}, u32[]{:S(2)}) collective-permute-start(bf16[112,2048]{1,0:T(8,128)(2,1)S(1)} %copy.178.refs_0_.refs_8_), channel_id=1, source_target_pairs={{1,0},{65,64},{0,1},{64,65},{3,2},{67,66},{2,3},{66,67},{5,4},{69,... | collective-permute-start | bytes 1376264 | tf_op jit(solution)/shard_map/ppermute | solution.py:41
  39.7 22.6 %collective-permute-start.1 = (bf16[112,2048]{1,0:T(8,128)(2,1)S(1)}, bf16[112,2048]{1,0:T(8,128)(2,1)S(1)}, u32[]{:S(2)}, u32[]{:S(2)}) collective-permute-start(bf16[112,2048]{1,0:T(8,128)(2,1)S(1)} %copy.178.refs_0_.refs_8_), channel_id=1, source_target_pairs={{64,0},{1,64},{65,1},{0,65},{66,2},{3,66},{67,3},{2,67},{68,4},{5,... | collective-permute-start | bytes 1376264 | tf_op jit(solution)/shard_map/ppermute | solution.py:41
  40.9 21.8 %collective-permute-start.2 = (bf16[112,2048]{1,0:T(8,128)(2,1)S(1)}, bf16[112,2048]{1,0:T(8,128)(2,1)S(1)}, u32[]{:S(2)}, u32[]{:S(2)}) collective-permute-start(bf16[112,2048]{1,0:T(8,128)(2,1)S(1)} %copy.178.refs_0_.refs_8_), channel_id=1, source_target_pairs={{65,0},{0,64},{64,1},{1,65},{67,2},{2,66},{66,3},{3,67},{69,4},{4,... | collective-permute-start | bytes 1376264 | tf_op jit(solution)/shard_map/ppermute | solution.py:41
  41.8 25.2 %collective-permute-start.3 = (bf16[112,2048]{1,0:T(8,128)(2,1)S(1)}, bf16[112,2048]{1,0:T(8,128)(2,1)S(1)}, u32[]{:S(2)}, u32[]{:S(2)}) collective-permute-start(bf16[112,2048]{1,0:T(8,128)(2,1)S(1)} %copy.178.refs_0_.refs_8_), channel_id=1, source_target_pairs={{0,2},{2,0},{1,3},{3,1},{4,6},{6,4},{5,7},{7,5},{8,10},{10,8},{9,1... | collective-permute-start | bytes 1376264 | tf_op jit(solution)/shard_map/ppermute | solution.py:50
  41.8 18.2 %collective-permute-start.9 = (s32[224]{0:T(256)S(1)}, s32[224]{0:T(256)S(1)}, u32[]{:S(2)}, u32[]{:S(2)}) collective-permute-start(s32[224]{0:T(256)S(1)} %copy-done.22), channel_id=1, source_target_pairs={{0,64},{64,0},{1,65},{65,1},{2,66},{66,2},{3,67},{67,3},{4,68},{68... | collective-permute-start | bytes 2696 | tf_op jit(solution)/shard_map/ppermute | solution.py:547
  86.2 14.9 %collective-permute-start.22 = (bf16[112,2048]{1,0:T(8,128)(2,1)S(1)}, bf16[112,2048]{1,0:T(8,128)(2,1)S(1)}, u32[]{:S(2)}, u32[]{:S(2)}) collective-permute-start(bf16[112,2048]{1,0:T(8,128)(2,1)S(1)} %copy.196.refs_8_), channel_id=1, source_target_pairs={{1,0},{65,64},{0,1},{64,65},{3,2},{67,66},{2,3},{66,67},{5,4},{69,... | collective-permute-start | bytes 1376264 | tf_op jit(solution)/shard_map/ppermute | solution.py:41
  89.2 21.7 %collective-permute-start.23 = (bf16[112,2048]{1,0:T(8,128)(2,1)S(1)}, bf16[112,2048]{1,0:T(8,128)(2,1)S(1)}, u32[]{:S(2)}, u32[]{:S(2)}) collective-permute-start(bf16[112,2048]{1,0:T(8,128)(2,1)S(1)} %copy.196.refs_8_), channel_id=1, source_target_pairs={{64,0},{1,64},{65,1},{0,65},{66,2},{3,66},{67,3},{2,67},{68,4},{5,... | collective-permute-start | bytes 1376264 | tf_op jit(solution)/shard_map/ppermute | solution.py:41
  92.2 28.5 %collective-permute-start.14 = (bf16[112,2048]{1,0:T(8,128)(2,1)S(1)}, bf16[112,2048]{1,0:T(8,128)(2,1)S(1)}, u32[]{:S(2)}, u32[]{:S(2)}) collective-permute-start(bf16[112,2048]{1,0:T(8,128)(2,1)S(1)} %get-tuple-element.134), channel_id=1, source_target_pairs={{0,65},{64,0},{1,64},{65,1},{2,67},{66,2},{3,66},{67,3},{4,69},{68... | collective-permute-start | bytes 1376264 | tf_op jit(solution)/shard_map/ppermute | solution.py:45
  94.3 26.5 %collective-permute-start.13 = (bf16[112,2048]{1,0:T(8,128)(2,1)S(1)}, bf16[112,2048]{1,0:T(8,128)(2,1)S(1)}, u32[]{:S(2)}, u32[]{:S(2)}) collective-permute-start(bf16[112,2048]{1,0:T(8,128)(2,1)S(1)} %get-tuple-element.135), channel_id=1, source_target_pairs={{0,64},{64,1},{1,65},{65,0},{2,66},{66,3},{3,67},{67,2},{4,68},{68... | collective-permute-start | bytes 1376264 | tf_op jit(solution)/shard_map/ppermute | solution.py:45
  94.3 27.0 %collective-permute-start.12 = (bf16[112,2048]{1,0:T(8,128)(2,1)S(1)}, bf16[112,2048]{1,0:T(8,128)(2,1)S(1)}, u32[]{:S(2)}, u32[]{:S(2)}) collective-permute-start(bf16[112,2048]{1,0:T(8,128)(2,1)S(1)} %get-tuple-element.133), channel_id=1, source_target_pairs={{0,1},{64,65},{1,0},{65,64},{2,3},{66,67},{3,2},{67,66},{4,5},{68,... | collective-permute-start | bytes 1376264 | tf_op jit(solution)/shard_map/ppermute | solution.py:45
  101.1 29.4 %collective-permute-start.24 = (bf16[112,2048]{1,0:T(8,128)(2,1)S(1)}, bf16[112,2048]{1,0:T(8,128)(2,1)S(1)}, u32[]{:S(2)}, u32[]{:S(2)}) collective-permute-start(bf16[112,2048]{1,0:T(8,128)(2,1)S(1)} %copy.196.refs_8_), channel_id=1, source_target_pairs={{65,0},{0,64},{64,1},{1,65},{67,2},{2,66},{66,3},{3,67},{69,4},{4,... | collective-permute-start | bytes 1376264 | tf_op jit(solution)/shard_map/ppermute | solution.py:41
  111.0 25.2 %collective-permute-start.25 = (bf16[112,2048]{1,0:T(8,128)(2,1)S(1)}, bf16[112,2048]{1,0:T(8,128)(2,1)S(1)}, u32[]{:S(2)}, u32[]{:S(2)}) collective-permute-start(bf16[112,2048]{1,0:T(8,128)(2,1)S(1)} %copy.196.refs_8_), channel_id=1, source_target_pairs={{0,2},{2,0},{1,3},{3,1},{4,6},{6,4},{5,7},{7,5},{8,10},{10,8},{9,1... | collective-permute-start | bytes 1376264 | tf_op jit(solution)/shard_map/ppermute | solution.py:50
  120.8 15.4 %collective-permute-start.26 = (bf16[112,2048]{1,0:T(8,128)(2,1)S(1)}, bf16[112,2048]{1,0:T(8,128)(2,1)S(1)}, u32[]{:S(2)}, u32[]{:S(2)}) collective-permute-start(bf16[112,2048]{1,0:T(8,128)(2,1)S(1)} %collective-permute-done.22.refs_9_), channel_id=1, source_target_pairs={{0,2},{2,0},{1,3},{3,1},{4,6},{6,4},{5,7},{7,5},{8,10},{10,8},{9,1... | collective-permute-start | bytes 1376264 | tf_op jit(solution)/shard_map/ppermute | solution.py:50
  120.8 15.5 %collective-permute-start.27 = (bf16[112,2048]{1,0:T(8,128)(2,1)S(1)}, bf16[112,2048]{1,0:T(8,128)(2,1)S(1)}, u32[]{:S(2)}, u32[]{:S(2)}) collective-permute-start(bf16[112,2048]{1,0:T(8,128)(2,1)S(1)} %collective-permute-done.23.refs_10_), channel_id=1, source_target_pairs={{0,2},{2,0},{1,3},{3,1},{4,6},{6,4},{5,7},{7,5},{8,10},{10,8},{9,1... | collective-permute-start | bytes 1376264 | tf_op jit(solution)/shard_map/ppermute | solution.py:50
  123.0 17.5 %collective-permute-start.15 = (bf16[112,2048]{1,0:T(8,128)(2,1)S(1)}, bf16[112,2048]{1,0:T(8,128)(2,1)S(1)}, u32[]{:S(2)}, u32[]{:S(2)}) collective-permute-start(bf16[112,2048]{1,0:T(8,128)(2,1)S(1)} %multiply_convert_fusion.refs_0_), channel_id=1, source_target_pairs={{1,0},{65,64},{0,1},{64,65},{3,2},{67,66},{2,3},{66,67},{5,4},{69,... | collective-permute-start | bytes 1376264 | tf_op jit(solution)/shard_map/ppermute | solution.py:41
  130.5 25.0 %collective-permute-start.16 = (bf16[112,2048]{1,0:T(8,128)(2,1)S(1)}, bf16[112,2048]{1,0:T(8,128)(2,1)S(1)}, u32[]{:S(2)}, u32[]{:S(2)}) collective-permute-start(bf16[112,2048]{1,0:T(8,128)(2,1)S(1)} %multiply_convert_fusion.refs_0_), channel_id=1, source_target_pairs={{64,0},{1,64},{65,1},{0,65},{66,2},{3,66},{67,3},{2,67},{68,4},{5,... | collective-permute-start | bytes 1376264 | tf_op jit(solution)/shard_map/ppermute | solution.py:41
  136.2 19.4 %collective-permute-start.17 = (bf16[112,2048]{1,0:T(8,128)(2,1)S(1)}, bf16[112,2048]{1,0:T(8,128)(2,1)S(1)}, u32[]{:S(2)}, u32[]{:S(2)}) collective-permute-start(bf16[112,2048]{1,0:T(8,128)(2,1)S(1)} %multiply_convert_fusion.refs_0_), channel_id=1, source_target_pairs={{65,0},{0,64},{64,1},{1,65},{67,2},{2,66},{66,3},{3,67},{69,4},{4,... | collective-permute-start | bytes 1376264 | tf_op jit(solution)/shard_map/ppermute | solution.py:41
  136.2 20.4 %collective-permute-start.28 = (bf16[112,2048]{1,0:T(8,128)(2,1)S(1)}, bf16[112,2048]{1,0:T(8,128)(2,1)S(1)}, u32[]{:S(2)}, u32[]{:S(2)}) collective-permute-start(bf16[112,2048]{1,0:T(8,128)(2,1)S(1)} %collective-permute-done.24.refs_11_), channel_id=1, source_target_pairs={{0,2},{2,0},{1,3},{3,1},{4,6},{6,4},{5,7},{7,5},{8,10},{10,8},{9,1... | collective-permute-start | bytes 1376264 | tf_op jit(solution)/shard_map/ppermute | solution.py:50
  136.3 20.3 %collective-permute-start.18 = (bf16[112,2048]{1,0:T(8,128)(2,1)S(1)}, bf16[112,2048]{1,0:T(8,128)(2,1)S(1)}, u32[]{:S(2)}, u32[]{:S(2)}) collective-permute-start(bf16[112,2048]{1,0:T(8,128)(2,1)S(1)} %multiply_convert_fusion.refs_0_), channel_id=1, source_target_pairs={{0,2},{2,0},{1,3},{3,1},{4,6},{6,4},{5,7},{7,5},{8,10},{10,8},{9,1... | collective-permute-start | bytes 1376264 | tf_op jit(solution)/shard_map/ppermute | solution.py:50
  140.5 16.1 %collective-permute-start.19 = (bf16[112,2048]{1,0:T(8,128)(2,1)S(1)}, bf16[112,2048]{1,0:T(8,128)(2,1)S(1)}, u32[]{:S(2)}, u32[]{:S(2)}) collective-permute-start(bf16[112,2048]{1,0:T(8,128)(2,1)S(1)} %collective-permute-done.15.refs_1_), channel_id=1, source_target_pairs={{0,2},{2,0},{1,3},{3,1},{4,6},{6,4},{5,7},{7,5},{8,10},{10,8},{9,1... | collective-permute-start | bytes 1376264 | tf_op jit(solution)/shard_map/ppermute | solution.py:50
  239.2 23.3 %collective-permute-start.38 = (bf16[112,2048]{1,0:T(8,128)(2,1)S(1)}, bf16[112,2048]{1,0:T(8,128)(2,1)S(1)}, u32[]{:S(2)}, u32[]{:S(2)}) collective-permute-start(bf16[112,2048]{1,0:T(8,128)(2,1)S(1)} %get-tuple-element.128), channel_id=1, source_target_pairs={{0,65},{64,0},{1,64},{65,1},{2,67},{66,2},{3,66},{67,3},{4,69},{68... | collective-permute-start | bytes 1376264 | tf_op jit(solution)/shard_map/ppermute | solution.py:45
  242.0 24.4 %collective-permute-start.37 = (bf16[112,2048]{1,0:T(8,128)(2,1)S(1)}, bf16[112,2048]{1,0:T(8,128)(2,1)S(1)}, u32[]{:S(2)}, u32[]{:S(2)}) collective-permute-start(bf16[112,2048]{1,0:T(8,128)(2,1)S(1)} %get-tuple-element.129), channel_id=1, source_target_pairs={{0,64},{64,1},{1,65},{65,0},{2,66},{66,3},{3,67},{67,2},{4,68},{68... | collective-permute-start | bytes 1376264 | tf_op jit(solution)/shard_map/ppermute | solution.py:45
  242.0 24.4 %collective-permute-start.36 = (bf16[112,2048]{1,0:T(8,128)(2,1)S(1)}, bf16[112,2048]{1,0:T(8,128)(2,1)S(1)}, u32[]{:S(2)}, u32[]{:S(2)}) collective-permute-start(bf16[112,2048]{1,0:T(8,128)(2,1)S(1)} %get-tuple-element.127), channel_id=1, source_target_pairs={{0,1},{64,65},{1,0},{65,64},{2,3},{66,67},{3,2},{67,66},{4,5},{68,... | collective-permute-start | bytes 1376264 | tf_op jit(solution)/shard_map/ppermute | solution.py:45
  244.9 36.7 %collective-permute-start.34 = (bf16[112,2048]{1,0:T(8,128)(2,1)S(1)}, bf16[112,2048]{1,0:T(8,128)(2,1)S(1)}, u32[]{:S(2)}, u32[]{:S(2)}) collective-permute-start(bf16[112,2048]{1,0:T(8,128)(2,1)S(1)} %get-tuple-element.131), channel_id=1, source_target_pairs={{0,65},{64,0},{1,64},{65,1},{2,67},{66,2},{3,66},{67,3},{4,69},{68... | collective-permute-start | bytes 1376264 | tf_op jit(solution)/shard_map/ppermute | solution.py:45
  246.1 38.9 %collective-permute-start.33 = (bf16[112,2048]{1,0:T(8,128)(2,1)S(1)}, bf16[112,2048]{1,0:T(8,128)(2,1)S(1)}, u32[]{:S(2)}, u32[]{:S(2)}) collective-permute-start(bf16[112,2048]{1,0:T(8,128)(2,1)S(1)} %get-tuple-element.132), channel_id=1, source_target_pairs={{0,64},{64,1},{1,65},{65,0},{2,66},{66,3},{3,67},{67,2},{4,68},{68... | collective-permute-start | bytes 1376264 | tf_op jit(solution)/shard_map/ppermute | solution.py:45
  262.6 22.4 %collective-permute-start.32 = (bf16[112,2048]{1,0:T(8,128)(2,1)S(1)}, bf16[112,2048]{1,0:T(8,128)(2,1)S(1)}, u32[]{:S(2)}, u32[]{:S(2)}) collective-permute-start(bf16[112,2048]{1,0:T(8,128)(2,1)S(1)} %get-tuple-element.130), channel_id=1, source_target_pairs={{0,1},{64,65},{1,0},{65,64},{2,3},{66,67},{3,2},{67,66},{4,5},{68,... | collective-permute-start | bytes 1376264 | tf_op jit(solution)/shard_map/ppermute | solution.py:45
  285.7 15.2 %collective-permute-start.39 = (bf16[112,2048]{1,0:T(8,128)(2,1)S(1)}, bf16[112,2048]{1,0:T(8,128)(2,1)}, u32[]{:S(2)}, u32[]{:S(2)}) collective-permute-start(bf16[112,2048]{1,0:T(8,128)(2,1)S(1)} %get-tuple-element.153.refs_0_), channel_id=1, source_target_pairs={{1,0},{65,64},{0,1},{64,65},{3,2},{67,66},{2,3},{66,67},{5,4},{69,... | collective-permute-start | bytes 1376264 | tf_op jit(solution)/shard_map/ppermute | solution.py:41
  286.4 20.3 %collective-permute-start.40 = (bf16[112,2048]{1,0:T(8,128)(2,1)S(1)}, bf16[112,2048]{1,0:T(8,128)(2,1)}, u32[]{:S(2)}, u32[]{:S(2)}) collective-permute-start(bf16[112,2048]{1,0:T(8,128)(2,1)S(1)} %get-tuple-element.153.refs_0_), channel_id=1, source_target_pairs={{64,0},{1,64},{65,1},{0,65},{66,2},{3,66},{67,3},{2,67},{68,4},{5,... | collective-permute-start | bytes 1376264 | tf_op jit(solution)/shard_map/ppermute | solution.py:41
  287.3 20.5 %collective-permute-start.41 = (bf16[112,2048]{1,0:T(8,128)(2,1)S(1)}, bf16[112,2048]{1,0:T(8,128)(2,1)}, u32[]{:S(2)}, u32[]{:S(2)}) collective-permute-start(bf16[112,2048]{1,0:T(8,128)(2,1)S(1)} %get-tuple-element.153.refs_0_), channel_id=1, source_target_pairs={{65,0},{0,64},{64,1},{1,65},{67,2},{2,66},{66,3},{3,67},{69,4},{4,... | collective-permute-start | bytes 1376264 | tf_op jit(solution)/shard_map/ppermute | solution.py:41
  288.4 20.0 %collective-permute-start.42 = (bf16[112,2048]{1,0:T(8,128)(2,1)S(1)}, bf16[112,2048]{1,0:T(8,128)(2,1)}, u32[]{:S(2)}, u32[]{:S(2)}) collective-permute-start(bf16[112,2048]{1,0:T(8,128)(2,1)S(1)} %get-tuple-element.153.refs_0_), channel_id=1, source_target_pairs={{0,2},{2,0},{1,3},{3,1},{4,6},{6,4},{5,7},{7,5},{8,10},{10,8},{9,1... | collective-permute-start | bytes 1376264 | tf_op jit(solution)/shard_map/ppermute | solution.py:50
  334.0 14.4 %collective-permute-start.64 = (bf16[1,512,256]{2,1,0:T(8,128)(2,1)S(1)}, bf16[1,512,256]{2,1,0:T(8,128)(2,1)S(1)}, u32[]{:S(2)}, u32[]{:S(2)}) collective-permute-start(bf16[1,512,256]{2,1,0:T(8,128)(2,1)S(1)} %get-tuple-element.151), channel_id=1, source_target_pairs={{0,48},{16,0},{32,16},{48,32},{1,49},{17,1},{33,17},{49,33},{2,50}... | collective-permute-start | bytes 786440 | tf_op jit(solution)/shard_map/ppermute | solution.py:105
  336.9 14.9 %collective-permute-start.63 = (bf16[1,512,256]{2,1,0:T(8,128)(2,1)S(1)}, bf16[1,512,256]{2,1,0:T(8,128)(2,1)S(1)}, u32[]{:S(2)}, u32[]{:S(2)}) collective-permute-start(bf16[1,512,256]{2,1,0:T(8,128)(2,1)S(1)} %get-tuple-element.152), channel_id=1, source_target_pairs={{0,16},{16,32},{32,48},{48,0},{1,17},{17,33},{33,49},{49,1},{2,18}... | collective-permute-start | bytes 786440 | tf_op jit(solution)/shard_map/ppermute | solution.py:105
  336.9 15.2 %collective-permute-start.62 = (bf16[1,512,256]{2,1,0:T(8,128)(2,1)S(1)}, bf16[1,512,256]{2,1,0:T(8,128)(2,1)S(1)}, u32[]{:S(2)}, u32[]{:S(2)}) collective-permute-start(bf16[1,512,256]{2,1,0:T(8,128)(2,1)S(1)} %get-tuple-element.150), channel_id=1, source_target_pairs={{0,32},{16,48},{32,0},{48,16},{1,33},{17,49},{33,1},{49,17},{2,34}... | collective-permute-start | bytes 786440 | tf_op jit(solution)/shard_map/ppermute | solution.py:105
  340.3 14.7 %collective-permute-start.58 = (bf16[4,128,256]{2,1,0:T(8,128)(2,1)S(1)}, bf16[4,128,256]{2,1,0:T(8,128)(2,1)S(1)}, u32[]{:S(2)}, u32[]{:S(2)}) collective-permute-start(bf16[4,128,256]{2,1,0:T(8,128)(2,1)S(1)} %get-tuple-element.148), channel_id=1, source_target_pairs={{0,12},{4,0},{8,4},{12,8},{1,13},{5,1},{9,5},{13,9},{2,14},{6,2},{... | collective-permute-start | bytes 786440 | tf_op jit(solution)/shard_map/ppermute | solution.py:105
  341.6 13.4 %collective-permute-start.57 = (bf16[4,128,256]{2,1,0:T(8,128)(2,1)S(1)}, bf16[4,128,256]{2,1,0:T(8,128)(2,1)S(1)}, u32[]{:S(2)}, u32[]{:S(2)}) collective-permute-start(bf16[4,128,256]{2,1,0:T(8,128)(2,1)S(1)} %get-tuple-element.149), channel_id=1, source_target_pairs={{0,4},{4,8},{8,12},{12,0},{1,5},{5,9},{9,13},{13,1},{2,6},{6,10},{... | collective-permute-start | bytes 786440 | tf_op jit(solution)/shard_map/ppermute | solution.py:105
  352.1 14.6 %collective-permute-start.51 = (bf16[1,512,256]{2,1,0:T(8,128)(2,1)S(1)}, bf16[1,512,256]{2,1,0:T(8,128)(2,1)S(1)}, u32[]{:S(2)}, u32[]{:S(2)}) collective-permute-start(bf16[1,512,256]{2,1,0:T(8,128)(2,1)S(1)} %get-tuple-element.146), channel_id=1, source_target_pairs={{0,16},{16,32},{32,48},{48,0},{1,17},{17,33},{33,49},{49,1},{2,18}... | collective-permute-start | bytes 786440 | tf_op jit(solution)/shard_map/ppermute | solution.py:105
  355.0 15.5 %collective-permute-start.50 = (bf16[1,512,256]{2,1,0:T(8,128)(2,1)S(1)}, bf16[1,512,256]{2,1,0:T(8,128)(2,1)S(1)}, u32[]{:S(2)}, u32[]{:S(2)}) collective-permute-start(bf16[1,512,256]{2,1,0:T(8,128)(2,1)S(1)} %get-tuple-element.144), channel_id=1, source_target_pairs={{0,32},{16,48},{32,0},{48,16},{1,33},{17,49},{33,1},{49,17},{2,34}... | collective-permute-start | bytes 786440 | tf_op jit(solution)/shard_map/ppermute | solution.py:105
  355.1 15.5 %collective-permute-start.67 = (bf16[1,128,256]{2,1,0:T(8,128)(2,1)S(1)}, bf16[1,128,256]{2,1,0:T(8,128)(2,1)S(1)}, u32[]{:S(2)}, u32[]{:S(2)}) collective-permute-start(bf16[1,128,256]{2,1,0:T(8,128)(2,1)S(1)} %get-tuple-element.174), channel_id=1, source_target_pairs={{0,12},{4,0},{8,4},{12,8},{1,13},{5,1},{9,5},{13,9},{2,14},{6,2},{... | collective-permute-start | bytes 196616 | tf_op jit(solution)/shard_map/ppermute | solution.py:105
  358.4 13.9 %collective-permute-start.66 = (bf16[1,128,256]{2,1,0:T(8,128)(2,1)S(1)}, bf16[1,128,256]{2,1,0:T(8,128)(2,1)S(1)}, u32[]{:S(2)}, u32[]{:S(2)}) collective-permute-start(bf16[1,128,256]{2,1,0:T(8,128)(2,1)S(1)} %get-tuple-element.175), channel_id=1, source_target_pairs={{0,4},{4,8},{8,12},{12,0},{1,5},{5,9},{9,13},{13,1},{2,6},{6,10},{... | collective-permute-start | bytes 196616 | tf_op jit(solution)/shard_map/ppermute | solution.py:105
  359.6 12.7 %collective-permute-start.65 = (bf16[1,128,256]{2,1,0:T(8,128)(2,1)S(1)}, bf16[1,128,256]{2,1,0:T(8,128)(2,1)S(1)}, u32[]{:S(2)}, u32[]{:S(2)}) collective-permute-start(bf16[1,128,256]{2,1,0:T(8,128)(2,1)S(1)} %get-tuple-element.173), channel_id=1, source_target_pairs={{0,8},{4,12},{8,0},{12,4},{1,9},{5,13},{9,1},{13,5},{2,10},{6,14},... | collective-permute-start | bytes 196616 | tf_op jit(solution)/shard_map/ppermute | solution.py:105
  381.0 14.4 %collective-permute-start.46 = (bf16[448,2048]{1,0:T(8,128)(2,1)}, bf16[448,2048]{1,0:T(8,128)(2,1)}, u32[]{:S(2)}, u32[]{:S(2)}) collective-permute-start(bf16[448,2048]{1,0:T(8,128)(2,1)} %get-tuple-element.52), channel_id=1, source_target_pairs={{0,2},{2,0},{1,3},{3,1},{4,6},{6,4},{5,7},{7,5},{8,10},{10,8},{9,1... | collective-permute-start | bytes 5505032 | tf_op jit(solution)/shard_map/ppermute | solution.py:54
  398.6 13.6 %collective-permute-start.49 = (bf16[112,2048]{1,0:T(8,128)(2,1)}, bf16[112,2048]{1,0:T(8,128)(2,1)S(1)}, u32[]{:S(2)}, u32[]{:S(2)}) collective-permute-start(bf16[112,2048]{1,0:T(8,128)(2,1)} %get-tuple-element.125), channel_id=1, source_target_pairs={{0,65},{64,0},{1,64},{65,1},{2,67},{66,2},{3,66},{67,3},{4,69},{68... | collective-permute-start | bytes 1376264 | tf_op jit(solution)/shard_map/ppermute | solution.py:45
  400.7 22.4 %collective-permute-start.48 = (bf16[112,2048]{1,0:T(8,128)(2,1)}, bf16[112,2048]{1,0:T(8,128)(2,1)}, u32[]{:S(2)}, u32[]{:S(2)}) collective-permute-start(bf16[112,2048]{1,0:T(8,128)(2,1)} %get-tuple-element.126), channel_id=1, source_target_pairs={{0,64},{64,1},{1,65},{65,0},{2,66},{66,3},{3,67},{67,2},{4,68},{68... | collective-permute-start | bytes 1376264 | tf_op jit(solution)/shard_map/ppermute | solution.py:45
  400.7 23.3 %collective-permute-start.47 = (bf16[112,2048]{1,0:T(8,128)(2,1)}, bf16[112,2048]{1,0:T(8,128)(2,1)}, u32[]{:S(2)}, u32[]{:S(2)}) collective-permute-start(bf16[112,2048]{1,0:T(8,128)(2,1)} %get-tuple-element.124), channel_id=1, source_target_pairs={{0,1},{64,65},{1,0},{65,64},{2,3},{66,67},{3,2},{67,66},{4,5},{68,... | collective-permute-start | bytes 1376264 | tf_op jit(solution)/shard_map/ppermute | solution.py:45
  403.6 25.6 %collective-permute-start.71 = (bf16[64,3072]{1,0:T(8,128)(2,1)S(1)}, bf16[64,3072]{1,0:T(8,128)(2,1)S(1)}, u32[]{:S(2)}, u32[]{:S(2)}) collective-permute-start(bf16[64,3072]{1,0:T(8,128)(2,1)S(1)} %broadcast_select_fusion.2), channel_id=1, source_target_pairs={{0,64},{64,0},{1,65},{65,1},{2,66},{66,2},{3,67},{67,3},{4,68},{68... | collective-permute-start | bytes 1179656 | tf_op jit(solution)/shard_map/ppermute | solution.py:89
  (75 other events, 887.6 us)
Sparse Core Ops, SparseCore 0:
  19.1 50.6 all-gather.2
  71.9 88.8 all-gather.4
  234.8 94.3 reduce-scatter.1

commit v3 on v2

v3 whole, which is shorter than its diff:
```python
import math

import jax
import jax.numpy as jnp
from jax import lax
from jax.experimental import pallas as pl
from jax.experimental.pallas import tpu as pltpu
from jax.sharding import Mesh
from jax.sharding import PartitionSpec as P

HEADS = 32
KV_HEADS = 8
GROUP = HEADS // KV_HEADS
EPSILON = 1e-05
ROPE_BASE = 500000.0
MASKED = -1e30
GAIN_COLS = 128
VMEM_LIMIT = 56 * 2**20
BF = jnp.bfloat16
F32 = jnp.float32


def cost(micros):
    return pl.CostEstimate(flops=micros * 10**9, bytes_accessed=2**20, transcendentals=0)


SWAP = [(0, 1), (1, 0)]


def mm(left, right):
    return jnp.dot(left, right, preferred_element_type=F32)


def mm_nt(left, right):
    return lax.dot_general(left, right, (((1,), (1,)), ((), ())), preferred_element_type=F32)


def mm_tn(left, right):
    return lax.dot_general(left, right, (((0,), (0,)), ((), ())), preferred_element_type=F32)


AT = (0, 2, 1, 3)


def from_chip(value, k):
    return lax.ppermute(value, ("a", "t"), [(AT[(i + k) % 4], AT[i]) for i in range(4)])


def to_chip(value, k):
    return lax.ppermute(value, ("a", "t"), [(AT[i], AT[(i + k) % 4]) for i in range(4)])


def after(value, *others):
    return lax.optimization_barrier((value, *others))[0]


def swap_core(value):
    return lax.ppermute(value, "c", SWAP)


def gather_rows(rows):
    mine = [rows, from_chip(rows, 2), from_chip(rows, 1), from_chip(rows, 3)]
    return mine + [swap_core(piece) for piece in mine]


def chip_parts(mine, got):
    rows = mine.shape[0] // 4
    parts = [
        mine[i * rows : (i + 1) * rows].astype(F32) + got[i * rows : (i + 1) * rows].astype(F32)
        for i in range(4)
    ]
    return [parts[0]] + [part.astype(BF) for part in parts[1:]]


def send_parts(parts):
    return [to_chip(part, k) for part, k in zip(parts[1:], (2, 1, 3))]


def total_of(parts, got):
    total = parts[0]
    for part in got:
        total = total + part.astype(F32)
    return total


def spread(quarters, a, c, wait=()):
    first = c == 0
    r = quarters[0].shape[0]
    keep = [jnp.where(first, quarters[2 * i], quarters[2 * i + 1]) for i in range(2)]
    give = [jnp.where(first, quarters[2 * i + 1], quarters[2 * i]) for i in range(2)]
    got = swap_core(jnp.concatenate(give, axis=0))
    both = [
        jnp.concatenate([jnp.where(first, k, g), jnp.where(first, g, k)], axis=0)
        for k, g in zip(keep, (got[:r], got[r:]))
    ]
    first_a = a == 0
    keep_a = jnp.where(first_a, both[0], both[1])
    give_a = jnp.where(first_a, both[1], both[0])
    got_a = lax.ppermute(after(give_a, *wait), "a", SWAP)
    rows = [jnp.where(first_a, keep_a, got_a), jnp.where(first_a, got_a, keep_a)]
    return jnp.concatenate(rows, axis=0), got_a


def unspread(rows, a, c, wait=()):
    half = rows.shape[0] // 2
    r = half // 2
    low, high = rows[:half], rows[half:]
    first_a, first = a == 0, c == 0
    keep_a = jnp.where(first_a, low, high)
    give_a = jnp.where(first_a, high, low)
    got_a = lax.ppermute(after(give_a, *wait), "a", SWAP)
    by_a = [jnp.where(first_a, keep_a, got_a), jnp.where(first_a, got_a, keep_a)]
    keep = [jnp.where(first, v[:r], v[r:]) for v in by_a]
    give = [jnp.where(first, v[r:], v[:r]) for v in by_a]
    got = swap_core(jnp.concatenate(give, axis=0))
    quarters = []
    for k, g in zip(keep, (got[:r], got[r:])):
        quarters += [jnp.where(first, k, g), jnp.where(first, g, k)]
    return quarters, got_a


def columns_of(quarters, start, width):
    return jnp.concatenate([q[:, start : start + width] for q in quarters], axis=1).astype(F32)


def sum_along(pieces, axis):
    total = pieces[0].astype(F32)
    for k in (2, 1, 3):
        got = lax.ppermute(pieces[k], axis, [(i, (i + k) % 4) for i in range(4)])
        total = total + got.astype(F32)
    return total.astype(BF)


def sum_zy(by_z, by_y, *others):
    z, y = lax.axis_index("z"), lax.axis_index("y")
    first = after((sum_along(by_z, "z"), sum_along(by_y, "y")), *others)
    both = []
    for part, axis, place in zip(first, ("y", "z"), (y, z)):
        rows = part.shape[0] // 4
        pieces = [
            lax.dynamic_slice_in_dim(part, (place + k) % 4 * rows, rows, axis=0) for k in range(4)
        ]
        both.append(sum_along(pieces, axis))
    return jnp.concatenate(both, axis=1)


def to_place(rows):
    n, d = rows.shape
    return rows.reshape(n, 2, 16, d // 32).transpose(0, 2, 1, 3).reshape(n, d)


def from_place(rows):
    n, d = rows.shape
    return rows.reshape(n, 16, 2, d // 32).transpose(0, 2, 1, 3).reshape(n, d)


def norm_back(rescaled, factor, gain, upstream):
    inner = upstream * gain
    return factor * (inner - rescaled * jnp.mean(inner * rescaled, axis=-1, keepdims=True))


def step_block(s):
    return (s + 2) % 4


def row_block(width):
    return lambda rows: pl.BlockSpec((rows, width), lambda s: (step_block(s), 0))


def fixed(shape):
    return pl.BlockSpec(shape, lambda *_: (0,) * len(shape))


def halves(rows, width):
    return [
        pl.BlockSpec((rows, width), lambda s: (jnp.maximum(s - 2, 0), 0)),
        pl.BlockSpec((rows, width), lambda s: (jnp.minimum(s, 1), 0)),
    ]


def load_block(s, pieces, scratch):
    part = pieces[0].shape[0]
    for b in range(4):

        @pl.when(step_block(s) == b)
        def _():
            scratch[:part] = pieces[2 * b][...]
            scratch[part:] = pieces[2 * b + 1][...]


def store_half(s, mine_ref, other_ref, value):
    @pl.when(s < 2)
    def _():
        other_ref[...] = value

    @pl.when(s >= 2)
    def _():
        mine_ref[...] = value


def pick_rows(columns):
    one = (
        lax.broadcasted_iota(jnp.int32, (8, columns.shape[1]), 0)
        == lax.broadcasted_iota(jnp.int32, (8, columns.shape[1]), 1)
    ).astype(BF)
    return mm_nt(one, columns)


def turn(values, cosines, sines, head):
    width = values.shape[1]
    lane = lax.broadcasted_iota(jnp.int32, values.shape, 1)
    low = lane % head < head // 2
    partner = jnp.where(
        low, pltpu.roll(values, width - head // 2, 1), pltpu.roll(values, head // 2, 1)
    )
    return values * cosines + partner * sines


def double(values, times):
    return jnp.concatenate([values] * times, axis=1)


def by_head(values, head):
    lane = lax.broadcasted_iota(jnp.int32, values.shape, 1) // head
    zero = jnp.zeros_like(values)
    return jnp.concatenate([jnp.where(lane == h, values, zero) for h in range(GROUP)], axis=0)


def take_heads(values, rows, head):
    lane = lax.broadcasted_iota(jnp.int32, (rows, values.shape[1]), 1) // head
    out = values[:rows]
    for h in range(1, GROUP):
        out = jnp.where(lane == h, values[h * rows : (h + 1) * rows], out)
    return out


def fold_heads(values, head):
    pair = values[:, : 2 * head] + values[:, 2 * head :]
    return pair + pltpu.roll(pair, head, 1)


def attn_forward_kernel(head, *refs):
    pieces = refs[:8]
    (w_ref, cos_ref, sin_ref, mask_ref,
     mine_ref, other_ref, normed_ref, factor_ref, q_ref, k_ref, v_ref, probs_ref, mixed_ref,
     gains_ref, x_ref, gain_scr) = refs[8:]
    s = pl.program_id(0)
    nq, cut = GROUP * head, (GROUP + 2) * head
    rows = x_ref.shape[0]

    @pl.when(s == 0)
    def _():
        gain_scr[...] = pick_rows(w_ref[:, cut + nq :])
        gains_ref[...] = gain_scr[...]

    load_block(s, pieces, x_ref)
    x = x_ref[...].astype(F32)
    factor = lax.rsqrt(jnp.mean(x * x, axis=-1, keepdims=True) + EPSILON)
    factor_ref[...] = jnp.broadcast_to(factor, factor_ref.shape)
    normed = (x * factor * gain_scr[0:1, :]).astype(BF)
    normed_ref[...] = normed
    qkv = mm(normed, w_ref[:, :cut])
    cosines, sines = cos_ref[...], sin_ref[...]
    query = turn(qkv[:, :nq], double(cosines, 2), double(sines, 2), head).astype(BF)
    kv = qkv[:, nq:]
    turned = turn(kv, cosines, sines, head)
    low = lax.broadcasted_iota(jnp.int32, kv.shape, 1) < head
    key = double(jnp.where(low, turned, pltpu.roll(turned, head, 1)), 2).astype(BF)
    value = double(jnp.where(low, pltpu.roll(kv, head, 1), kv), 2).astype(BF)
    q_ref[...] = query
    k_ref[...] = key
    v_ref[...] = value
    scores = mm_nt(by_head(query, head), key) * (1.0 / math.sqrt(head))
    allowed = mask_ref[...] == 0
    scores = jnp.where(jnp.concatenate([allowed] * GROUP, axis=0), scores, MASKED)
    weights = jnp.exp(scores - jnp.max(scores, axis=-1, keepdims=True))
    probs = weights / jnp.sum(weights, axis=-1, keepdims=True)
    probs_ref[...] = probs
    mixed = take_heads(mm(probs.astype(BF), value), rows, head).astype(BF)
    mixed_ref[...] = mixed
    store_half(s, mine_ref, other_ref, mm_nt(mixed, w_ref[:, cut : cut + nq]).astype(BF))


def attn_forward(pieces, w, cosines, sines, mask, head):
    part, d = pieces[0].shape
    rows = 2 * part
    nq = GROUP * head
    spec = lambda width: row_block(width)(rows)
    return pl.pallas_call(
        lambda *refs: attn_forward_kernel(head, *refs),
        grid=(4,),
        in_specs=[fixed(p.shape) for p in pieces]
        + [fixed(w.shape), spec(2 * head), spec(2 * head), spec(rows)],
        out_specs=halves(rows, d)
        + [spec(d), spec(128), spec(nq), spec(nq), spec(nq)]
        + [pl.BlockSpec((GROUP * rows, rows), lambda s: (step_block(s), 0)), spec(nq), fixed((8, d))],
        out_shape=[jax.ShapeDtypeStruct((2 * rows, d), BF)] * 2
        + [jax.ShapeDtypeStruct((4 * rows, d), BF), jax.ShapeDtypeStruct((4 * rows, 128), F32)]
        + [jax.ShapeDtypeStruct((4 * rows, nq), BF)] * 3
        + [
            jax.ShapeDtypeStruct((4 * GROUP * rows, rows), F32),
            jax.ShapeDtypeStruct((4 * rows, nq), BF),
            jax.ShapeDtypeStruct((8, d), F32),
        ],
        scratch_shapes=[pltpu.VMEM((rows, d), BF), pltpu.VMEM((8, d), F32)],
        compiler_params=pltpu.CompilerParams(vmem_limit_bytes=VMEM_LIMIT),
        cost_estimate=cost(30),
    )(*pieces, w, cosines, sines, mask)


def attn_backward_kernel(head, *refs):
    d_pieces, x_pieces = refs[:8], refs[8:16]
    (w_ref, cos_ref, sin_ref, factor_ref, normed_ref, q_ref, k_ref, v_ref, probs_ref, mixed_ref,
     extra_ref, place_ref, mine_ref, other_ref) = refs[16:30]
    ga_refs, gb_refs = refs[30:34], refs[34:38]
    db_ref, x_ref, acc_a, acc_o, gain_acc = refs[38:]
    s = pl.program_id(0)
    nq, cut = GROUP * head, (GROUP + 2) * head
    rows = x_ref.shape[0]
    scale = 1.0 / math.sqrt(head)

    @pl.when(s == 0)
    def _():
        acc_a[...] = jnp.zeros_like(acc_a)
        acc_o[...] = jnp.zeros_like(acc_o)
        gain_acc[...] = jnp.zeros_like(gain_acc)

    load_block(s, d_pieces, db_ref)
    load_block(s, x_pieces, x_ref)
    d_branch = db_ref[...]
    acc_o[:, :nq] += mm_tn(d_branch, mixed_ref[...])
    d_mixed = by_head(mm(d_branch, w_ref[:, cut : cut + nq]).astype(BF), head)
    d_probs = mm_nt(d_mixed, v_ref[...])
    probs = probs_ref[...]
    d_value = fold_heads(mm_tn(probs.astype(BF), d_mixed), head)
    d_scores = probs * (d_probs - jnp.sum(d_probs * probs, axis=-1, keepdims=True))
    d_scores = d_scores.astype(BF)
    d_query = take_heads(mm(d_scores, k_ref[...]), rows, head) * scale
    d_key = fold_heads(mm_tn(d_scores, by_head(q_ref[...], head)), head) * scale
    cosines, sines = cos_ref[...], -sin_ref[...]
    d_query = turn(d_query, double(cosines, 2), double(sines, 2), head).astype(BF)
    d_key = turn(d_key, cosines, sines, head)
    low = lax.broadcasted_iota(jnp.int32, d_key.shape, 1) < head
    d_kv = jnp.where(low, d_key, d_value).astype(BF)
    d_qkv = jnp.concatenate([d_query, d_kv], axis=1)
    acc_a[...] += mm_tn(normed_ref[...], d_qkv)
    d_normed = mm_nt(d_qkv, w_ref[:, :cut])
    store_half(s, mine_ref, other_ref, d_normed.astype(BF))
    u1 = x_ref[...].astype(F32) * factor_ref[:, :1]
    gain_acc[0:1, :] += jnp.sum(d_normed * u1, axis=0, keepdims=True)

    @pl.when(s == 3)
    def _():
        gains = gain_acc[...] + extra_ref[...]
        one = (
            lax.broadcasted_iota(jnp.int32, (8, GAIN_COLS), 0)
            == lax.broadcasted_iota(jnp.int32, (8, GAIN_COLS), 1)
        ).astype(BF)
        acc_o[:, nq:] = mm_tn(gains.astype(BF), one)
        part = ga_refs[0].shape[0]
        small = part // 4
        for k in range(4):
            z = lax.rem(place_ref[0] + k, 4)
            y = lax.rem(place_ref[1] + k, 4)
            ga_refs[k][...] = acc_a[pl.ds(pl.multiple_of(z * part, part), part)].astype(BF)
            for i in range(4):
                at = pl.ds(pl.multiple_of(i * part + y * small, small), small)
                gb_refs[k][i * small : (i + 1) * small] = acc_o[at].astype(BF)


def attn_backward(d_pieces, x_pieces, w, cosines, sines, saved, extra, place, head):
    factor, normed, query, key, value, probs, mixed = saved
    part, d = d_pieces[0].shape
    rows = 2 * part
    nq, cut = GROUP * head, (GROUP + 2) * head
    spec = lambda width: row_block(width)(rows)
    grads = [(d // 4, cut)] * 4 + [(d // 4, nq + GAIN_COLS)] * 4
    return pl.pallas_call(
        lambda *refs: attn_backward_kernel(head, *refs),
        grid=(4,),
        in_specs=[fixed(p.shape) for p in (*d_pieces, *x_pieces)]
        + [fixed(w.shape), spec(2 * head), spec(2 * head), spec(128), spec(d)]
        + [spec(nq), spec(nq), spec(nq)]
        + [pl.BlockSpec((GROUP * rows, rows), lambda s: (step_block(s), 0)), spec(nq)]
        + [fixed((8, d)), pl.BlockSpec(memory_space=pltpu.SMEM)],
        out_specs=halves(rows, d) + [fixed(shape) for shape in grads],
        out_shape=[jax.ShapeDtypeStruct((2 * rows, d), BF)] * 2
        + [jax.ShapeDtypeStruct(shape, BF) for shape in grads],
        scratch_shapes=[
            pltpu.VMEM((rows, d), BF),
            pltpu.VMEM((rows, d), BF),
            pltpu.VMEM((d, cut), F32),
            pltpu.VMEM((d, nq + GAIN_COLS), F32),
            pltpu.VMEM((8, d), F32),
        ],
        compiler_params=pltpu.CompilerParams(vmem_limit_bytes=VMEM_LIMIT),
        cost_estimate=cost(10),
    )(*d_pieces, *x_pieces, w, cosines, sines, factor, normed, query, key, value, probs, mixed,
      extra, place)


def mlp_kernel(*refs):
    n_pieces, c_pieces = refs[:8], refs[8:16]
    (wg_ref, wu_ref, wd_ref, dg_ref, du_ref, hid_ref, mine_ref, other_ref,
     n_scr, c_scr, w_scr, d_scr) = refs[16:]
    j = pl.program_id(0)
    part = n_pieces[0].shape[0]
    tile = wg_ref.shape[1]
    ff = 4 * tile

    @pl.when(j == 0)
    def _():
        for i in range(8):
            n_scr[i * part : (i + 1) * part] = n_pieces[i][...]
            c_scr[i * part : (i + 1) * part] = c_pieces[i][...]

    for step in range(4):

        @pl.when(j == step)
        def _():
            w_scr[:, step * tile : (step + 1) * tile] = wg_ref[...]
            w_scr[:, ff + step * tile : ff + (step + 1) * tile] = wu_ref[...]
            gate = mm(n_scr[...], wg_ref[...])
            up = mm(n_scr[...], wu_ref[...])
            d_hidden = mm(c_scr[...], wd_ref[...])
            sig = jax.nn.sigmoid(gate)
            silu = gate * sig
            hid_ref[...] = (silu * up).astype(BF)
            d_gate = (d_hidden * up * sig * (1.0 + gate * (1.0 - sig))).astype(BF)
            d_up = (d_hidden * silu).astype(BF)
            dg_ref[...] = d_gate
            du_ref[...] = d_up
            d_scr[:, step * tile : (step + 1) * tile] = d_gate
            d_scr[:, ff + step * tile : ff + (step + 1) * tile] = d_up

    @pl.when(j >= 4)
    def _():
        wide = mine_ref.shape[1]
        rows = pl.ds(pl.multiple_of((j - 4) * wide, wide), wide)
        d_n2 = mm_nt(d_scr[...], w_scr[rows, :]).astype(BF)
        mine_ref[...] = d_n2[: 4 * part]
        other_ref[...] = d_n2[4 * part :]


def mlp(n_pieces, c_pieces, w):
    part, d = n_pieces[0].shape
    rows, ff = 8 * part, w.shape[1] // 3
    tile, wide = ff // 4, d // 4
    at = lambda k: pl.BlockSpec((d, tile), lambda j: (0, 4 * k + jnp.minimum(j, 3)))
    return pl.pallas_call(
        mlp_kernel,
        grid=(8,),
        in_specs=[fixed((part, d))] * 16 + [at(0), at(1), at(2)],
        out_specs=[pl.BlockSpec((rows, tile), lambda j: (0, jnp.minimum(j, 3)))] * 3
        + [pl.BlockSpec((rows // 2, wide), lambda j: (0, jnp.maximum(j - 4, 0)))] * 2,
        out_shape=[jax.ShapeDtypeStruct((rows, ff), BF)] * 3
        + [jax.ShapeDtypeStruct((rows // 2, d), BF)] * 2,
        scratch_shapes=[
            pltpu.VMEM((rows, d), BF),
            pltpu.VMEM((rows, d), BF),
            pltpu.VMEM((d, 2 * ff), BF),
            pltpu.VMEM((rows, 2 * ff), BF),
        ],
        compiler_params=pltpu.CompilerParams(vmem_limit_bytes=VMEM_LIMIT),
        cost_estimate=cost(40),
    )(*n_pieces, *c_pieces, w, w, w)


def mlp_grads_kernel(sides, *refs):
    pieces, rights = refs[:8], refs[8 : 8 + sides]
    g_ref, all_ref, turned_ref = refs[-3:]
    part = pieces[0].shape[0]
    j = pl.program_id(0)

    @pl.when(j == 0)
    def _():
        for i in range(8):
            all_ref[i * part : (i + 1) * part] = pieces[i][...]
        turned_ref[...] = all_ref[...].T

    for k in range(sides):

        @pl.when((j >= 4 * k) & (j < 4 * k + 4))
        def _():
            g_ref[...] = mm(turned_ref[...], rights[k][...]).astype(BF)


def mlp_grads(pieces, rights, into=None):
    part, d = pieces[0].shape
    rows, ff = rights[0].shape
    tile = ff // 4
    sides = len(rights)
    start = 0 if into is None else 12 - 4 * sides
    at = lambda k: pl.BlockSpec((rows, tile), lambda j: (0, jnp.clip(j - 4 * k, 0, 3)))
    extra = [] if into is None else [into]
    return pl.pallas_call(
        lambda *refs: mlp_grads_kernel(sides, *refs),
        grid=(4 * sides,),
        in_specs=[fixed((part, d))] * 8
        + [at(k) for k in range(sides)]
        + [pl.BlockSpec(memory_space=pl.ANY)] * len(extra),
        out_specs=pl.BlockSpec((d, tile), lambda j: (0, start + j)),
        out_shape=jax.ShapeDtypeStruct((d, 3 * ff), BF),
        input_output_aliases={8 + sides: 0} if extra else {},
        scratch_shapes=[pltpu.VMEM((rows, d), BF), pltpu.VMEM((d, rows), BF)],
        compiler_params=pltpu.CompilerParams(vmem_limit_bytes=VMEM_LIMIT),
        cost_estimate=cost(20 * sides),
    )(*pieces, *rights, *extra)


def mlp_out_kernel(x_ref, w_ref, mine_ref, other_ref):
    half = x_ref.shape[0] // 2
    out = mm_nt(x_ref[...], w_ref[...]).astype(BF)
    mine_ref[...] = out[:half]
    other_ref[...] = out[half:]


def mlp_out(hid, w):
    rows, ff = hid.shape
    d = w.shape[0]
    wide = d // 4
    return pl.pallas_call(
        mlp_out_kernel,
        grid=(4,),
        in_specs=[fixed((rows, ff)), pl.BlockSpec((wide, ff), lambda j: (j, 2))],
        out_specs=[pl.BlockSpec((rows // 2, wide), lambda j: (0, j))] * 2,
        out_shape=[jax.ShapeDtypeStruct((rows // 2, d), BF)] * 2,
        compiler_params=pltpu.CompilerParams(vmem_limit_bytes=VMEM_LIMIT),
        cost_estimate=cost(5),
    )(hid, w)


def token_tables(seg, shift, own, head):
    count, block = seg.shape
    seg = jnp.where(shift == 0, seg, jnp.roll(seg, own, axis=1))
    order = (jnp.arange(block, dtype=jnp.int32)[None, :] + shift * own) % block
    earlier = jnp.sum((seg[:, None, :] < seg[:, :, None]).astype(jnp.int32), axis=2)
    positions = (order - earlier).reshape(count * block, 1)
    allowed = (seg[:, :, None] == seg[:, None, :]) & (order[:, None, :] <= order[:, :, None])
    mask = jnp.where(allowed, 0.0, MASKED).astype(F32).reshape(count * block, block)
    lane = jnp.arange(2 * head)
    frequency = jnp.exp(-math.log(ROPE_BASE) * ((lane % (head // 2)).astype(F32) / (head // 2)))
    angles = positions.astype(F32) * frequency
    sines = jnp.where(lane % head < head // 2, -1.0, 1.0) * jnp.sin(angles)
    return jnp.cos(angles), sines, mask


def local(
    tokens, segment_ids, attn_gain, w_query, w_key, w_value, w_out,
    mlp_gain, w_gate, w_up, w_down, cotangent,
):
    a, c, t = lax.axis_index("a"), lax.axis_index("c"), lax.axis_index("t")
    own = tokens.shape[0]
    nq = w_query.shape[1] // 4
    nk = w_key.shape[1] // 4
    ff = w_gate.shape[1] // 4
    head = nk
    cut = nq + 2 * nk

    gains = jnp.stack([attn_gain, mlp_gain], axis=1)
    gains = jnp.pad(gains, ((0, 0), (0, GAIN_COLS - 2)))
    quarter = lambda w, i: w[:, i * w.shape[1] // 4 : (i + 1) * w.shape[1] // 4]
    attn_pack = [
        jnp.concatenate(
            [quarter(w, i) for w in (w_query, w_key, w_value, w_out.T)] + [gains], axis=1
        )
        for i in range(4)
    ]
    attn_rows, attn_got = spread(attn_pack, a, c)
    attn_w = lax.all_gather(attn_rows, ("z", "y"), axis=0, tiled=True)
    x_own, c_own = to_place(tokens), to_place(cotangent)
    x_pieces = gather_rows(after(x_own, attn_got))
    mlp_pack = [
        jnp.concatenate([quarter(w, i) for w in (w_gate, w_up, w_down.T)], axis=1) for i in range(4)
    ]
    mlp_rows, mlp_got = spread(mlp_pack, a, c, x_pieces[1:4])
    mlp_w = lax.all_gather(mlp_rows, ("z", "y"), axis=0, tiled=True)
    c_pieces = gather_rows(after(c_own, *x_pieces[1:4]))

    seg = jnp.stack([segment_ids, lax.ppermute(segment_ids, "a", SWAP)])
    seg = jnp.concatenate([seg, swap_core(seg)], axis=0)
    shift = jnp.stack([t, t ^ a, t, t ^ a])[:, None]
    cosines, sines, mask = token_tables(seg, shift, own, head)

    forward = attn_forward(
        after(x_pieces, *c_pieces[1:4]), attn_w, cosines, sines, mask, head
    )
    mine, other, normed, factor1, query, key, value, probs, mixed, gain_rows = forward
    gain_a, gain_m = gain_rows[0], gain_rows[1]
    parts = chip_parts(mine, swap_core(other))
    resid = x_own.astype(F32) + total_of(parts, send_parts(parts))

    factor2 = lax.rsqrt(jnp.mean(resid * resid, axis=-1, keepdims=True) + EPSILON)
    u2 = resid * factor2
    n_pieces = gather_rows((u2 * gain_m).astype(BF))
    d_gate, d_up, hidden, mine, other = mlp(n_pieces, c_pieces, mlp_w)
    parts = chip_parts(mine, swap_core(other))
    got = send_parts(parts)
    grads = mlp_grads(after(n_pieces, parts[1]), (d_gate, d_up))
    grads = mlp_grads(c_pieces, (hidden,), grads)
    *got, grads = after((*got, grads))
    d_n2 = total_of(parts, got)
    mlp_grad = lax.psum_scatter(grads, ("z", "y"), scatter_dimension=0, tiled=True)

    d_resid = c_own.astype(F32) + norm_back(u2, factor2, gain_m, d_n2)
    d_branch = d_resid.astype(BF)
    mlp_gain_part = jnp.sum(d_n2 * u2, axis=0)
    d_pieces = gather_rows(d_branch)
    out_mine, out_other = mlp_out(after(hidden, d_branch), mlp_w)
    out_parts = chip_parts(out_mine, swap_core(after(out_other, *d_pieces[1:4])))
    out_got = send_parts(out_parts)
    extra = jnp.pad(mlp_gain_part[None], ((1, 6), (0, 0)))
    place = jnp.stack([lax.axis_index("z"), lax.axis_index("y")]).astype(jnp.int32)
    saved = (factor1, normed, query, key, value, probs, mixed)
    mine, other, *sums = attn_backward(
        after(d_pieces, out_parts[1]), x_pieces, attn_w, cosines, sines, saved, extra, place, head
    )
    sums, other = after((sums, other), *out_got)
    parts = chip_parts(mine, swap_core(other))
    got = send_parts(parts)
    d_n1 = total_of(parts, got)
    layer_output = from_place((resid + total_of(out_parts, out_got)).astype(BF))
    h = sum_zy(sums[:4], sums[4:], layer_output, *got)

    factor1 = factor1[:own, :1]
    u1 = x_own.astype(F32) * factor1
    input_grad = from_place(d_resid + norm_back(u1, factor1, gain_a, d_n1))

    g, g_got = unspread(mlp_grad, a, c)
    gate_grad, up_grad, down_grad = (columns_of(g, i * ff, ff) for i in range(3))
    h, _ = unspread(h, a, c, (g_got,))
    query_grad = columns_of(h, 0, nq)
    key_grad = columns_of(h, nq, nk)
    value_grad = columns_of(h, nq + nk, nk)
    out_grad = columns_of(h, cut, nq).T
    gain_grads = sum(q[:, cut + nq : cut + nq + 2].astype(F32) for q in h).T
    gain_grads = gain_grads + lax.ppermute(gain_grads, "t", SWAP)
    return (
        layer_output, input_grad, gain_grads[0], query_grad, key_grad, value_grad, out_grad,
        gain_grads[1], gate_grad, up_grad, down_grad.T,
    )


def solution(mesh):
    fine = Mesh(mesh.devices.reshape(2, 4, 4, 2, 2), ("a", "z", "y", "c", "t"))
    dp = ("a", "z", "y", "c")
    rows = P(dp + ("t",), None)
    return jax.shard_map(
        local,
        mesh=fine,
        in_specs=(
            rows, P(dp), P(dp), P(dp, "t"), P(dp, "t"), P(dp, "t"), P("t", dp),
            P(dp), P(dp, "t"), P(dp, "t"), P("t", dp), rows,
        ),
        out_specs=(
            rows, rows, P(dp), P(dp, "t"), P(dp, "t"), P(dp, "t"), P("t", dp),
            P(dp), P(dp, "t"), P(dp, "t"), P("t", dp),
        ),
        check_vma=False,
    )
```

time: 467 us -> 399 us (0.85)
  waiting for transfers between devices: 186 us -> 144 us
  local copies, waits for them, and re-layouts: 36.7 us -> 21.8 us
  Pallas kernels: 112 us -> 101 us
  starting transfers between devices: 78.1 us -> 69.3 us
  other arithmetic: 31 us -> 39.7 us
    ppermute x12, waiting for transfers between devices: 63.9 us -> 23.8 us  [to_chip(): lax.ppermute(value, ('a', 't'), [(AT[i], AT[(i + k) % 4]) for i in range(...]
    pallas_call x2 -> x4, Pallas kernels: 73.8 us -> 61.4 us  [the longest x1 29 us: mlp(): pl.pallas_call(mlp_kernel, grid=(8,), in_specs=[fixed((part, d))] * 16 +...]
    ppermute x12, waiting for transfers between devices: 54.9 us -> 66.2 us  [from_chip(): lax.ppermute(value, ('a', 't'), [(AT[(i + k) % 4], AT[i]) for i in range(...]
    convert_element_type x13 -> x15, other arithmetic: 10.4 us -> 20 us  [the longest x4 11.2 us: chip_parts(): return [parts[0]] + [part.astype(BF) for part in parts[1:]]]
    reshape x14 -> x0, local copies, waits for them, and re-layouts: 9.27 us -> none  [the longest x7 5.29 us: whole_columns(): return quarters.transpose(1, 0, 2).reshape(rows, 4 * columns)]
    ppermute x48 -> x42, waiting for transfers between devices: 62.2 us -> 54.2 us  [the longest x12 18.7 us: sum_along(): got = lax.ppermute(pieces[k], axis, [(i, (i + k) % 4) for i in range(4)])]
    ppermute x12, starting transfers between devices: 21.8 us -> 16.3 us  [from_chip(): lax.ppermute(value, ('a', 't'), [(AT[(i + k) % 4], AT[i]) for i in range(...]
    ppermute x48 -> x42, starting transfers between devices: 38.6 us -> 34.3 us  [the longest x12 23.3 us: sum_along(): got = lax.ppermute(pieces[k], axis, [(i, (i + k) % 4) for i in range(4)])]
  transfers between devices with their start and end apart: 76 -> 70, of which waited for: 37 -> 33; matrix products, arithmetic and copies ran while one was open for 10% -> 12% of each run, Pallas kernels for 8% -> 18%
where the time goes in v3:
time: 399 us; the launch traced here: 391 us
  waiting for transfers between devices  144 us (36%)
  Pallas kernels  101 us (25%)
  starting transfers between devices  69.3 us (17%)
  other arithmetic  39.7 us (10%)
  local copies, waits for them, and re-layouts  21.8 us (5%)
  between operations  15.3 us (4%)
    ppermute x12, waiting for transfers between devices, from_chip(): lax.ppermute(value, ('a', 't'), [(AT[(i + k) % 4], AT[i]) for i in range(...  66.2 us
    pallas_call x1, Pallas kernels, mlp(): pl.pallas_call(mlp_kernel, grid=(8,), in_specs=[fixed((part, d))] * 16 +...  29 us
    pallas_call x2, Pallas kernels, mlp_grads(): pl.pallas_call(lambda *refs: mlp_grads_kernel(sides, *refs), grid=(4 * si...  24.6 us
    ppermute x12, waiting for transfers between devices, to_chip(): lax.ppermute(value, ('a', 't'), [(AT[i], AT[(i + k) % 4]) for i in range(...  23.8 us
    pallas_call x1, Pallas kernels, attn_backward(): pl.pallas_call(lambda *refs: attn_backward_kernel(head, *refs), grid=(4,)...  23.5 us
    ppermute x12, starting transfers between devices, sum_along(): got = lax.ppermute(pieces[k], axis, [(i, (i + k) % 4) for i in range(4)])  23.3 us
    ppermute x12, waiting for transfers between devices, sum_along(): got = lax.ppermute(pieces[k], axis, [(i, (i + k) % 4) for i in range(4)])  18.7 us
    ppermute x12, starting transfers between devices, from_chip(): lax.ppermute(value, ('a', 't'), [(AT[(i + k) % 4], AT[i]) for i in range(...  16.3 us
  transfers between devices with their start and end apart: 70, of which 33 were waited for; matrix products, arithmetic and copies ran while one was open for 12% of the time, Pallas kernels for 18%

profile of v3, /device:TPU:0, one launch (start us, length us, event | category | flops | bytes accessed | tf_op | source)
XLA Modules:
  0.0 391.2 jit_solution(2077086404254816463)
XLA Ops:
  14.9 3.3 collective-permute-done.1
  23.8 1.9 collective-permute-start.2
  26.0 8.1 %collective-permute-done.4.refs_3_.refs_11_ = bf16[112,2048]{1,0:T(8,128)(2,1)S(1)} collective-permute-done((bf16[112,2048]{1,0:T(8,128)(2,1)S(1)}, bf16[112,2048]{1,0:T(8,128)(2,1)S(1)}, u32[]{:S(2)}, u32[]{:S(2)}) %collective-permute-start.4) | collective-permute-done | bytes 458784 | tf_op jit(solution)/shard_map/ppermute | solution.py:46
  35.5 9.4 %collective-permute-done.2.refs_1_.refs_9_ = bf16[112,2048]{1,0:T(8,128)(2,1)S(1)} collective-permute-done((bf16[112,2048]{1,0:T(8,128)(2,1)S(1)}, bf16[112,2048]{1,0:T(8,128)(2,1)S(1)}, u32[]{:S(2)}, u32[]{:S(2)}) %collective-permute-start.2) | collective-permute-done | bytes 458784 | tf_op jit(solution)/shard_map/ppermute | solution.py:46
  46.1 8.9 %collective-permute-done.30 = bf16[64,3072]{1,0:T(8,128)(2,1)S(1)} collective-permute-done((bf16[64,3072]{1,0:T(8,128)(2,1)S(1)}, bf16[64,3072]{1,0:T(8,128)(2,1)S(1)}, u32[]{:S(2)}, u32[]{:S(2)}) %collective-permute-start.30) | collective-permute-done | bytes 393248 | tf_op jit(solution)/shard_map/ppermute | solution.py:99
  57.3 2.6 collective-permute-done.12
  63.7 2.4 collective-permute-start.10
  68.0 2.6 fusion.8
  70.7 15.8 %collective-permute-done.11.refs_11_.refs_3_ = bf16[112,2048]{1,0:T(8,128)(2,1)S(1)} collective-permute-done((bf16[112,2048]{1,0:T(8,128)(2,1)S(1)}, bf16[112,2048]{1,0:T(8,128)(2,1)S(1)}, u32[]{:S(2)}, u32[]{:S(2)}) %collective-permute-start.11) | collective-permute-done | bytes 458784 | tf_op jit(solution)/shard_map/ppermute | solution.py:46
  89.1 15.8 %shard_map.203 = (bf16[448,2048]{1,0:T(8,128)(2,1)}, bf16[448,2048]{1,0:T(8,128)(2,1)}, bf16[896,2048]{1,0:T(8,128)(2,1)}, f32[896,128]{1,0:T(8,128)}, bf16[896,...) custom-call(bf16[112,2048]{1,0:T(8,128)(2,1)} %copy.69.refs_0_, ...), custom_call_target="tpu_custom_call" | custom-call | flops 30000001024 | bytes 1048576 | tf_op jit(solution)/shard_map/pallas_call | solution.py:289
  104.9 4.0 %collective-permute-done.14 = bf16[448,2048]{1,0:T(8,128)(2,1)S(1)} collective-permute-done((bf16[448,2048]{1,0:T(8,128)(2,1)}, bf16[448,2048]{1,0:T(8,128)(2,1)S(1)}, u32[]{:S(2)}, u32[]{:S(2)}) %collective-permute-start.14) | collective-permute-done | bytes 1835040 | tf_op jit(solution)/shard_map/ppermute | solution.py:58
  108.9 3.3 add_convert_fusion.12
  112.2 2.2 collective-permute-start.17
  117.0 10.3 %collective-permute-done.15 = bf16[112,2048]{1,0:T(8,128)(2,1)S(1)} collective-permute-done((bf16[112,2048]{1,0:T(8,128)(2,1)}, bf16[112,2048]{1,0:T(8,128)(2,1)S(1)}, u32[]{:S(2)}, u32[]{:S(2)}) %collective-permute-start.15) | collective-permute-done | bytes 458784 | tf_op jit(solution)/shard_map/ppermute | solution.py:50
  127.4 8.6 %collective-permute-done.17 = bf16[112,2048]{1,0:T(8,128)(2,1)S(1)} collective-permute-done((bf16[112,2048]{1,0:T(8,128)(2,1)}, bf16[112,2048]{1,0:T(8,128)(2,1)S(1)}, u32[]{:S(2)}, u32[]{:S(2)}) %collective-permute-start.17) | collective-permute-done | bytes 458784 | tf_op jit(solution)/shard_map/ppermute | solution.py:50
  138.6 3.2 collective-permute-start.19
  142.5 10.9 %collective-permute-done.20.refs_3_ = bf16[112,2048]{1,0:T(8,128)(2,1)S(1)} collective-permute-done((bf16[112,2048]{1,0:T(8,128)(2,1)S(1)}, bf16[112,2048]{1,0:T(8,128)(2,1)S(1)}, u32[]{:S(2)}, u32[]{:S(2)}) %collective-permute-start.20) | collective-permute-done | bytes 458784 | tf_op jit(solution)/shard_map/ppermute | solution.py:46
  153.3 8.0 %collective-permute-done.19.refs_2_ = bf16[112,2048]{1,0:T(8,128)(2,1)S(1)} collective-permute-done((bf16[112,2048]{1,0:T(8,128)(2,1)S(1)}, bf16[112,2048]{1,0:T(8,128)(2,1)S(1)}, u32[]{:S(2)}, u32[]{:S(2)}) %collective-permute-start.19) | collective-permute-done | bytes 458784 | tf_op jit(solution)/shard_map/ppermute | solution.py:46
  164.4 29.0 %shard_map.204 = (bf16[896,1024]{1,0:T(8,128)(2,1)}, bf16[896,1024]{1,0:T(8,128)(2,1)}, bf16[896,1024]{1,0:T(8,128)(2,1)}, bf16[448,2048]{1,0:T(8,128)(2,1)}, bf16[448,2048]{1,0:T(8,128)(2,1)}) custom-call(bf16[112,2048]{1,0:T(8,128)(2,1)} %copy-done.10, bf16[112,2048]{1,0:T(8,128)(2,1)} %copy-done.39, bf16[112,2048]{1,0:T(8,128)(2,1)} %copy-done.38, ...), custom_call_target="tpu_custom_call" | custom-call | flops 40000000000 | bytes 1048576 | tf_op jit(solution)/shard_map/pallas_call | solution.py:450
  194.0 3.6 collective-permute-done.31
  197.6 3.3 add_convert_fusion.7
  201.6 3.2 collective-permute-start.34
  205.2 15.0 %shard_map.205.refs_9_ = bf16[2048,3072]{1,0:T(8,128)(2,1)} custom-call(bf16[112,2048]{1,0:T(8,128)(2,1)} %copy-done.10, bf16[112,2048]{1,0:T(8,128)(2,1)} %copy-done.39, bf16[112,2048]{1,0:T(8,128)(2,1)} %copy-done.38, bf16[112,2048]{1,0:T(8,128)(2,1)} %copy-done.36, bf16[112,2048]{1,0:T(8,128)(2,1)} %copy-done.42, ...), custom_call_target="tpu_custom_call" | custom-call | flops 40000000000 | bytes 1048576 | tf_op jit(solution)/shard_map/pallas_call | solution.py:496
  220.2 9.5 %shard_map.206 = bf16[2048,3072]{1,0:T(8,128)(2,1)} custom-call(bf16[112,2048]{1,0:T(8,128)(2,1)} %copy-done.9, bf16[112,2048]{1,0:T(8,128)(2,1)} %collective-permute-done.9.refs_9_.refs_1_, bf16[112,2048]{1,0:T(8,128)(2,1)} %copy-done.29, bf16[112,2048]{1,0:T(8,128)(2,1)} %copy-done.28, ...), custom_call_target="tpu_custom_call", output_to_operand_aliasing={{}: (9, {})} | custom-call | flops 20000000000 | bytes 1048576 | tf_op jit(solution)/shard_map/pallas_call | solution.py:496
  230.7 2.0 multiply_reduce_fusion
  233.1 2.1 collective-permute-start.37
  237.4 7.9 %shard_map.207 = (bf16[448,2048]{1,0:T(8,128)(2,1)}, bf16[448,2048]{1,0:T(8,128)(2,1)}) custom-call(bf16[896,1024]{1,0:T(8,128)(2,1)} %get-tuple-element.113.refs_8_.x_ref, bf16[2048,3072]{1,0:T(8,128)(2,1)} %all-gather.5.cloned.1.call-done.refs_16_.refs_17_.refs_18_.w_ref), custom_call_target="tpu_custom_call" | custom-call | flops 5000000000 | bytes 1048576 | tf_op jit(solution)/shard_map/pallas_call | solution.py:522
  248.6 8.5 %collective-permute-done.35.refs_1_ = bf16[112,2048]{1,0:T(8,128)(2,1)S(1)} collective-permute-done((bf16[112,2048]{1,0:T(8,128)(2,1)S(1)}, bf16[112,2048]{1,0:T(8,128)(2,1)S(1)}, u32[]{:S(2)}, u32[]{:S(2)}) %collective-permute-start.35) | collective-permute-done | bytes 458784 | tf_op jit(solution)/shard_map/ppermute | solution.py:46
  262.1 2.3 add_convert_fusion.6
  266.0 2.6 collective-permute-start.41
  268.7 23.5 %shard_map.208 = (bf16[448,2048]{1,0:T(8,128)(2,1)}, bf16[448,2048]{1,0:T(8,128)(2,1)}, bf16[512,384]{1,0:T(8,128)(2,1)}, bf16[512,384]{1,0:T(8,128)(2,1)}, bf16...) custom-call(bf16[112,2048]{1,0:T(8,128)(2,1)} %copy-done.5, ...), custom_call_target="tpu_custom_call" | custom-call | flops 10000000000 | bytes 1048576 | tf_op jit(solution)/shard_map/pallas_call | solution.py:378
  293.9 4.1 %collective-permute-start.50 = (bf16[512,384]{1,0:T(8,128)(2,1)}, bf16[512,384]{1,0:T(8,128)(2,1)}, u32[]{:S(2)}, u32[]{:S(2)}) collective-permute-start(bf16[512,384]{1,0:T(8,128)(2,1)} %get-tuple-element.144), channel_id=1, source_target_pairs={{0,32},{16,48},{32,0},{48,16},{1,33},{17,49},{33,1},{49,17},{2,34}... | collective-permute-start | bytes 1179656 | tf_op jit(solution)/shard_map/ppermute | solution.py:129
  298.0 2.0 add_convert_fusion.3
  303.1 2.2 collective-permute-start.52
  305.4 2.9 collective-permute-start.53
  310.1 2.4 collective-permute-start.55
  312.5 2.2 add_convert_fusion.2
  314.7 2.8 collective-permute-done.51
  317.5 2.3 collective-permute-start.47
  323.5 12.0 %collective-permute-done.54 = bf16[512,384]{1,0:T(8,128)(2,1)S(1)} collective-permute-done((bf16[512,384]{1,0:T(8,128)(2,1)}, bf16[512,384]{1,0:T(8,128)(2,1)S(1)}, u32[]{:S(2)}, u32[]{:S(2)}) %collective-permute-start.54) | collective-permute-done | bytes 393248 | tf_op jit(solution)/shard_map/ppermute | solution.py:129
  337.0 4.3 %collective-permute-done.49 = bf16[112,2048]{1,0:T(8,128)(2,1)S(1)} collective-permute-done((bf16[112,2048]{1,0:T(8,128)(2,1)S(1)}, bf16[112,2048]{1,0:T(8,128)(2,1)S(1)}, u32[]{:S(2)}, u32[]{:S(2)}) %collective-permute-start.49) | collective-permute-done | bytes 458784 | tf_op jit(solution)/shard_map/ppermute | solution.py:50
  343.0 2.8 fusion.5
  348.7 2.3 collective-permute-start.56
  353.1 3.3 collective-permute-start.59
  361.0 3.3 collective-permute-done.60
  364.3 4.4 %collective-permute-done.62 = bf16[64,3072]{1,0:T(8,128)(2,1)S(1)} collective-permute-done((bf16[64,3072]{1,0:T(8,128)(2,1)S(1)}, bf16[64,3072]{1,0:T(8,128)(2,1)S(1)}, u32[]{:S(2)}, u32[]{:S(2)}) %collective-permute-start.62) | collective-permute-done | bytes 393248 | tf_op jit(solution)/shard_map/ppermute | solution.py:111
  370.0 3.5 collective-permute-done.63
  375.4 2.7 collective-permute-start.65
  (316 shorter events, 82.5 us)
Async XLA Ops:
  7.2 81.9 %all-gather.3.cloned.1.call-start = ((), (), s32[]{:S(2)}) async-start(), calls=%async_computation.1 | async-start | bytes 3342336 | tf_op jit(solution)/shard_map/all_gather | solution.py:570
  18.9 145.5 %all-gather.5.cloned.1.call-start = ((), (), s32[]{:S(2)}) async-start(), calls=%async_computation.2 | async-start | bytes 13369344 | tf_op jit(solution)/shard_map/all_gather | solution.py:577
  20.4 13.6 %collective-permute-start.4 = (bf16[112,2048]{1,0:T(8,128)(2,1)S(1)}, bf16[112,2048]{1,0:T(8,128)(2,1)S(1)}, u32[]{:S(2)}, u32[]{:S(2)}) collective-permute-start(bf16[112,2048]{1,0:T(8,128)(2,1)S(1)} %copy.60.refs_8_), channel_id=1, source_target_pairs={{65,0},{0,64},{64,1},{1,65},{67,2},{2,66},{66,3},{3,67},{69,4},{4,... | collective-permute-start | bytes 1376264 | tf_op jit(solution)/shard_map/ppermute | solution.py:46
  22.1 13.4 %collective-permute-start.3 = (bf16[112,2048]{1,0:T(8,128)(2,1)S(1)}, bf16[112,2048]{1,0:T(8,128)(2,1)S(1)}, u32[]{:S(2)}, u32[]{:S(2)}) collective-permute-start(bf16[112,2048]{1,0:T(8,128)(2,1)S(1)} %copy.60.refs_8_), channel_id=1, source_target_pairs={{64,0},{1,64},{65,1},{0,65},{66,2},{3,66},{67,3},{2,67},{68,4},{5,... | collective-permute-start | bytes 1376264 | tf_op jit(solution)/shard_map/ppermute | solution.py:46
  23.8 21.2 %collective-permute-start.2 = (bf16[112,2048]{1,0:T(8,128)(2,1)S(1)}, bf16[112,2048]{1,0:T(8,128)(2,1)S(1)}, u32[]{:S(2)}, u32[]{:S(2)}) collective-permute-start(bf16[112,2048]{1,0:T(8,128)(2,1)S(1)} %copy.60.refs_8_), channel_id=1, source_target_pairs={{1,0},{65,64},{0,1},{64,65},{3,2},{67,66},{2,3},{66,67},{5,4},{69,... | collective-permute-start | bytes 1376264 | tf_op jit(solution)/shard_map/ppermute | solution.py:46
  45.0 10.1 %collective-permute-start.30 = (bf16[64,3072]{1,0:T(8,128)(2,1)S(1)}, bf16[64,3072]{1,0:T(8,128)(2,1)S(1)}, u32[]{:S(2)}, u32[]{:S(2)}) collective-permute-start(bf16[64,3072]{1,0:T(8,128)(2,1)S(1)} %broadcast_select_fusion.6), channel_id=1, source_target_pairs={{0,64},{64,0},{1,65},{65,1},{2,66},{66,2},{3,67},{67,3},{4,68},{68... | collective-permute-start | bytes 1179656 | tf_op jit(solution)/shard_map/ppermute | solution.py:99
  56.2 300.9 %reduce-scatter.2.cloned.1.call-start = ((), (), s32[]{:S(2)}) async-start(), calls=%async_computation.3 | async-start | bytes 13369344 | tf_op jit(solution)/shard_map/reduce_scatter | solution.py:603
  62.8 23.7 %collective-permute-start.11 = (bf16[112,2048]{1,0:T(8,128)(2,1)S(1)}, bf16[112,2048]{1,0:T(8,128)(2,1)S(1)}, u32[]{:S(2)}, u32[]{:S(2)}) collective-permute-start(bf16[112,2048]{1,0:T(8,128)(2,1)S(1)} %copy.66.refs_8_.refs_0_), channel_id=1, source_target_pairs={{65,0},{0,64},{64,1},{1,65},{67,2},{2,66},{66,3},{3,67},{69,4},{4,... | collective-permute-start | bytes 1376264 | tf_op jit(solution)/shard_map/ppermute | solution.py:46
  63.7 22.8 %collective-permute-start.10 = (bf16[112,2048]{1,0:T(8,128)(2,1)S(1)}, bf16[112,2048]{1,0:T(8,128)(2,1)S(1)}, u32[]{:S(2)}, u32[]{:S(2)}) collective-permute-start(bf16[112,2048]{1,0:T(8,128)(2,1)S(1)} %copy.66.refs_8_.refs_0_), channel_id=1, source_target_pairs={{64,0},{1,64},{65,1},{0,65},{66,2},{3,66},{67,3},{2,67},{68,4},{5,... | collective-permute-start | bytes 1376264 | tf_op jit(solution)/shard_map/ppermute | solution.py:46
  66.1 22.0 %collective-permute-start.9 = (bf16[112,2048]{1,0:T(8,128)(2,1)S(1)}, bf16[112,2048]{1,0:T(8,128)(2,1)}, u32[]{:S(2)}, u32[]{:S(2)}) collective-permute-start(bf16[112,2048]{1,0:T(8,128)(2,1)S(1)} %copy.66.refs_8_.refs_0_), channel_id=1, source_target_pairs={{1,0},{65,64},{0,1},{64,65},{3,2},{67,66},{2,3},{66,67},{5,4},{69,... | collective-permute-start | bytes 1376264 | tf_op jit(solution)/shard_map/ppermute | solution.py:46
  112.2 15.1 %collective-permute-start.15 = (bf16[112,2048]{1,0:T(8,128)(2,1)}, bf16[112,2048]{1,0:T(8,128)(2,1)S(1)}, u32[]{:S(2)}, u32[]{:S(2)}) collective-permute-start(bf16[112,2048]{1,0:T(8,128)(2,1)} %get-tuple-element.195), channel_id=1, source_target_pairs={{0,1},{64,65},{1,0},{65,64},{2,3},{66,67},{3,2},{67,66},{4,5},{68,... | collective-permute-start | bytes 1376264 | tf_op jit(solution)/shard_map/ppermute | solution.py:50
  112.2 23.7 %collective-permute-start.17 = (bf16[112,2048]{1,0:T(8,128)(2,1)}, bf16[112,2048]{1,0:T(8,128)(2,1)S(1)}, u32[]{:S(2)}, u32[]{:S(2)}) collective-permute-start(bf16[112,2048]{1,0:T(8,128)(2,1)} %get-tuple-element.196), channel_id=1, source_target_pairs={{0,65},{64,0},{1,64},{65,1},{2,67},{66,2},{3,66},{67,3},{4,69},{68... | collective-permute-start | bytes 1376264 | tf_op jit(solution)/shard_map/ppermute | solution.py:50
  114.5 22.0 %collective-permute-start.16 = (bf16[112,2048]{1,0:T(8,128)(2,1)}, bf16[112,2048]{1,0:T(8,128)(2,1)}, u32[]{:S(2)}, u32[]{:S(2)}) collective-permute-start(bf16[112,2048]{1,0:T(8,128)(2,1)} %get-tuple-element.197), channel_id=1, source_target_pairs={{0,64},{64,1},{1,65},{65,0},{2,66},{66,3},{3,67},{67,2},{4,68},{68... | collective-permute-start | bytes 1376264 | tf_op jit(solution)/shard_map/ppermute | solution.py:50
  115.5 26.3 %collective-permute-start.25 = (bf16[112,2048]{1,0:T(8,128)(2,1)S(1)}, bf16[112,2048]{1,0:T(8,128)(2,1)S(1)}, u32[]{:S(2)}, u32[]{:S(2)}) collective-permute-start(bf16[112,2048]{1,0:T(8,128)(2,1)S(1)} %copy.66.refs_8_.refs_0_), channel_id=1, source_target_pairs={{0,2},{2,0},{1,3},{3,1},{4,6},{6,4},{5,7},{7,5},{8,10},{10,8},{9,1... | collective-permute-start | bytes 1376264 | tf_op jit(solution)/shard_map/ppermute | solution.py:58
  115.6 26.3 %collective-permute-start.28 = (bf16[112,2048]{1,0:T(8,128)(2,1)}, bf16[112,2048]{1,0:T(8,128)(2,1)S(1)}, u32[]{:S(2)}, u32[]{:S(2)}) collective-permute-start(bf16[112,2048]{1,0:T(8,128)(2,1)} %copy-done.28), channel_id=1, source_target_pairs={{0,2},{2,0},{1,3},{3,1},{4,6},{6,4},{5,7},{7,5},{8,10},{10,8},{9,1... | collective-permute-start | bytes 1376264 | tf_op jit(solution)/shard_map/ppermute | solution.py:58
  127.4 14.6 %collective-permute-start.27 = (bf16[112,2048]{1,0:T(8,128)(2,1)}, bf16[112,2048]{1,0:T(8,128)(2,1)S(1)}, u32[]{:S(2)}, u32[]{:S(2)}) collective-permute-start(bf16[112,2048]{1,0:T(8,128)(2,1)} %copy-done.29), channel_id=1, source_target_pairs={{0,2},{2,0},{1,3},{3,1},{4,6},{6,4},{5,7},{7,5},{8,10},{10,8},{9,1... | collective-permute-start | bytes 1376264 | tf_op jit(solution)/shard_map/ppermute | solution.py:58
  138.5 14.8 %collective-permute-start.20 = (bf16[112,2048]{1,0:T(8,128)(2,1)S(1)}, bf16[112,2048]{1,0:T(8,128)(2,1)S(1)}, u32[]{:S(2)}, u32[]{:S(2)}) collective-permute-start(bf16[112,2048]{1,0:T(8,128)(2,1)S(1)} %multiply_convert_fusion.refs_0_), channel_id=1, source_target_pairs={{65,0},{0,64},{64,1},{1,65},{67,2},{2,66},{66,3},{3,67},{69,4},{4,... | collective-permute-start | bytes 1376264 | tf_op jit(solution)/shard_map/ppermute | solution.py:46
  138.6 22.7 %collective-permute-start.19 = (bf16[112,2048]{1,0:T(8,128)(2,1)S(1)}, bf16[112,2048]{1,0:T(8,128)(2,1)S(1)}, u32[]{:S(2)}, u32[]{:S(2)}) collective-permute-start(bf16[112,2048]{1,0:T(8,128)(2,1)S(1)} %multiply_convert_fusion.refs_0_), channel_id=1, source_target_pairs={{64,0},{1,64},{65,1},{0,65},{66,2},{3,66},{67,3},{2,67},{68,4},{5,... | collective-permute-start | bytes 1376264 | tf_op jit(solution)/shard_map/ppermute | solution.py:46
  141.8 20.2 %collective-permute-start.18 = (bf16[112,2048]{1,0:T(8,128)(2,1)S(1)}, bf16[112,2048]{1,0:T(8,128)(2,1)S(1)}, u32[]{:S(2)}, u32[]{:S(2)}) collective-permute-start(bf16[112,2048]{1,0:T(8,128)(2,1)S(1)} %multiply_convert_fusion.refs_0_), channel_id=1, source_target_pairs={{1,0},{65,64},{0,1},{64,65},{3,2},{67,66},{2,3},{66,67},{5,4},{69,... | collective-permute-start | bytes 1376264 | tf_op jit(solution)/shard_map/ppermute | solution.py:46
  141.9 20.5 %collective-permute-start.26 = (bf16[112,2048]{1,0:T(8,128)(2,1)}, bf16[112,2048]{1,0:T(8,128)(2,1)S(1)}, u32[]{:S(2)}, u32[]{:S(2)}) collective-permute-start(bf16[112,2048]{1,0:T(8,128)(2,1)} %collective-permute-done.9.refs_9_.refs_1_), channel_id=1, source_target_pairs={{0,2},{2,0},{1,3},{3,1},{4,6},{6,4},{5,7},{7,5},{8,10},{10,8},{9,1... | collective-permute-start | bytes 1376264 | tf_op jit(solution)/shard_map/ppermute | solution.py:58
  142.0 20.5 %collective-permute-start.21 = (bf16[112,2048]{1,0:T(8,128)(2,1)S(1)}, bf16[112,2048]{1,0:T(8,128)(2,1)S(1)}, u32[]{:S(2)}, u32[]{:S(2)}) collective-permute-start(bf16[112,2048]{1,0:T(8,128)(2,1)S(1)} %multiply_convert_fusion.refs_0_), channel_id=1, source_target_pairs={{0,2},{2,0},{1,3},{3,1},{4,6},{6,4},{5,7},{7,5},{8,10},{10,8},{9,1... | collective-permute-start | bytes 1376264 | tf_op jit(solution)/shard_map/ppermute | solution.py:58
  153.3 9.2 %collective-permute-start.24 = (bf16[112,2048]{1,0:T(8,128)(2,1)S(1)}, bf16[112,2048]{1,0:T(8,128)(2,1)S(1)}, u32[]{:S(2)}, u32[]{:S(2)}) collective-permute-start(bf16[112,2048]{1,0:T(8,128)(2,1)S(1)} %collective-permute-done.20.refs_3_), channel_id=1, source_target_pairs={{0,2},{2,0},{1,3},{3,1},{4,6},{6,4},{5,7},{7,5},{8,10},{10,8},{9,1... | collective-permute-start | bytes 1376264 | tf_op jit(solution)/shard_map/ppermute | solution.py:58
  201.0 28.8 %collective-permute-start.32 = (bf16[112,2048]{1,0:T(8,128)(2,1)}, bf16[112,2048]{1,0:T(8,128)(2,1)S(1)}, u32[]{:S(2)}, u32[]{:S(2)}) collective-permute-start(bf16[112,2048]{1,0:T(8,128)(2,1)} %get-tuple-element.194), channel_id=1, source_target_pairs={{0,1},{64,65},{1,0},{65,64},{2,3},{66,67},{3,2},{67,66},{4,5},{68,... | collective-permute-start | bytes 1376264 | tf_op jit(solution)/shard_map/ppermute | solution.py:50
  201.6 28.2 %collective-permute-start.34 = (bf16[112,2048]{1,0:T(8,128)(2,1)}, bf16[112,2048]{1,0:T(8,128)(2,1)S(1)}, u32[]{:S(2)}, u32[]{:S(2)}) collective-permute-start(bf16[112,2048]{1,0:T(8,128)(2,1)} %get-tuple-element.192), channel_id=1, source_target_pairs={{0,65},{64,0},{1,64},{65,1},{2,67},{66,2},{3,66},{67,3},{4,69},{68... | collective-permute-start | bytes 1376264 | tf_op jit(solution)/shard_map/ppermute | solution.py:50
  204.7 25.0 %collective-permute-start.33 = (bf16[112,2048]{1,0:T(8,128)(2,1)}, bf16[112,2048]{1,0:T(8,128)(2,1)}, u32[]{:S(2)}, u32[]{:S(2)}) collective-permute-start(bf16[112,2048]{1,0:T(8,128)(2,1)} %get-tuple-element.193), channel_id=1, source_target_pairs={{0,64},{64,1},{1,65},{65,0},{2,66},{66,3},{3,67},{67,2},{4,68},{68... | collective-permute-start | bytes 1376264 | tf_op jit(solution)/shard_map/ppermute | solution.py:50
  233.1 13.8 %collective-permute-start.37 = (bf16[112,2048]{1,0:T(8,128)(2,1)S(1)}, bf16[112,2048]{1,0:T(8,128)(2,1)S(1)}, u32[]{:S(2)}, u32[]{:S(2)}) collective-permute-start(bf16[112,2048]{1,0:T(8,128)(2,1)S(1)} %fusion.13.refs_0_), channel_id=1, source_target_pairs={{65,0},{0,64},{64,1},{1,65},{67,2},{2,66},{66,3},{3,67},{69,4},{4,... | collective-permute-start | bytes 1376264 | tf_op jit(solution)/shard_map/ppermute | solution.py:46
  235.2 13.5 %collective-permute-start.36 = (bf16[112,2048]{1,0:T(8,128)(2,1)S(1)}, bf16[112,2048]{1,0:T(8,128)(2,1)S(1)}, u32[]{:S(2)}, u32[]{:S(2)}) collective-permute-start(bf16[112,2048]{1,0:T(8,128)(2,1)S(1)} %fusion.13.refs_0_), channel_id=1, source_target_pairs={{64,0},{1,64},{65,1},{0,65},{66,2},{3,66},{67,3},{2,67},{68,4},{5,... | collective-permute-start | bytes 1376264 | tf_op jit(solution)/shard_map/ppermute | solution.py:46
  236.4 20.8 %collective-permute-start.35 = (bf16[112,2048]{1,0:T(8,128)(2,1)S(1)}, bf16[112,2048]{1,0:T(8,128)(2,1)S(1)}, u32[]{:S(2)}, u32[]{:S(2)}) collective-permute-start(bf16[112,2048]{1,0:T(8,128)(2,1)S(1)} %fusion.13.refs_0_), channel_id=1, source_target_pairs={{1,0},{65,64},{0,1},{64,65},{3,2},{67,66},{2,3},{66,67},{5,4},{69,... | collective-permute-start | bytes 1376264 | tf_op jit(solution)/shard_map/ppermute | solution.py:46
  258.5 7.5 %collective-permute-start.42 = (bf16[112,2048]{1,0:T(8,128)(2,1)S(1)}, bf16[112,2048]{1,0:T(8,128)(2,1)S(1)}, u32[]{:S(2)}, u32[]{:S(2)}) collective-permute-start(bf16[112,2048]{1,0:T(8,128)(2,1)S(1)} %fusion.13.refs_0_), channel_id=1, source_target_pairs={{0,2},{2,0},{1,3},{3,1},{4,6},{6,4},{5,7},{7,5},{8,10},{10,8},{9,1... | collective-permute-start | bytes 1376264 | tf_op jit(solution)/shard_map/ppermute | solution.py:58
  264.4 27.8 %collective-permute-start.39 = (bf16[112,2048]{1,0:T(8,128)(2,1)S(1)}, bf16[112,2048]{1,0:T(8,128)(2,1)}, u32[]{:S(2)}, u32[]{:S(2)}) collective-permute-start(bf16[112,2048]{1,0:T(8,128)(2,1)S(1)} %get-tuple-element.189), channel_id=1, source_target_pairs={{0,1},{64,65},{1,0},{65,64},{2,3},{66,67},{3,2},{67,66},{4,5},{68,... | collective-permute-start | bytes 1376264 | tf_op jit(solution)/shard_map/ppermute | solution.py:50
  266.0 26.1 %collective-permute-start.41 = (bf16[112,2048]{1,0:T(8,128)(2,1)S(1)}, bf16[112,2048]{1,0:T(8,128)(2,1)}, u32[]{:S(2)}, u32[]{:S(2)}) collective-permute-start(bf16[112,2048]{1,0:T(8,128)(2,1)S(1)} %get-tuple-element.190), channel_id=1, source_target_pairs={{0,65},{64,0},{1,64},{65,1},{2,67},{66,2},{3,66},{67,3},{4,69},{68... | collective-permute-start | bytes 1376264 | tf_op jit(solution)/shard_map/ppermute | solution.py:50
  268.6 23.6 %collective-permute-start.40 = (bf16[112,2048]{1,0:T(8,128)(2,1)S(1)}, bf16[112,2048]{1,0:T(8,128)(2,1)}, u32[]{:S(2)}, u32[]{:S(2)}) collective-permute-start(bf16[112,2048]{1,0:T(8,128)(2,1)S(1)} %get-tuple-element.191), channel_id=1, source_target_pairs={{0,64},{64,1},{1,65},{65,0},{2,66},{66,3},{3,67},{67,2},{4,68},{68... | collective-permute-start | bytes 1376264 | tf_op jit(solution)/shard_map/ppermute | solution.py:50
  292.2 17.8 %collective-permute-start.46 = (bf16[448,2048]{1,0:T(8,128)(2,1)}, bf16[448,2048]{1,0:T(8,128)(2,1)}, u32[]{:S(2)}, u32[]{:S(2)}) collective-permute-start(bf16[448,2048]{1,0:T(8,128)(2,1)} %get-tuple-element.142), channel_id=1, source_target_pairs={{0,2},{2,0},{1,3},{3,1},{4,6},{6,4},{5,7},{7,5},{8,10},{10,8},{9,1... | collective-permute-start | bytes 5505032 | tf_op jit(solution)/shard_map/ppermute | solution.py:58
  293.9 15.4 %collective-permute-start.50 = (bf16[512,384]{1,0:T(8,128)(2,1)}, bf16[512,384]{1,0:T(8,128)(2,1)}, u32[]{:S(2)}, u32[]{:S(2)}) collective-permute-start(bf16[512,384]{1,0:T(8,128)(2,1)} %get-tuple-element.144), channel_id=1, source_target_pairs={{0,32},{16,48},{32,0},{48,16},{1,33},{17,49},{33,1},{49,17},{2,34}... | collective-permute-start | bytes 1179656 | tf_op jit(solution)/shard_map/ppermute | solution.py:129
  302.1 15.5 %collective-permute-start.51 = (bf16[512,384]{1,0:T(8,128)(2,1)}, bf16[512,384]{1,0:T(8,128)(2,1)}, u32[]{:S(2)}, u32[]{:S(2)}) collective-permute-start(bf16[512,384]{1,0:T(8,128)(2,1)} %get-tuple-element.145), channel_id=1, source_target_pairs={{0,16},{16,32},{32,48},{48,0},{1,17},{17,33},{33,49},{49,1},{2,18}... | collective-permute-start | bytes 1179656 | tf_op jit(solution)/shard_map/ppermute | solution.py:129
  303.1 16.6 %collective-permute-start.52 = (bf16[512,384]{1,0:T(8,128)(2,1)}, bf16[512,384]{1,0:T(8,128)(2,1)}, u32[]{:S(2)}, u32[]{:S(2)}) collective-permute-start(bf16[512,384]{1,0:T(8,128)(2,1)} %get-tuple-element.146), channel_id=1, source_target_pairs={{0,48},{16,0},{32,16},{48,32},{1,49},{17,1},{33,17},{49,33},{2,50}... | collective-permute-start | bytes 1179656 | tf_op jit(solution)/shard_map/ppermute | solution.py:129
  305.4 16.0 %collective-permute-start.53 = (bf16[512,384]{1,0:T(8,128)(2,1)}, bf16[512,384]{1,0:T(8,128)(2,1)}, u32[]{:S(2)}, u32[]{:S(2)}) collective-permute-start(bf16[512,384]{1,0:T(8,128)(2,1)} %get-tuple-element.148), channel_id=1, source_target_pairs={{0,8},{4,12},{8,0},{12,4},{1,9},{5,13},{9,1},{13,5},{2,10},{6,14},... | collective-permute-start | bytes 1179656 | tf_op jit(solution)/shard_map/ppermute | solution.py:129
  309.2 26.3 %collective-permute-start.54 = (bf16[512,384]{1,0:T(8,128)(2,1)}, bf16[512,384]{1,0:T(8,128)(2,1)S(1)}, u32[]{:S(2)}, u32[]{:S(2)}) collective-permute-start(bf16[512,384]{1,0:T(8,128)(2,1)} %get-tuple-element.149), channel_id=1, source_target_pairs={{0,4},{4,8},{8,12},{12,0},{1,5},{5,9},{9,13},{13,1},{2,6},{6,10},{... | collective-permute-start | bytes 1179656 | tf_op jit(solution)/shard_map/ppermute | solution.py:129
  310.1 25.7 %collective-permute-start.55 = (bf16[512,384]{1,0:T(8,128)(2,1)}, bf16[512,384]{1,0:T(8,128)(2,1)S(1)}, u32[]{:S(2)}, u32[]{:S(2)}) collective-permute-start(bf16[512,384]{1,0:T(8,128)(2,1)} %get-tuple-element.150), channel_id=1, source_target_pairs={{0,12},{4,0},{8,4},{12,8},{1,13},{5,1},{9,5},{13,9},{2,14},{6,2},{... | collective-permute-start | bytes 1179656 | tf_op jit(solution)/shard_map/ppermute | solution.py:129
  317.5 19.5 %collective-permute-start.47 = (bf16[112,2048]{1,0:T(8,128)(2,1)S(1)}, bf16[112,2048]{1,0:T(8,128)(2,1)S(1)}, u32[]{:S(2)}, u32[]{:S(2)}) collective-permute-start(bf16[112,2048]{1,0:T(8,128)(2,1)S(1)} %get-tuple-element.186), channel_id=1, source_target_pairs={{0,1},{64,65},{1,0},{65,64},{2,3},{66,67},{3,2},{67,66},{4,5},{68,... | collective-permute-start | bytes 1376264 | tf_op jit(solution)/shard_map/ppermute | solution.py:50
  319.8 21.5 %collective-permute-start.49 = (bf16[112,2048]{1,0:T(8,128)(2,1)S(1)}, bf16[112,2048]{1,0:T(8,128)(2,1)S(1)}, u32[]{:S(2)}, u32[]{:S(2)}) collective-permute-start(bf16[112,2048]{1,0:T(8,128)(2,1)S(1)} %get-tuple-element.187), channel_id=1, source_target_pairs={{0,65},{64,0},{1,64},{65,1},{2,67},{66,2},{3,66},{67,3},{4,69},{68... | collective-permute-start | bytes 1376264 | tf_op jit(solution)/shard_map/ppermute | solution.py:50
  321.4 20.0 %collective-permute-start.48 = (bf16[112,2048]{1,0:T(8,128)(2,1)S(1)}, bf16[112,2048]{1,0:T(8,128)(2,1)S(1)}, u32[]{:S(2)}, u32[]{:S(2)}) collective-permute-start(bf16[112,2048]{1,0:T(8,128)(2,1)S(1)} %get-tuple-element.188), channel_id=1, source_target_pairs={{0,64},{64,1},{1,65},{65,0},{2,66},{66,3},{3,67},{67,2},{4,68},{68... | collective-permute-start | bytes 1376264 | tf_op jit(solution)/shard_map/ppermute | solution.py:50
  348.7 9.6 %collective-permute-start.56 = (bf16[128,384]{1,0:T(8,128)(2,1)S(1)}, bf16[128,384]{1,0:T(8,128)(2,1)S(1)}, u32[]{:S(2)}, u32[]{:S(2)}) collective-permute-start(bf16[128,384]{1,0:T(8,128)(2,1)S(1)} %get-tuple-element.212), channel_id=1, source_target_pairs={{0,8},{4,12},{8,0},{12,4},{1,9},{5,13},{9,1},{13,5},{2,10},{6,14},... | collective-permute-start | bytes 294920 | tf_op jit(solution)/shard_map/ppermute | solution.py:129
  351.0 8.7 %collective-permute-start.58 = (bf16[128,384]{1,0:T(8,128)(2,1)S(1)}, bf16[128,384]{1,0:T(8,128)(2,1)S(1)}, u32[]{:S(2)}, u32[]{:S(2)}) collective-permute-start(bf16[128,384]{1,0:T(8,128)(2,1)S(1)} %get-tuple-element.213), channel_id=1, source_target_pairs={{0,12},{4,0},{8,4},{12,8},{1,13},{5,1},{9,5},{13,9},{2,14},{6,2},{... | collective-permute-start | bytes 294920 | tf_op jit(solution)/shard_map/ppermute | solution.py:129
  352.7 7.8 %collective-permute-start.57 = (bf16[128,384]{1,0:T(8,128)(2,1)S(1)}, bf16[128,384]{1,0:T(8,128)(2,1)S(1)}, u32[]{:S(2)}, u32[]{:S(2)}) collective-permute-start(bf16[128,384]{1,0:T(8,128)(2,1)S(1)} %get-tuple-element.214), channel_id=1, source_target_pairs={{0,4},{4,8},{8,12},{12,0},{1,5},{5,9},{9,13},{13,1},{2,6},{6,10},{... | collective-permute-start | bytes 294920 | tf_op jit(solution)/shard_map/ppermute | solution.py:129
  353.1 7.5 %collective-permute-start.59 = (bf16[128,384]{1,0:T(8,128)(2,1)S(1)}, bf16[128,384]{1,0:T(8,128)(2,1)S(1)}, u32[]{:S(2)}, u32[]{:S(2)}) collective-permute-start(bf16[128,384]{1,0:T(8,128)(2,1)S(1)} %get-tuple-element.215), channel_id=1, source_target_pairs={{0,32},{16,48},{32,0},{48,16},{1,33},{17,49},{33,1},{49,17},{2,34}... | collective-permute-start | bytes 294920 | tf_op jit(solution)/shard_map/ppermute | solution.py:129
  359.7 9.1 %collective-permute-start.62 = (bf16[64,3072]{1,0:T(8,128)(2,1)S(1)}, bf16[64,3072]{1,0:T(8,128)(2,1)S(1)}, u32[]{:S(2)}, u32[]{:S(2)}) collective-permute-start(bf16[64,3072]{1,0:T(8,128)(2,1)S(1)} %broadcast_select_fusion.3), channel_id=1, source_target_pairs={{0,64},{64,0},{1,65},{65,1},{2,66},{66,2},{3,67},{67,3},{4,68},{68... | collective-permute-start | bytes 1179656 | tf_op jit(solution)/shard_map/ppermute | solution.py:111
  373.8 7.7 %collective-permute-start.66 = (bf16[64,3072]{1,0:T(8,128)(2,1)S(1)}, bf16[64,3072]{1,0:T(8,128)(2,1)S(1)}, u32[]{:S(2)}, u32[]{:S(2)}) collective-permute-start(bf16[64,3072]{1,0:T(8,128)(2,1)S(1)} %pad_maximum_fusion.4), channel_id=1, source_target_pairs={{0,2},{2,0},{1,3},{3,1},{4,6},{6,4},{5,7},{7,5},{8,10},{10,8},{9,1... | collective-permute-start | bytes 1179656 | tf_op jit(solution)/shard_map/ppermute | solution.py:58
  (69 other events, 718.2 us)
Sparse Core Ops, SparseCore 0:
  19.0 50.6 all-gather.2
  71.8 88.9 all-gather.4
  230.6 110.2 reduce-scatter.1
